TPU v7x, 32 devices: a whole 2x2x4 slice. The times are simulated.
32 devices in a mesh: dp: 16 (over z, x, core), tensor: 2 (over y).
Axes of the slice: x: 2, y: 2, z: 4, core: 2. Of those that a mesh axis runs over, the one named last changes fastest.
Arguments:
- grads: bfloat16 [32, 1024, 1024], P(None, 'dp', 'tensor'), may hold values from -63 to 63
- momentum: float32 [32, 1024, 1024], P(None, 'dp', 'tensor'), may hold values from -63 to 63
- left_root: bfloat16 [48, 1024, 1024], P('dp', 'tensor'), may hold values from -3.5 to 3.5
- right_root: bfloat16 [48, 1024, 1024], P('dp', 'tensor'), may hold values from -3.5 to 3.5
- assign_list: int32 [32], replicated, may hold values from 0 to 31, each once
- owner_counts: int32 [16], replicated, may hold values from 1 to 3, 32 in all
Outputs:
- moment_out: float32 [32, 1024, 1024], P(None, 'dp', 'tensor')
- update: bfloat16 [32, 1024, 1024], P(None, 'dp', 'tensor')
Inputs may be any that keep to these rules, and one draw needn't show every extreme that they name: owner_counts sum to 32; the largest is 3.
All inputs are finite; a program needn't handle non-finite values.
Results may differ from a plain program's by a relative error of at most 0.0057.
Values may be sent and summed in bfloat16 or wider, within the bound.
No kernel may reach another device: no remote copies, remote signals or barrier semaphores. Data moves between devices by JAX's collectives and lax.ppermute only.
A program may use at most 128 MiB of HBM per device.

v0:
```python
import jax
import jax.numpy as jnp
from jax import lax
from jax.sharding import PartitionSpec as P

BETA = 0.9
EPS = 1e-06


def tables(assign_list, owner_counts, cap):
    blocks = assign_list.shape[0]
    offsets = jnp.cumsum(owner_counts) - owner_counts
    slot_ids = jnp.arange(cap, dtype=jnp.int32)
    where_at = offsets[:, None] + slot_ids[None, :]
    live = slot_ids[None, :] < owner_counts[:, None]
    picked = assign_list[jnp.clip(where_at, 0, blocks - 1)]
    slot_block = jnp.where(live, picked, -1).reshape(-1)
    position = (
        jnp.zeros((blocks,), jnp.int32).at[assign_list].set(jnp.arange(blocks, dtype=jnp.int32))
    )
    owner_of = jnp.sum((offsets[None, :] <= position[:, None]).astype(jnp.int32), axis=1) - 1
    block_slot = owner_of * cap + position - offsets[owner_of]
    return (slot_block, block_slot)


def body(grads, momentum, left_root, right_root, assign_list, owner_counts):
    cap = left_root.shape[0]
    width = left_root.shape[2]
    cells = float(width * width)
    slot_block, block_slot = tables(assign_list, owner_counts, cap)
    moment_out = BETA * momentum + (1.0 - BETA) * grads.astype(jnp.float32)
    moment_half = moment_out.astype(jnp.bfloat16)
    squares = jnp.sum(moment_out * moment_out, axis=(1, 2))
    live = slot_block >= 0
    safe = jnp.maximum(slot_block, 0)
    outgoing = jnp.where(live[:, None, None], moment_half[safe], jnp.zeros((), jnp.bfloat16))
    owner_here = lax.axis_index("dp")
    mine = lax.dynamic_slice_in_dim(slot_block, owner_here * cap, cap)
    block_squares = lax.psum(squares, ("dp", "tensor"))
    columns = lax.all_to_all(outgoing, "dp", split_axis=0, concat_axis=1, tiled=True)
    owned_squares = block_squares[jnp.maximum(mine, 0)]
    product = jnp.einsum(
        "sij,skj->sik",
        lax.all_gather(columns, "tensor", axis=2, tiled=True),
        right_root,
        preferred_element_type=jnp.float32,
    )
    product_half = product.astype(jnp.bfloat16)
    direction = jnp.einsum(
        "sij,sjk->sik",
        left_root,
        lax.all_gather(product_half, "tensor", axis=2, tiled=True),
        preferred_element_type=jnp.float32,
    )
    direction_part = jnp.sum(direction * direction, axis=(1, 2))
    direction_squares = lax.psum(direction_part, "tensor")
    scale = jnp.sqrt(owned_squares / cells + EPS) / jnp.sqrt(direction_squares / cells + EPS)
    scaled = (direction * scale[:, None, None]).astype(jnp.bfloat16)
    update_columns = lax.all_to_all(scaled, "tensor", split_axis=2, concat_axis=1, tiled=True)
    arrived = lax.all_to_all(update_columns, "dp", split_axis=1, concat_axis=0, tiled=True)
    update = arrived[block_slot]
    return (moment_out, update)


def solution(mesh):
    in_specs = (
        P(None, "dp", "tensor"),
        P(None, "dp", "tensor"),
        P("dp", "tensor", None),
        P("dp", "tensor", None),
        P(),
        P(),
    )
    out_specs = (P(None, "dp", "tensor"), P(None, "dp", "tensor"))
    return jax.shard_map(body, mesh=mesh, in_specs=in_specs, out_specs=out_specs, check_vma=False)
```

profile of v0, /device:TPU:11, one launch (start us, length us, event | category | flops | bytes accessed | tf_op | source)
XLA Modules:
  0.0 466.4 jit_solution(15690830366280891701)
XLA Ops:
  7.2 0.0 copy-start
  7.2 0.0 copy-start.2
  7.2 0.0 all-gather.3.cloned.1.call-start
  7.2 0.9 copy.31
  8.2 0.1 reduce.1
  8.3 0.7 sub.12
  8.9 0.1 compare_select_fusion
  9.0 0.1 reshape.158
  9.1 0.0 copy-done.2
  9.1 0.0 copy-start.4
  9.1 0.8 gather_fusion
  9.9 0.1 reshape.157
  10.0 0.0 copy-done.4
  10.0 0.1 broadcast_maximum_fusion
  10.1 0.1 select_n.57
  10.2 0.1 reshape.166
  10.3 3.9 multiply_reduce_fusion.1
  14.2 0.0 copy-start.3
  14.2 1.8 convert_element_type.19
  16.0 0.8 copy-done.3
  16.8 4.1 gather_fusion.1
  20.9 2.2 broadcast_select_fusion
  23.1 76.1 %all_to_all.54 = bf16[48,64,512]{2,1,0:T(8,128)(2,1)S(1)} all-to-all(bf16[48,64,512]{2,1,0:T(8,128)(2,1)S(1)} %broadcast_select_fusion), channel_id=1, replica_groups=mesh['dp'=16,'tensor'=2] {'dp'}, dimensions={0} | all-to-all | bytes 6291456 | tf_op jit(solution)/shard_map/all_to_all | solution.py:40
  99.2 1.9 copy.32
  101.1 0.0 all-gather.3.cloned.1.call-update
  101.2 0.0 all-gather.5.cloned.1.call-start
  101.2 80.3 %all-gather.3.cloned.1.call-done = bf16[3,1024,1024]{2,1,0:T(8,128)(2,1)} async-done(((bf16[3,1024,512]{2,1,0:T(8,128)(2,1)}), bf16[3,1024,1024]{2,1,0:T(8,128)(2,1)}) %all-gather.3.cloned.1.call-update) | async-done | bytes 6291472 | tf_op jit(solution)/shard_map/all_gather | solution.py:44
  181.5 8.9 %convolution_convert_fusion = bf16[3,1024,512]{2,1,0:T(8,128)(2,1)} fusion(bf16[3,1024,1024]{2,1,0:T(8,128)(2,1)} %all-gather.3.cloned.1.call-done, bf16[3,512,1024]{2,1,0:T(8,128)(2,1)} %param.9), kind=kOutput, calls=%fused_computation.12 | convolution fusion | flops 3222798336 | bytes 12582912 | tf_op jit(solution)/shard_map/sij,skj->sik/dot_general | solution.py:42
  190.3 0.0 all-gather.5.cloned.1.call-update
  190.4 39.8 %psum.14 = f32[32]{0:T(128)S(1)} all-reduce(f32[32]{0:T(128)S(1)} %get-tuple-element.2), channel_id=1, replica_groups=mesh['dp'=16,'tensor'=2] {'dp','tensor'}, use_global_device_ids=true, to_apply=%region_2.3 | all-reduce | flops 32 | bytes 256 | tf_op jit(solution)/shard_map/psum | solution.py:39
  230.2 0.1 dynamic-slice_maximum_fusion
  230.2 0.6 gather_fusion.2
  230.9 40.9 %all-gather.5.cloned.1.call-done = bf16[3,1024,1024]{2,1,0:T(8,128)(2,1)} async-done(((bf16[3,1024,512]{2,1,0:T(8,128)(2,1)}), bf16[3,1024,1024]{2,1,0:T(8,128)(2,1)}) %all-gather.5.cloned.1.call-update) | async-done | bytes 6291472 | tf_op jit(solution)/shard_map/all_gather | solution.py:52
  271.8 0.0 copy-done
  271.8 9.3 %multiply_reduce_fusion = (f32[3]{0:T(128)S(1)}, f32[3,1024,512]{2,1,0:T(8,128)}) fusion(bf16[3,1024,1024]{2,1,0:T(8,128)(2,1)} %all-gather.5.cloned.1.call-done, bf16[3,512,1024]{2,1,0:T(8,128)(2,1)S(1)} %copy-done), kind=kOutput, calls=%fused_computation.7 | convolution fusion | flops 3224371200 | bytes 15728652 | tf_op jit(solution)/shard_map/sij,sjk->sik/dot_general | solution.py:49
  281.0 3.9 psum.15
  285.0 3.7 fusion
  288.7 2.7 copy.34
  291.4 48.3 %all_to_all.55 = bf16[3,512,1024]{1,0,2:T(4,128)(2,1)S(1)} all-to-all(bf16[3,512,1024]{1,0,2:T(4,128)(2,1)S(1)} %copy.34), channel_id=1, replica_groups=mesh['dp'=16,'tensor'=2] {'tensor'}, dimensions={2} | all-to-all | bytes 6291456 | tf_op jit(solution)/shard_map/all_to_all | solution.py:59
  339.7 0.8 copy.35
  340.5 2.8 copy.36
  343.3 6.5 %copy.37 = bf16[3,1024,512]{2,0,1:T(4,128)(2,1)} copy(bf16[3,1024,512]{2,1,0:T(8,128)(2,1)} %bitcast.28) | data formatting | bytes 6291456 | tf_op jit(solution)/shard_map/all_to_all | solution.py:59
  349.9 8.3 %all-to-all-start.2 = ((bf16[3,1024,512]{2,0,1:T(4,128)(2,1)}), bf16[3,1024,512]{2,0,1:T(4,128)(2,1)}, u32[]{:S(2)}, u32[]{:S(2)}) async-start(bf16[3,1024,512]{2,0,1:T(4,128)(2,1)} %copy.37), calls=%async_computation.2 | async-start | bytes 8388608 | tf_op jit(solution)/shard_map/all_to_all | solution.py:60
  358.2 0.7 scatter_custom_fusion
  358.9 0.1 convert_reduce_fusion
  359.0 0.7 gather_fusion.3
  359.7 90.9 %all-to-all-done.2 = bf16[3,1024,512]{2,0,1:T(4,128)(2,1)} async-done(((bf16[3,1024,512]{2,0,1:T(4,128)(2,1)}), bf16[3,1024,512]{2,0,1:T(4,128)(2,1)}, u32[]{:S(2)}, u32[]{:S(2)}) %all-to-all-start.2) | async-done | bytes 3145760 | tf_op jit(solution)/shard_map/all_to_all | solution.py:60
  450.6 3.0 copy.38
  453.6 0.0 copy-start.1
  453.6 1.9 copy.39
  455.5 4.1 gather_fusion.4
  459.6 0.0 copy-done.1
  (12 shorter events, 0.1 us)
Async XLA Ops:
  7.2 264.6 %copy-start = (bf16[3,512,1024]{2,1,0:T(8,128)(2,1)S(1)}, bf16[3,512,1024]{2,1,0:T(8,128)(2,1)}, u32[]{:S(2)}) copy-start(bf16[3,512,1024]{2,1,0:T(8,128)(2,1)} %param.8) | copy-start | bytes 9437188
  7.2 1.9 copy-start.2
  7.2 174.3 %all-gather.3.cloned.1.call-start = ((), (), s32[]{:S(2)}) async-start(), calls=%async_computation.3 | async-start | bytes 9437184 | tf_op jit(solution)/shard_map/all_gather | solution.py:44
  9.1 0.9 copy-start.4
  14.2 2.6 copy-start.3
  101.2 170.6 %all-gather.5.cloned.1.call-start = ((), (), s32[]{:S(2)}) async-start(), calls=%async_computation.4 | async-start | bytes 9437184 | tf_op jit(solution)/shard_map/all_gather | solution.py:52
  349.9 100.8 %all-to-all-start.2 = ((bf16[3,1024,512]{2,0,1:T(4,128)(2,1)}), bf16[3,1024,512]{2,0,1:T(4,128)(2,1)}, u32[]{:S(2)}, u32[]{:S(2)}) async-start(bf16[3,1024,512]{2,0,1:T(4,128)(2,1)} %copy.37), calls=%async_computation.2 | async-start | bytes 8388608 | tf_op jit(solution)/shard_map/all_to_all | solution.py:60
  453.6 6.0 %copy-start.1 = (bf16[3,512,1024]{2,1,0:T(8,128)(2,1)S(1)}, bf16[3,512,1024]{2,1,0:T(8,128)(2,1)}, u32[]{:S(2)}) copy-start(bf16[3,512,1024]{2,1,0:T(8,128)(2,1)} %param.8) | copy-start | bytes 9437188
Sparse Core Ops, SparseCore 0:
  101.3 80.1 all-gather.2
  190.5 81.2 all-gather.4
where the time goes:
time: 467 us; the launch traced here: 466 us
  waiting for transfers between devices  212 us (45%)
  blocking collectives  168 us (36%)
  local copies, waits for them, and re-layouts  32.6 us (7%)
  matrix products  18.1 us (4%)
  between operations  14.2 us (3%)
  other arithmetic  12.8 us (3%)
  starting transfers between devices  8.39 us (2%)
    all_to_all x1, waiting for transfers between devices, body(): lax.all_to_all(update_columns, 'dp', split_axis=1, concat_axis=0, tiled=T...  90.9 us
    all_gather x1, waiting for transfers between devices, body(): lax.all_gather(columns, 'tensor', axis=2, tiled=True)  80.3 us
    all_to_all x1, blocking collectives, body(): lax.all_to_all(outgoing, 'dp', split_axis=0, concat_axis=1, tiled=True)  76.1 us
    all_to_all x1, blocking collectives, body(): lax.all_to_all(scaled, 'tensor', split_axis=2, concat_axis=1, tiled=True)  48.3 us
    all_gather x1, waiting for transfers between devices, body(): lax.all_gather(product_half, 'tensor', axis=2, tiled=True)  40.9 us
    psum x1, blocking collectives, body(): block_squares = lax.psum(squares, ('dp', 'tensor'))  39.8 us
    all_to_all x3, local copies, waits for them, and re-layouts, body(): lax.all_to_all(scaled, 'tensor', split_axis=2, concat_axis=1, tiled=True)  10.1 us
  transfers between devices with their start and end apart: 3, of which 3 were waited for; matrix products, arithmetic and copies ran while one was open for 0% of the time, Pallas kernels for 0%

commit v1 on v0

v1 whole, which is shorter than its diff:
```python
import functools

import jax
import jax.numpy as jnp
from jax import lax
from jax.experimental import pallas as pl
from jax.experimental.pallas import tpu as pltpu
from jax.sharding import PartitionSpec as P

BETA = 0.9
EPS = 1e-06
MIB = 1 << 20


def tables(assign_list, owner_counts, cap):
    blocks, owners = assign_list.shape[0], owner_counts.shape[0]
    before = jnp.arange(owners)[None, :] < jnp.arange(owners)[:, None]
    offsets = jnp.sum(jnp.where(before, owner_counts[None, :], 0), axis=1)
    slots = jnp.arange(cap, dtype=jnp.int32)
    where_at = offsets[None, :] + slots[:, None]
    live = slots[:, None] < owner_counts[None, :]
    hit = (where_at[:, :, None] == jnp.arange(blocks)) & live[:, :, None]
    slot_block = jnp.sum(jnp.where(hit, assign_list, 0), axis=2)
    mine = (slot_block[:, :, None] == jnp.arange(blocks)) & live[:, :, None]
    place = jnp.arange(cap * owners, dtype=jnp.int32).reshape(cap, owners, 1)
    block_place = jnp.sum(jnp.where(mine, place, 0), axis=(0, 1))
    return slot_block, block_place


def root_kernel(parts, turn_ref, *refs):
    moments, right, lefts = refs[:parts], refs[parts], refs[parts + 1 : 2 * parts + 1]
    out_ref, square_ref, product = refs[2 * parts + 1 :]
    order, width = moments[0].shape
    step = min(256, order)
    turn = turn_ref[0]

    def places(d):
        at = lax.rem(turn - d + parts, parts) * width
        return pl.multiple_of(at, width)

    def first(i, carry):
        rows = pl.ds(pl.multiple_of(i * step, step), step)
        total = None
        for d in range(parts):
            term = lax.dot_general(
                moments[d][rows, :],
                right[0, :, pl.ds(places(d), width)],
                (((1,), (1,)), ((), ())),
                preferred_element_type=jnp.float32,
            )
            total = term if total is None else total + term
        product[rows, :] = total.astype(jnp.bfloat16)
        return carry

    lax.fori_loop(0, order // step, first, 0)
    small = min(256, width)
    squares = jnp.zeros((1, product.shape[1]), jnp.float32)
    for d in range(parts):
        def second(i, squares, d=d):
            at = pl.multiple_of(i * small, small)
            left = lefts[d][0, pl.ds(at, small), :] if d == 0 else lefts[d][pl.ds(at, small), :]
            direction = jnp.dot(left, product[...], preferred_element_type=jnp.float32)
            rows = pl.ds(pl.multiple_of(places(d) + at, small), small)
            out_ref[rows, :] = direction.astype(jnp.bfloat16)
            return squares + jnp.sum(direction * direction, axis=0, keepdims=True)

        squares = lax.fori_loop(0, width // small, second, squares)
    square_ref[...] = squares


def precondition(slot, turn, moments, right_root, left_root, lefts):
    parts = len(moments)
    order, width = moments[0].shape
    whole = pl.BlockSpec((order, width), lambda i, t: (0, 0))
    piece = pl.BlockSpec((width, order), lambda i, t: (0, 0))
    picked = pl.BlockSpec((1, width, order), lambda i, t: (slot, 0, 0))
    return pl.pallas_call(
        functools.partial(root_kernel, parts),
        grid_spec=pltpu.PrefetchScalarGridSpec(
            num_scalar_prefetch=1,
            grid=(1,),
            in_specs=[whole] * parts + [picked, picked] + [piece] * (parts - 1),
            out_specs=[whole, pl.BlockSpec((1, width), lambda i, t: (0, 0))],
            scratch_shapes=[pltpu.VMEM((order, width), jnp.bfloat16)],
        ),
        out_shape=[
            jax.ShapeDtypeStruct((order, width), jnp.bfloat16),
            jax.ShapeDtypeStruct((1, width), jnp.float32),
        ],
        compiler_params=pltpu.CompilerParams(vmem_limit_bytes=40 * MIB),
        cost_estimate=pl.CostEstimate(
            flops=4 * order * order * width, bytes_accessed=12 * order * width, transcendentals=0
        ),
    )(turn, *moments, right_root, left_root, *lefts)


def finish_kernel(place_ref, scale_ref, *refs):
    slots, out_ref = refs[:-1], refs[-1]
    owners = slots[0].shape[0]

    def one(b, carry):
        place = place_ref[b]
        scale = scale_ref[b]
        for s, slot in enumerate(slots):
            @pl.when(place // owners == s)
            def _(slot=slot, s=s):
                value = slot[place - s * owners].astype(jnp.float32) * scale
                out_ref[b] = value.astype(jnp.bfloat16)
        return carry

    lax.fori_loop(0, out_ref.shape[0], one, 0)


def finish(block_place, scale, arrived):
    owners, rows, columns = arrived[0].shape
    blocks = block_place.shape[0]
    full = pl.BlockSpec((owners, rows, columns), lambda i, *_: (0, 0, 0))
    return pl.pallas_call(
        finish_kernel,
        grid_spec=pltpu.PrefetchScalarGridSpec(
            num_scalar_prefetch=2,
            grid=(1,),
            in_specs=[full] * len(arrived),
            out_specs=pl.BlockSpec((blocks, rows, columns), lambda i, *_: (0, 0, 0)),
        ),
        out_shape=jax.ShapeDtypeStruct((blocks, rows, columns), jnp.bfloat16),
        compiler_params=pltpu.CompilerParams(vmem_limit_bytes=40 * MIB),
    )(block_place, scale, *arrived)


def body(parts, grads, momentum, left_root, right_root, assign_list, owner_counts):
    cap, width, order = left_root.shape
    owners = owner_counts.shape[0]
    cells = float(order * order)
    turn = lax.axis_index("tensor").astype(jnp.int32).reshape(1)
    me = lax.axis_index("dp")

    def around(x):
        return [
            lax.ppermute(x, "tensor", [(s, (s + d) % parts) for s in range(parts)])
            for d in range(1, parts)
        ]

    slot_block, block_place = tables(assign_list, owner_counts, cap)
    moment_out = BETA * momentum + (1.0 - BETA) * grads.astype(jnp.float32)
    moment_half = moment_out.astype(jnp.bfloat16)
    squares = jnp.sum(moment_out * moment_out, axis=(1, 2))

    lefts = [around(left_root[s]) for s in range(cap)]
    arrived, direction_squares = [], []
    for s in range(cap):
        outgoing = moment_half[slot_block[s]]
        columns = lax.all_to_all(outgoing, "dp", split_axis=0, concat_axis=0, tiled=True)
        columns = columns.reshape(order, width)
        direction, square = precondition(
            s, turn, [columns] + around(columns), right_root, left_root, lefts[s]
        )
        direction_squares.append(jnp.sum(square))
        direction = direction.reshape(owners, order // owners, width)
        arrived.append(lax.all_to_all(direction, "dp", split_axis=0, concat_axis=0, tiled=True))
    own = jnp.where(jnp.arange(owners)[None, :] == me, jnp.stack(direction_squares)[:, None], 0.0)
    sums = lax.psum(jnp.concatenate([squares, own.reshape(-1)]), ("dp", "tensor"))
    blocks = squares.shape[0]
    owned = sums[blocks:][block_place]
    scale = jnp.sqrt(sums[:blocks] / cells + EPS) / jnp.sqrt(owned / cells + EPS)
    return (moment_out, finish(block_place, scale, arrived))


def solution(mesh):
    parts = mesh.shape["tensor"]
    in_specs = (
        P(None, "dp", "tensor"),
        P(None, "dp", "tensor"),
        P("dp", "tensor", None),
        P("dp", "tensor", None),
        P(),
        P(),
    )
    out_specs = (P(None, "dp", "tensor"), P(None, "dp", "tensor"))
    return jax.shard_map(
        functools.partial(body, parts), mesh=mesh, in_specs=in_specs, out_specs=out_specs, check_vma=False
    )
```

time: 467 us -> 319 us (0.68)
  blocking collectives: 168 us -> 39.7 us
  starting transfers between devices: 8.39 us -> 41.4 us
  waiting for transfers between devices: 212 us -> 180 us
  Pallas kernels: 0 us -> 20 us
  matrix products: 18.1 us -> 0 us
  between operations: 14.2 us -> 0.78 us
  local copies, waits for them, and re-layouts: 32.6 us -> 21.4 us
    ppermute x0 -> x6, waiting for transfers between devices: none -> 137 us  [around(): lax.ppermute(x, 'tensor', [(s, (s + d) % parts) for s in range(parts)])]
    all_to_all x2 -> x0, blocking collectives: 124 us -> none  [the longest x1 76.1 us: body(): lax.all_to_all(outgoing, 'dp', split_axis=0, concat_axis=1, tiled=True)]
    all_gather x2 -> x0, waiting for transfers between devices: 121 us -> none  [the longest x1 80.3 us: body(): lax.all_gather(columns, 'tensor', axis=2, tiled=True)]
    all_to_all x1 -> x6, waiting for transfers between devices: 90.9 us -> 43.4 us  [the longest x3 43.3 us: body(): lax.all_to_all(outgoing, 'dp', split_axis=0, concat_axis=0, tiled=True)]
    all_to_all x1 -> x6, starting transfers between devices: 8.31 us -> 37 us  [the longest x3 20.6 us: body(): lax.all_to_all(direction, 'dp', split_axis=0, concat_axis=0, tiled=True)]
    pallas_call x0 -> x4, Pallas kernels: none -> 20 us  [the longest x3 15.4 us: precondition(): pl.pallas_call(functools.partial(root_kernel, parts), grid_spec=pltpu.Pre...]
    dot_general x2 -> x0, matrix products: 18.1 us -> none  [the longest x1 9.27 us: body(): jnp.einsum('sij,sjk->sik', left_root, lax.all_gather(product_half, 'tenso...]
    all_to_all x6 -> x0, local copies, waits for them, and re-layouts: 16.9 us -> none  [the longest x3 10.1 us: body(): lax.all_to_all(scaled, 'tensor', split_axis=2, concat_axis=1, tiled=True)]
  transfers between devices with their start and end apart: 3 -> 12, of which waited for: 3 -> 8; matrix products, arithmetic and copies ran while one was open for 0% -> 4% of each run, Pallas kernels for 0% -> 5%
where the time goes in v1:
time: 319 us; the launch traced here: 314 us
  waiting for transfers between devices  180 us (56%)
  starting transfers between devices  41.4 us (13%)
  blocking collectives  39.7 us (12%)
  local copies, waits for them, and re-layouts  21.4 us (7%)
  Pallas kernels  20 us (6%)
  other arithmetic  10.6 us (3%)
    ppermute x6, waiting for transfers between devices, around(): lax.ppermute(x, 'tensor', [(s, (s + d) % parts) for s in range(parts)])  137 us
    all_to_all x3, waiting for transfers between devices, body(): lax.all_to_all(outgoing, 'dp', split_axis=0, concat_axis=0, tiled=True)  43.3 us
    psum x1, blocking collectives, body(): lax.psum(jnp.concatenate([squares, own.reshape(-1)]), ('dp', 'tensor'))  39.7 us
    all_to_all x3, starting transfers between devices, body(): lax.all_to_all(direction, 'dp', split_axis=0, concat_axis=0, tiled=True)  20.6 us
    all_to_all x3, starting transfers between devices, body(): lax.all_to_all(outgoing, 'dp', split_axis=0, concat_axis=0, tiled=True)  16.4 us
    pallas_call x3, Pallas kernels, precondition(): pl.pallas_call(functools.partial(root_kernel, parts), grid_spec=pltpu.Pre...  15.4 us
    unnamed x18, local copies, waits for them, and re-layouts  10.6 us
    gather x3, local copies, waits for them, and re-layouts, body(): outgoing = moment_half[slot_block[s]]  8.24 us
  transfers between devices with their start and end apart: 12, of which 8 were waited for; matrix products, arithmetic and copies ran while one was open for 4% of the time, Pallas kernels for 5%

profile of v1, /device:TPU:11, one launch (start us, length us, event | category | flops | bytes accessed | tf_op | source)
XLA Modules:
  0.0 314.3 jit_solution(6578272606637887760)
XLA Ops:
  0.6 0.7 iota_compare_fusion.3
  1.3 0.8 select_reduce_fusion.2
  2.1 0.9 select_reduce_fusion.1
  3.0 3.9 %multiply_reduce_fusion = (f32[32]{0:T(128)S(1)}, f32[32,64,512]{2,1,0:T(8,128)S(1)}) fusion(bf16[32,64,512]{2,1,0:T(8,128)(2,1)} %param.6, f32[32,64,512]{2,1,0:T(8,128)} %param.7), kind=kLoop, calls=%fused_computation.4 | loop fusion | flops 6291424 | bytes 10485888 | tf_op jit(solution)/shard_map/reduce_sum | solution.py:147
  6.9 0.0 copy-start.7
  6.9 2.0 copy-done.7
  8.9 0.3 convert_element_type.7
  9.2 0.0 copy-start.8
  9.2 1.7 gather_fusion.2
  10.9 6.6 %all-to-all-start.2 = ((bf16[16,64,512]{2,1,0:T(8,128)(2,1)}), bf16[16,64,512]{2,1,0:T(8,128)(2,1)}, u32[]{:S(2)}, u32[]{:S(2)}) async-start(bf16[16,64,512]{2,1,0:T(8,128)(2,1)} %gather_fusion.2), calls=%async_computation.2 | async-start | bytes 2097152 | tf_op jit(solution)/shard_map/all_to_all | solution.py:153
  17.4 0.0 copy-done.8
  17.4 0.0 copy-start
  17.5 3.4 %gather_fusion.1 = bf16[16,64,512]{2,1,0:T(8,128)(2,1)} fusion(bf16[32,64,512]{2,1,0:T(8,128)(2,1)} %copy-done.8, s32[1024]{0:T(1024)S(1)} %pad_clamp_fusion.2), kind=kCustom, calls=%fused_computation.1 | custom fusion | bytes 2097216 | tf_op jit(solution)/shard_map/gather | solution.py:152
  20.8 21.6 %all-to-all-done.2 = bf16[16,64,512]{2,1,0:T(8,128)(2,1)} async-done(((bf16[16,64,512]{2,1,0:T(8,128)(2,1)}), bf16[16,64,512]{2,1,0:T(8,128)(2,1)}, u32[]{:S(2)}, u32[]{:S(2)}) %all-to-all-start.2) | async-done | bytes 1048608 | tf_op jit(solution)/shard_map/all_to_all | solution.py:153
  42.4 4.9 %all-to-all-start.1 = ((bf16[16,64,512]{2,1,0:T(8,128)(2,1)}), bf16[16,64,512]{2,1,0:T(8,128)(2,1)}, u32[]{:S(2)}, u32[]{:S(2)}) async-start(bf16[16,64,512]{2,1,0:T(8,128)(2,1)} %gather_fusion.1), calls=%async_computation.1 | async-start | bytes 2097152 | tf_op jit(solution)/shard_map/all_to_all | solution.py:153
  47.4 3.2 %gather_fusion = bf16[16,64,512]{2,1,0:T(8,128)(2,1)} fusion(bf16[32,64,512]{2,1,0:T(8,128)(2,1)} %copy-done.8, s32[1024]{0:T(1024)S(1)} %pad_clamp_fusion.3), kind=kCustom, calls=%fused_computation | custom fusion | bytes 2097216 | tf_op jit(solution)/shard_map/gather | solution.py:152
  50.6 21.8 %all-to-all-done.1 = bf16[16,64,512]{2,1,0:T(8,128)(2,1)} async-done(((bf16[16,64,512]{2,1,0:T(8,128)(2,1)}), bf16[16,64,512]{2,1,0:T(8,128)(2,1)}, u32[]{:S(2)}, u32[]{:S(2)}) %all-to-all-start.1) | async-done | bytes 1048608 | tf_op jit(solution)/shard_map/all_to_all | solution.py:153
  72.3 4.9 %all-to-all-start = ((bf16[16,64,512]{2,1,0:T(8,128)(2,1)}), bf16[16,64,512]{2,1,0:T(8,128)(2,1)}, u32[]{:S(2)}, u32[]{:S(2)}) async-start(bf16[16,64,512]{2,1,0:T(8,128)(2,1)} %gather_fusion), calls=%async_computation | async-start | bytes 2097152 | tf_op jit(solution)/shard_map/all_to_all | solution.py:153
  77.3 0.0 copy-done
  77.3 1.8 slice_bitcast_fusion.2
  79.0 1.2 collective-permute-start.3
  80.3 0.2 collective-permute-start.2
  80.5 23.2 %collective-permute-done.3.refs_4_ = bf16[512,1024]{1,0:T(8,128)(2,1)} collective-permute-done((bf16[512,1024]{1,0:T(8,128)(2,1)}, bf16[512,1024]{1,0:T(8,128)(2,1)}, u32[]{:S(2)}, u32[]{:S(2)}) %collective-permute-start.3) | collective-permute-done | bytes 1048608 | tf_op jit(solution)/shard_map/ppermute | solution.py:140
  103.8 22.5 %collective-permute-done.2.refs_1_ = bf16[1024,512]{1,0:T(8,128)(2,1)} collective-permute-done((bf16[1024,512]{1,0:T(8,128)(2,1)}, bf16[1024,512]{1,0:T(8,128)(2,1)}, u32[]{:S(2)}, u32[]{:S(2)}) %collective-permute-start.2) | collective-permute-done | bytes 1048608 | tf_op jit(solution)/shard_map/ppermute | solution.py:140
  126.2 0.0 copy-start.1
  126.2 1.9 copy-done.1
  128.1 5.5 %shard_map.78 = (bf16[1024,512]{1,0:T(8,128)(2,1)S(1)}, f32[1,512]{1,0:T(1,128)S(1)}) custom-call(s32[1]{0:T(128)} %bitcast.turn_ref, bf16[1024,512]{1,0:T(8,128)(2,1)} %bitcast.8.refs_0_, bf16[1024,512]{1,0:T(8,128)(2,1)} %collective-permute-done.2.refs_1_, bf16[3,512,1024]{2,1,0:T(8,128)(2,1)S(1)} %copy-done.1, bf16[3,512,1024]{2,1,0:T(8,128)(2,1)S(1)} %copy-done, ...), custom_call_target="tpu_custom_call" | custom-call | flops 2147483648 | bytes 6291456 | tf_op jit(solution)/shard_map/pallas_call | solution.py:77
  133.7 0.0 copy-start.6
  133.7 1.0 copy-done.6
  134.6 0.0 all-to-all-done
  134.6 6.9 %all-to-all-start.4 = ((bf16[16,64,512]{2,1,0:T(8,128)(2,1)}), bf16[16,64,512]{2,1,0:T(8,128)(2,1)}, u32[]{:S(2)}, u32[]{:S(2)}) async-start(bf16[16,64,512]{2,1,0:T(8,128)(2,1)} %bitcast.34), calls=%async_computation.4 | async-start | bytes 2097152 | tf_op jit(solution)/shard_map/all_to_all | solution.py:160
  141.5 1.2 collective-permute-start.1
  142.7 0.2 collective-permute-start
  142.9 23.2 %collective-permute-done.1.refs_4_ = bf16[512,1024]{1,0:T(8,128)(2,1)S(1)} collective-permute-done((bf16[512,1024]{1,0:T(8,128)(2,1)}, bf16[512,1024]{1,0:T(8,128)(2,1)S(1)}, u32[]{:S(2)}, u32[]{:S(2)}) %collective-permute-start.1) | collective-permute-done | bytes 1048608 | tf_op jit(solution)/shard_map/ppermute | solution.py:140
  166.2 22.4 %collective-permute-done.refs_1_ = bf16[1024,512]{1,0:T(8,128)(2,1)S(1)} collective-permute-done((bf16[1024,512]{1,0:T(8,128)(2,1)}, bf16[1024,512]{1,0:T(8,128)(2,1)S(1)}, u32[]{:S(2)}, u32[]{:S(2)}) %collective-permute-start) | collective-permute-done | bytes 1048608 | tf_op jit(solution)/shard_map/ppermute | solution.py:140
  188.5 1.9 copy-done.2
  190.4 4.9 %shard_map.77 = (bf16[1024,512]{1,0:T(8,128)(2,1)S(1)}, f32[1,512]{1,0:T(1,128)S(1)}) custom-call(s32[1]{0:T(128)} %bitcast.turn_ref, bf16[1024,512]{1,0:T(8,128)(2,1)} %bitcast.3.refs_0_, bf16[1024,512]{1,0:T(8,128)(2,1)S(1)} %collective-permute-done.refs_1_, bf16[3,512,1024]{2,1,0:T(8,128)(2,1)S(1)} %copy-done.2, bf16[3,512,1024]{2,1,0:T(8,128)(2,1)S(1)} %copy-done, ...), custom_call_target="tpu_custom_call" | custom-call | flops 2147483648 | bytes 6291456 | tf_op jit(solution)/shard_map/pallas_call | solution.py:77
  195.3 0.0 copy-start.5
  195.4 1.0 copy-done.5
  196.3 0.0 all-to-all-done.4.refs_1_
  196.3 6.9 %all-to-all-start.3 = ((bf16[16,64,512]{2,1,0:T(8,128)(2,1)}), bf16[16,64,512]{2,1,0:T(8,128)(2,1)}, u32[]{:S(2)}, u32[]{:S(2)}) async-start(bf16[16,64,512]{2,1,0:T(8,128)(2,1)} %bitcast.33), calls=%async_computation.3 | async-start | bytes 2097152 | tf_op jit(solution)/shard_map/all_to_all | solution.py:160
  203.2 1.2 collective-permute-start.5
  204.4 0.2 collective-permute-start.4
  204.6 23.2 %collective-permute-done.5.refs_4_ = bf16[512,1024]{1,0:T(8,128)(2,1)S(1)} collective-permute-done((bf16[512,1024]{1,0:T(8,128)(2,1)}, bf16[512,1024]{1,0:T(8,128)(2,1)S(1)}, u32[]{:S(2)}, u32[]{:S(2)}) %collective-permute-start.5) | collective-permute-done | bytes 1048608 | tf_op jit(solution)/shard_map/ppermute | solution.py:140
  227.9 22.4 %collective-permute-done.4.refs_1_ = bf16[1024,512]{1,0:T(8,128)(2,1)S(1)} collective-permute-done((bf16[1024,512]{1,0:T(8,128)(2,1)}, bf16[1024,512]{1,0:T(8,128)(2,1)S(1)}, u32[]{:S(2)}, u32[]{:S(2)}) %collective-permute-start.4) | collective-permute-done | bytes 1048608 | tf_op jit(solution)/shard_map/ppermute | solution.py:140
  250.2 1.9 copy-done.3
  252.1 4.9 %shard_map.79 = (bf16[1024,512]{1,0:T(8,128)(2,1)S(1)}, f32[1,512]{1,0:T(1,128)S(1)}) custom-call(s32[1]{0:T(128)} %bitcast.turn_ref, bf16[1024,512]{1,0:T(8,128)(2,1)} %bitcast.13.refs_0_, bf16[1024,512]{1,0:T(8,128)(2,1)S(1)} %collective-permute-done.4.refs_1_, bf16[3,512,1024]{2,1,0:T(8,128)(2,1)S(1)} %copy-done.3, bf16[3,512,1024]{2,1,0:T(8,128)(2,1)S(1)} %copy-done, ...), custom_call_target="tpu_custom_call" | custom-call | flops 2147483648 | bytes 6291456 | tf_op jit(solution)/shard_map/pallas_call | solution.py:77
  257.0 0.0 copy-start.4
  257.1 1.0 copy-done.4
  258.0 0.0 all-to-all-done.3.refs_0_
  258.0 6.9 %all-to-all-start.5 = ((bf16[16,64,512]{2,1,0:T(8,128)(2,1)}), bf16[16,64,512]{2,1,0:T(8,128)(2,1)S(1)}, u32[]{:S(2)}, u32[]{:S(2)}) async-start(bf16[16,64,512]{2,1,0:T(8,128)(2,1)} %bitcast.32), calls=%async_computation.5 | async-start | bytes 2097152 | tf_op jit(solution)/shard_map/all_to_all | solution.py:160
  264.9 0.1 select_reduce_fusion.place_ref
  265.0 0.6 reduce_sum.70
  265.6 0.6 reduce_sum.69
  266.3 0.6 reduce_sum.71
  266.9 2.0 pad_maximum_fusion
  268.8 0.1 broadcast_select_fusion
  268.9 0.1 select_n.67
  269.0 0.1 pad_maximum_fusion.1
  269.1 39.7 %psum.7 = f32[80]{0:T(128)S(1)} all-reduce(f32[80]{0:T(128)S(1)} %pad_maximum_fusion.1), channel_id=1, replica_groups=mesh['dp'=16,'tensor'=2] {'dp','tensor'}, use_global_device_ids=true, to_apply=%region_7.8 | all-reduce | flops 80 | bytes 640 | tf_op jit(solution)/shard_map/psum | solution.py:162
  308.8 0.1 slice.31
  308.9 0.7 gather_fusion.3
  309.6 0.0 all-to-all-done.5.refs_2_
  309.6 4.7 %shard_map.80 = bf16[32,64,512]{2,1,0:T(8,128)(2,1)} custom-call(s32[32]{0:T(128)S(1)} %select_reduce_fusion.place_ref, f32[32]{0:T(128)S(1)} %rsqrt_multiply_fusion.scale_ref, bf16[16,64,512]{2,1,0:T(8,128)(2,1)} %all-to-all-done.3.refs_0_, bf16[16,64,512]{2,1,0:T(8,128)(2,1)} %all-to-all-done.4.refs_1_, bf16[16,64,512]{2,1,0:T(8,128)(2,1)S(1)} %all-to-all-done.5.refs_2_), custom_call_target="tpu_custom_call" | custom-call | tf_op jit(solution)/shard_map/pallas_call | solution.py:118
  (12 shorter events, 0.1 us)
Async XLA Ops:
  6.9 2.0 copy-start.7
  9.2 8.2 %copy-start.8 = (bf16[32,64,512]{2,1,0:T(8,128)(2,1)}, bf16[32,64,512]{2,1,0:T(8,128)(2,1)S(1)}, u32[]{:S(2)}) copy-start(bf16[32,64,512]{2,1,0:T(8,128)(2,1)S(1)} %convert_element_type.7) | copy-start | bytes 6291460
  10.9 31.5 %all-to-all-start.2 = ((bf16[16,64,512]{2,1,0:T(8,128)(2,1)}), bf16[16,64,512]{2,1,0:T(8,128)(2,1)}, u32[]{:S(2)}, u32[]{:S(2)}) async-start(bf16[16,64,512]{2,1,0:T(8,128)(2,1)} %gather_fusion.2), calls=%async_computation.2 | async-start | bytes 2097152 | tf_op jit(solution)/shard_map/all_to_all | solution.py:153
  17.4 59.8 %copy-start = (bf16[3,512,1024]{2,1,0:T(8,128)(2,1)S(1)}, bf16[3,512,1024]{2,1,0:T(8,128)(2,1)}, u32[]{:S(2)}) copy-start(bf16[3,512,1024]{2,1,0:T(8,128)(2,1)} %refs_3_.5) | copy-start | bytes 9437188
  42.4 29.9 %all-to-all-start.1 = ((bf16[16,64,512]{2,1,0:T(8,128)(2,1)}), bf16[16,64,512]{2,1,0:T(8,128)(2,1)}, u32[]{:S(2)}, u32[]{:S(2)}) async-start(bf16[16,64,512]{2,1,0:T(8,128)(2,1)} %gather_fusion.1), calls=%async_computation.1 | async-start | bytes 2097152 | tf_op jit(solution)/shard_map/all_to_all | solution.py:153
  72.3 62.3 %all-to-all-start = ((bf16[16,64,512]{2,1,0:T(8,128)(2,1)}), bf16[16,64,512]{2,1,0:T(8,128)(2,1)}, u32[]{:S(2)}, u32[]{:S(2)}) async-start(bf16[16,64,512]{2,1,0:T(8,128)(2,1)} %gather_fusion), calls=%async_computation | async-start | bytes 2097152 | tf_op jit(solution)/shard_map/all_to_all | solution.py:153
  79.0 24.7 %collective-permute-start.3 = (bf16[512,1024]{1,0:T(8,128)(2,1)}, bf16[512,1024]{1,0:T(8,128)(2,1)}, u32[]{:S(2)}, u32[]{:S(2)}) collective-permute-start(bf16[512,1024]{1,0:T(8,128)(2,1)} %get-tuple-element.17), channel_id=1, source_target_pairs={{0,1},{1,0},{2,3},{3,2},{4,5},{5,4},{6,7},{7,6},{8,9},{9,8},{10,11... | collective-permute-start | bytes 3145736 | tf_op jit(solution)/shard_map/ppermute | solution.py:140
  80.3 45.9 %collective-permute-start.2 = (bf16[1024,512]{1,0:T(8,128)(2,1)}, bf16[1024,512]{1,0:T(8,128)(2,1)}, u32[]{:S(2)}, u32[]{:S(2)}) collective-permute-start(bf16[1024,512]{1,0:T(8,128)(2,1)} %bitcast.8.refs_0_), channel_id=1, source_target_pairs={{0,1},{1,0},{2,3},{3,2},{4,5},{5,4},{6,7},{7,6},{8,9},{9,8},{10,11... | collective-permute-start | bytes 3145736 | tf_op jit(solution)/shard_map/ppermute | solution.py:140
  126.2 1.9 copy-start.1
  133.7 1.0 copy-start.6
  134.6 61.7 %all-to-all-start.4 = ((bf16[16,64,512]{2,1,0:T(8,128)(2,1)}), bf16[16,64,512]{2,1,0:T(8,128)(2,1)}, u32[]{:S(2)}, u32[]{:S(2)}) async-start(bf16[16,64,512]{2,1,0:T(8,128)(2,1)} %bitcast.34), calls=%async_computation.4 | async-start | bytes 2097152 | tf_op jit(solution)/shard_map/all_to_all | solution.py:160
  141.5 24.7 %collective-permute-start.1 = (bf16[512,1024]{1,0:T(8,128)(2,1)}, bf16[512,1024]{1,0:T(8,128)(2,1)S(1)}, u32[]{:S(2)}, u32[]{:S(2)}) collective-permute-start(bf16[512,1024]{1,0:T(8,128)(2,1)} %get-tuple-element.16), channel_id=1, source_target_pairs={{0,1},{1,0},{2,3},{3,2},{4,5},{5,4},{6,7},{7,6},{8,9},{9,8},{10,11... | collective-permute-start | bytes 3145736 | tf_op jit(solution)/shard_map/ppermute | solution.py:140
  142.7 45.8 %collective-permute-start = (bf16[1024,512]{1,0:T(8,128)(2,1)}, bf16[1024,512]{1,0:T(8,128)(2,1)S(1)}, u32[]{:S(2)}, u32[]{:S(2)}) collective-permute-start(bf16[1024,512]{1,0:T(8,128)(2,1)} %bitcast.3.refs_0_), channel_id=1, source_target_pairs={{0,1},{1,0},{2,3},{3,2},{4,5},{5,4},{6,7},{7,6},{8,9},{9,8},{10,11... | collective-permute-start | bytes 3145736 | tf_op jit(solution)/shard_map/ppermute | solution.py:140
  188.5 1.9 copy-start.2
  195.3 1.0 copy-start.5
  196.3 61.7 %all-to-all-start.3 = ((bf16[16,64,512]{2,1,0:T(8,128)(2,1)}), bf16[16,64,512]{2,1,0:T(8,128)(2,1)}, u32[]{:S(2)}, u32[]{:S(2)}) async-start(bf16[16,64,512]{2,1,0:T(8,128)(2,1)} %bitcast.33), calls=%async_computation.3 | async-start | bytes 2097152 | tf_op jit(solution)/shard_map/all_to_all | solution.py:160
  203.2 24.7 %collective-permute-start.5 = (bf16[512,1024]{1,0:T(8,128)(2,1)}, bf16[512,1024]{1,0:T(8,128)(2,1)S(1)}, u32[]{:S(2)}, u32[]{:S(2)}) collective-permute-start(bf16[512,1024]{1,0:T(8,128)(2,1)} %get-tuple-element.18), channel_id=1, source_target_pairs={{0,1},{1,0},{2,3},{3,2},{4,5},{5,4},{6,7},{7,6},{8,9},{9,8},{10,11... | collective-permute-start | bytes 3145736 | tf_op jit(solution)/shard_map/ppermute | solution.py:140
  204.4 45.8 %collective-permute-start.4 = (bf16[1024,512]{1,0:T(8,128)(2,1)}, bf16[1024,512]{1,0:T(8,128)(2,1)S(1)}, u32[]{:S(2)}, u32[]{:S(2)}) collective-permute-start(bf16[1024,512]{1,0:T(8,128)(2,1)} %bitcast.13.refs_0_), channel_id=1, source_target_pairs={{0,1},{1,0},{2,3},{3,2},{4,5},{5,4},{6,7},{7,6},{8,9},{9,8},{10,11... | collective-permute-start | bytes 3145736 | tf_op jit(solution)/shard_map/ppermute | solution.py:140
  250.2 1.9 copy-start.3
  257.0 1.0 copy-start.4
  258.0 51.6 %all-to-all-start.5 = ((bf16[16,64,512]{2,1,0:T(8,128)(2,1)}), bf16[16,64,512]{2,1,0:T(8,128)(2,1)S(1)}, u32[]{:S(2)}, u32[]{:S(2)}) async-start(bf16[16,64,512]{2,1,0:T(8,128)(2,1)} %bitcast.32), calls=%async_computation.5 | async-start | bytes 2097152 | tf_op jit(solution)/shard_map/all_to_all | solution.py:160

commit v2 on v0

v2 whole, which is shorter than its diff:
```python
import functools

import jax
import jax.numpy as jnp
from jax import lax
from jax.experimental import pallas as pl
from jax.experimental.pallas import tpu as pltpu
from jax.sharding import PartitionSpec as P

BETA = 0.9
EPS = 1e-06
MIB = 1 << 20
ANY = pl.BlockSpec(memory_space=pl.ANY)


def for_slots(slots, assign_ref, count_ref, visit):
    owners = count_ref.shape[0]

    def one(o, offset):
        count = count_ref[o]
        for k, s in enumerate(slots):
            @pl.when(s < count)
            def _(k=k, s=s):
                visit(k * owners + o, assign_ref[offset + s], k, o)
        return offset + count

    lax.fori_loop(0, owners, one, 0)


def moment_kernel(slots, assign_ref, count_ref, *refs):
    grads, momentum = refs[:2]
    moment_out, outgoing, grad, old, new, half, in_sem, out_sem = refs[-8:]

    def reads(i, b):
        return (
            pltpu.make_async_copy(grads.at[b], grad.at[i], in_sem.at[0, i]),
            pltpu.make_async_copy(momentum.at[b], old.at[i], in_sem.at[1, i]),
        )

    def writes(i, b, k, o):
        return (
            pltpu.make_async_copy(half.at[i], outgoing.at[k, o], out_sem.at[0, i]),
            pltpu.make_async_copy(new.at[i], moment_out.at[b], out_sem.at[1, i]),
        )

    def start(i, b, k, o):
        for copy in reads(i, b):
            copy.start()

    def work(i, b, k, o):
        for copy in reads(i, b):
            copy.wait()
        moment = BETA * old[i] + (1.0 - BETA) * grad[i].astype(jnp.float32)
        new[i] = moment
        half[i] = moment.astype(jnp.bfloat16)
        for copy in writes(i, b, k, o):
            copy.start()

    def end(i, b, k, o):
        for copy in writes(i, b, k, o):
            copy.wait()

    for visit in (start, work, end):
        for_slots(slots, assign_ref, count_ref, visit)


def make_moment(slots, assign_list, owner_counts, grads, momentum, *earlier):
    blocks, rows, columns = grads.shape
    owners = owner_counts.shape[0]
    n = len(slots) * owners
    return pl.pallas_call(
        functools.partial(moment_kernel, slots),
        grid_spec=pltpu.PrefetchScalarGridSpec(
            num_scalar_prefetch=2,
            grid=(1,),
            in_specs=[ANY] * (2 + len(earlier)),
            out_specs=[ANY, ANY],
            scratch_shapes=[
                pltpu.VMEM((n, rows, columns), jnp.bfloat16),
                pltpu.VMEM((n, rows, columns), jnp.float32),
                pltpu.VMEM((n, rows, columns), jnp.float32),
                pltpu.VMEM((n, rows, columns), jnp.bfloat16),
                pltpu.SemaphoreType.DMA((2, n)),
                pltpu.SemaphoreType.DMA((2, n)),
            ],
        ),
        out_shape=[
            jax.ShapeDtypeStruct((blocks, rows, columns), jnp.float32),
            jax.ShapeDtypeStruct((len(slots), owners, rows, columns), jnp.bfloat16),
        ],
        input_output_aliases={4: 0} if earlier else {},
        compiler_params=pltpu.CompilerParams(vmem_limit_bytes=60 * MIB),
        cost_estimate=pl.CostEstimate(
            flops=3 * n * rows * columns, bytes_accessed=12 * n * rows * columns, transcendentals=0
        ),
    )(assign_list, owner_counts, grads, momentum, *earlier)


def finish_kernel(assign_ref, count_ref, scale_ref, *refs):
    arrived, update = refs[:-1], refs[-1]
    owners = count_ref.shape[0]

    def one(i, b, k, o):
        value = arrived[k][o].astype(jnp.float32) * scale_ref[k * owners + o]
        update[b] = value.astype(jnp.bfloat16)

    for_slots(range(len(arrived)), assign_ref, count_ref, one)


def finish(assign_list, owner_counts, scale, arrived):
    owners, rows, columns = arrived[0].shape
    blocks = assign_list.shape[0]
    full = pl.BlockSpec((owners, rows, columns), lambda i, *_: (0, 0, 0))
    return pl.pallas_call(
        finish_kernel,
        grid_spec=pltpu.PrefetchScalarGridSpec(
            num_scalar_prefetch=3,
            grid=(1,),
            in_specs=[full] * len(arrived),
            out_specs=pl.BlockSpec((blocks, rows, columns), lambda i, *_: (0, 0, 0)),
        ),
        out_shape=jax.ShapeDtypeStruct((blocks, rows, columns), jnp.bfloat16),
        compiler_params=pltpu.CompilerParams(vmem_limit_bytes=60 * MIB),
    )(assign_list, owner_counts, scale, *arrived)


def root_kernel(parts, count, turn_ref, *refs):
    moments, right, own_left, lefts = refs[:parts], refs[parts], refs[parts + 1], refs[parts + 2 : -3]
    out_ref, square_ref, product = refs[-3:]
    order, width = moments[0].shape
    step = min(256, order)
    turn = turn_ref[0]

    def position(d):
        return pl.multiple_of(lax.rem(turn - d + parts, parts) * width, width)

    def first(i, squares):
        rows = pl.ds(pl.multiple_of(i * step, step), step)
        total = None
        for d in range(parts):
            moment = moments[d][rows, :]
            term = lax.dot_general(
                moment,
                right[0, :, pl.ds(position(d), width)],
                (((1,), (1,)), ((), ())),
                preferred_element_type=jnp.float32,
            )
            total = term if total is None else total + term
            wide = moment.astype(jnp.float32)
            squares = squares + jnp.sum(wide * wide, axis=0, keepdims=True)
        product[rows, :] = total.astype(jnp.bfloat16)
        return squares

    zero = jnp.zeros((1, width), jnp.float32)
    moment_squares = lax.fori_loop(0, order // step, first, zero)
    squares = zero
    pieces = [(own_left.at[0], position(0))]
    for d in range(1, parts):
        base = position(d)
        for ref in lefts[(d - 1) * count : d * count]:
            pieces.append((ref, base))
            base = base + ref.shape[0]
    for left, base in pieces:
        height = left.shape[0]
        small = 256 if height % 256 == 0 else height
        for i in range(height // small):
            direction = jnp.dot(left[i * small : (i + 1) * small, :], product[...], preferred_element_type=jnp.float32)
            out_ref[pl.ds(pl.multiple_of(base + i * small, 16), small), :] = direction.astype(jnp.bfloat16)
            squares = squares + jnp.sum(direction * direction, axis=0, keepdims=True)
    for r, lines in enumerate((moment_squares, squares)):
        square_ref[r : r + 1, :] = jnp.broadcast_to(jnp.sum(lines, axis=1, keepdims=True), (1, 128))


def precondition(slot, turn, moments, right_root, left_root, lefts):
    parts = len(moments)
    order, width = moments[0].shape
    whole = pl.BlockSpec((order, width), lambda i, t: (0, 0))
    picked = pl.BlockSpec((1, width, order), lambda i, t: (slot, 0, 0))
    pieces = [piece for one in lefts for piece in one]
    return pl.pallas_call(
        functools.partial(root_kernel, parts, len(lefts[0])),
        grid_spec=pltpu.PrefetchScalarGridSpec(
            num_scalar_prefetch=1,
            grid=(1,),
            in_specs=[whole] * parts
            + [picked, picked]
            + [pl.BlockSpec((rows, order), lambda i, t, at=at: (at, 0)) for _, rows, at in pieces],
            out_specs=[whole, pl.BlockSpec((2, 128), lambda i, t: (0, 0))],
            scratch_shapes=[pltpu.VMEM((order, width), jnp.bfloat16)],
        ),
        out_shape=[
            jax.ShapeDtypeStruct((order, width), jnp.bfloat16),
            jax.ShapeDtypeStruct((2, 128), jnp.float32),
        ],
        compiler_params=pltpu.CompilerParams(vmem_limit_bytes=60 * MIB),
        cost_estimate=pl.CostEstimate(
            flops=4 * order * order * width, bytes_accessed=12 * order * width, transcendentals=0
        ),
    )(turn, *moments, right_root, left_root, *[x for x, _, _ in pieces])


def around(x, parts):
    return [
        lax.ppermute(x, "tensor", [(s, (s + d) % parts) for s in range(parts)]) for d in range(1, parts)
    ]


def all_sum(x, axis, size):
    stride = 1
    while stride < size:
        radix = min(4, size // stride)
        terms = [
            lax.ppermute(x, axis, [(s, s ^ (k * stride)) for s in range(size)]) for k in range(1, radix)
        ]
        x = sum(terms, x)
        stride *= radix
    return x


def after(x, *others):
    return lax.optimization_barrier((x, *others))[0]


def body(parts, grads, momentum, left_root, right_root, assign_list, owner_counts):
    cap, width, order = left_root.shape
    owners = owner_counts.shape[0]
    cells = float(order * order)
    turn = lax.axis_index("tensor").astype(jnp.int32).reshape(1)
    me = lax.axis_index("dp")

    def swap(x):
        return lax.all_to_all(x, "dp", split_axis=0, concat_axis=0, tiled=True)

    def solve(s, columns, others, lefts):
        direction, square = precondition(s, turn, [columns] + others, right_root, left_root, lefts)
        return direction.reshape(owners, order // owners, width), square[:, 0]

    unit = width // 4
    ahead = 9 * unit
    flat = left_root.reshape(cap * width, order)
    p0 = around(flat[:ahead], parts)
    moment_out, out0 = make_moment((0,), assign_list, owner_counts, grads, momentum)
    columns0 = swap(out0[0]).reshape(order, width)
    moment_out, rest = make_moment((1, 2), assign_list, owner_counts, grads, momentum, moment_out)
    m0 = around(columns0, parts)
    columns1 = swap(after(rest[0], columns0, *p0)).reshape(order, width)
    m1 = around(columns1, parts)
    columns2 = swap(after(rest[1], columns1, *m0)).reshape(order, width)
    d0, q0 = solve(0, columns0, m0, [[(p, width, 0)] for p in p0])
    m2 = around(columns2, parts)
    b0 = swap(after(d0, columns2, *m1))
    d1, q1 = solve(1, columns1, m1, [[(p, width, 1)] for p in p0])
    p1 = around(after(flat[ahead:], *m2), parts)
    b1 = swap(after(d1, b0, *m2))
    d2, q2 = solve(2, columns2, m2, [[(p, unit, 8), (q, 3 * unit, 0)] for p, q in zip(p0, p1)])
    b2 = swap(after(d2, b1))
    squares = jnp.stack([q0, q1, q2], axis=1)
    own = jnp.where(jnp.arange(owners)[None, None, :] == me, squares[:, :, None], 0.0)
    sums = all_sum(all_sum(own.reshape(2, -1), "tensor", parts), "dp", owners)
    scale = jnp.sqrt(sums[0] / (parts * cells) + EPS) / jnp.sqrt(sums[1] / cells + EPS)
    return (moment_out, finish(assign_list, owner_counts, scale, [b0, b1, b2]))


def solution(mesh):
    parts = mesh.shape["tensor"]
    in_specs = (
        P(None, "dp", "tensor"),
        P(None, "dp", "tensor"),
        P("dp", "tensor", None),
        P("dp", "tensor", None),
        P(),
        P(),
    )
    out_specs = (P(None, "dp", "tensor"), P(None, "dp", "tensor"))
    return jax.shard_map(
        functools.partial(body, parts), mesh=mesh, in_specs=in_specs, out_specs=out_specs, check_vma=False
    )
```

time: 467 us -> 227 us (0.49)
  blocking collectives: 168 us -> 0 us
  waiting for transfers between devices: 212 us -> 125 us
  starting transfers between devices: 8.39 us -> 53.5 us
  Pallas kernels: 0 us -> 33.2 us
  local copies, waits for them, and re-layouts: 32.6 us -> 9.7 us
  matrix products: 18.1 us -> 0 us
  between operations: 14.2 us -> 0.72 us
  other arithmetic: 12.8 us -> 1.34 us
    all_to_all x2 -> x0, blocking collectives: 124 us -> none  [the longest x1 76.1 us: body(): lax.all_to_all(outgoing, 'dp', split_axis=0, concat_axis=1, tiled=True)]
    all_gather x2 -> x0, waiting for transfers between devices: 121 us -> none  [the longest x1 80.3 us: body(): lax.all_gather(columns, 'tensor', axis=2, tiled=True)]
    ppermute x0 -> x12, waiting for transfers between devices: none -> 105 us  [the longest x5 89.2 us: around(): lax.ppermute(x, 'tensor', [(s, (s + d) % parts) for s in range(parts)])]
    all_to_all x1 -> x6, waiting for transfers between devices: 90.9 us -> 19.6 us  [swap(): return lax.all_to_all(x, 'dp', split_axis=0, concat_axis=0, tiled=True)]
    psum x2 -> x0, blocking collectives: 43.7 us -> none  [the longest x1 39.8 us: body(): block_squares = lax.psum(squares, ('dp', 'tensor'))]
    pallas_call x0 -> x6, Pallas kernels: none -> 33.2 us  [the longest x3 19.9 us: precondition(): pl.pallas_call(functools.partial(root_kernel, parts, len(lefts[0])), grid...]
    all_to_all x1 -> x6, starting transfers between devices: 8.31 us -> 39.5 us  [swap(): return lax.all_to_all(x, 'dp', split_axis=0, concat_axis=0, tiled=True)]
    dot_general x2 -> x0, matrix products: 18.1 us -> none  [the longest x1 9.27 us: body(): jnp.einsum('sij,sjk->sik', left_root, lax.all_gather(product_half, 'tenso...]
  transfers between devices with their start and end apart: 3 -> 18, of which waited for: 3 -> 14; matrix products, arithmetic and copies ran while one was open for 0% -> 3% of each run, Pallas kernels for 0% -> 13%
where the time goes in v2:
time: 227 us; the launch traced here: 223 us
  waiting for transfers between devices  125 us (55%)
  starting transfers between devices  53.5 us (24%)
  Pallas kernels  33.2 us (15%)
  local copies, waits for them, and re-layouts  9.7 us (4%)
    ppermute x5, waiting for transfers between devices, around(): lax.ppermute(x, 'tensor', [(s, (s + d) % parts) for s in range(parts)])  89.2 us
    all_to_all x6, starting transfers between devices, swap(): return lax.all_to_all(x, 'dp', split_axis=0, concat_axis=0, tiled=True)  39.5 us
    pallas_call x3, Pallas kernels, precondition(): pl.pallas_call(functools.partial(root_kernel, parts, len(lefts[0])), grid...  19.9 us
    all_to_all x6, waiting for transfers between devices, swap(): return lax.all_to_all(x, 'dp', split_axis=0, concat_axis=0, tiled=True)  19.6 us
    ppermute x7, waiting for transfers between devices, all_sum(): lax.ppermute(x, axis, [(s, s ^ k * stride) for s in range(size)])  16 us
    pallas_call x2, Pallas kernels, make_moment(): pl.pallas_call(functools.partial(moment_kernel, slots), grid_spec=pltpu.P...  8.73 us
    ppermute x7, starting transfers between devices, all_sum(): lax.ppermute(x, axis, [(s, s ^ k * stride) for s in range(size)])  7.69 us
    ppermute x5, starting transfers between devices, around(): lax.ppermute(x, 'tensor', [(s, (s + d) % parts) for s in range(parts)])  6.26 us
  transfers between devices with their start and end apart: 18, of which 14 were waited for; matrix products, arithmetic and copies ran while one was open for 3% of the time, Pallas kernels for 13%

profile of v2, /device:TPU:11, one launch (start us, length us, event | category | flops | bytes accessed | tf_op | source)
XLA Modules:
  0.0 223.2 jit_solution(4226832531610740915)
XLA Ops:
  0.6 3.3 %slice.36 = bf16[1152,1024]{1,0:T(8,128)(2,1)} slice(bf16[1536,1024]{1,0:T(8,128)(2,1)} %bitcast.18), slice={[0:1152], [0:1024]} | slice | bytes 4718592 | tf_op jit(solution)/shard_map/slice | solution.py:241
  3.9 1.2 collective-permute-start.1
  5.2 4.1 %shard_map.77 = (f32[32,64,512]{2,1,0:T(8,128)}, bf16[1,16,64,512]{3,2,1,0:T(8,128)(2,1)}) custom-call(s32[32]{0:T(128)} %assign_ref.5, s32[16]{0:T(128)} %count_ref.5, bf16[32,64,512]{2,1,0:T(8,128)(2,1)} %refs_0_.3, f32[32,64,512]{2,1,0:T(8,128)} %refs_1_.3), custom_call_target="tpu_custom_call" | custom-call | flops 1572864 | bytes 6291456 | tf_op jit(solution)/shard_map/pallas_call | solution.py:71
  9.2 6.8 %all-to-all-start = ((bf16[16,64,512]{2,1,0:T(8,128)(2,1)}), bf16[16,64,512]{2,1,0:T(8,128)(2,1)S(1)}, u32[]{:S(2)}, u32[]{:S(2)}) async-start(bf16[16,64,512]{2,1,0:T(8,128)(2,1)} %bitcast.27), calls=%async_computation | async-start | bytes 2097152 | tf_op jit(solution)/shard_map/all_to_all | solution.py:232
  16.1 4.7 %shard_map.78 = (f32[32,64,512]{2,1,0:T(8,128)}, bf16[2,16,64,512]{3,2,1,0:T(8,128)(2,1)}) custom-call(s32[32]{0:T(128)} %assign_ref.5, s32[16]{0:T(128)} %count_ref.5, bf16[32,64,512]{2,1,0:T(8,128)(2,1)} %refs_0_.3, f32[32,64,512]{2,1,0:T(8,128)} %refs_1_.3, f32[32,64,512]{2,1,0:T(8,128)} %get-tuple-element.18.refs_2_), custom_call_target="tpu_custom_call", output_to_operand_aliasing={{0}: (4, {})} | custom-call | flops 3145728 | bytes 12582912 | tf_op jit(solution)/shard_map/pallas_call | solution.py:71
  20.8 3.1 %slice_bitcast_fusion.1 = (bf16[16,64,512]{2,1,0:T(8,128)(2,1)}, bf16[16,64,512]{2,1,0:T(8,128)(2,1)}) fusion(bf16[2,16,64,512]{3,2,1,0:T(8,128)(2,1)} %get-tuple-element.22), kind=kLoop, calls=%fused_computation.1 | loop fusion | bytes 4194304 | tf_op jit(solution)/shard_map/squeeze | solution.py:246
  23.9 17.4 %all-to-all-done = bf16[16,64,512]{2,1,0:T(8,128)(2,1)S(1)} async-done(((bf16[16,64,512]{2,1,0:T(8,128)(2,1)}), bf16[16,64,512]{2,1,0:T(8,128)(2,1)S(1)}, u32[]{:S(2)}, u32[]{:S(2)}) %all-to-all-start) | async-done | bytes 1048608 | tf_op jit(solution)/shard_map/all_to_all | solution.py:232
  41.3 0.0 copy-start.5
  41.3 15.0 %collective-permute-done.1.refs_4_ = bf16[1152,1024]{1,0:T(8,128)(2,1)S(1)} collective-permute-done((bf16[1152,1024]{1,0:T(8,128)(2,1)}, bf16[1152,1024]{1,0:T(8,128)(2,1)S(1)}, u32[]{:S(2)}, u32[]{:S(2)}) %collective-permute-start.1) | collective-permute-done | bytes 2359328 | tf_op jit(solution)/shard_map/ppermute | solution.py:204
  56.2 0.0 copy-start
  56.3 7.4 %all-to-all-start.1 = ((bf16[16,64,512]{2,1,0:T(8,128)(2,1)}), bf16[16,64,512]{2,1,0:T(8,128)(2,1)}, u32[]{:S(2)}, u32[]{:S(2)}) async-start(bf16[16,64,512]{2,1,0:T(8,128)(2,1)} %get-tuple-element.23), calls=%async_computation.1 | async-start | bytes 2097152 | tf_op jit(solution)/shard_map/all_to_all | solution.py:232
  63.7 1.2 collective-permute-start
  64.9 23.2 %collective-permute-done.refs_1_ = bf16[1024,512]{1,0:T(8,128)(2,1)} collective-permute-done((bf16[1024,512]{1,0:T(8,128)(2,1)S(1)}, bf16[1024,512]{1,0:T(8,128)(2,1)}, u32[]{:S(2)}, u32[]{:S(2)}) %collective-permute-start) | collective-permute-done | bytes 1048608 | tf_op jit(solution)/shard_map/ppermute | solution.py:204
  88.2 0.8 all-to-all-done.1
  89.0 0.0 copy-done.5
  89.0 6.1 %all-to-all-start.2 = ((bf16[16,64,512]{2,1,0:T(8,128)(2,1)}), bf16[16,64,512]{2,1,0:T(8,128)(2,1)S(1)}, u32[]{:S(2)}, u32[]{:S(2)}) async-start(bf16[16,64,512]{2,1,0:T(8,128)(2,1)} %get-tuple-element.25), calls=%async_computation.2 | async-start | bytes 2097152 | tf_op jit(solution)/shard_map/all_to_all | solution.py:232
  95.0 1.2 collective-permute-start.2
  96.3 0.0 copy-done
  96.3 6.6 %shard_map.79 = (bf16[1024,512]{1,0:T(8,128)(2,1)}, f32[2,128]{1,0:T(2,128)}) custom-call(s32[1]{0:T(128)} %bitcast.turn_ref, bf16[1024,512]{1,0:T(8,128)(2,1)} %bitcast.23, bf16[1024,512]{1,0:T(8,128)(2,1)} %collective-permute-done.refs_1_, bf16[3,512,1024]{2,1,0:T(8,128)(2,1)} %refs_2_.5, bf16[3,512,1024]{2,1,0:T(8,128)(2,1)} %refs_3_.5, ...), custom_call_target="tpu_custom_call" | custom-call | flops 2147483648 | bytes 6291456 | tf_op jit(solution)/shard_map/pallas_call | solution.py:180
  102.9 16.8 %collective-permute-done.2.refs_1_ = bf16[1024,512]{1,0:T(8,128)(2,1)} collective-permute-done((bf16[1024,512]{1,0:T(8,128)(2,1)}, bf16[1024,512]{1,0:T(8,128)(2,1)}, u32[]{:S(2)}, u32[]{:S(2)}) %collective-permute-start.2) | collective-permute-done | bytes 1048608 | tf_op jit(solution)/shard_map/ppermute | solution.py:204
  119.7 0.6 all-to-all-done.2
  120.3 6.3 %all-to-all-start.3 = ((bf16[16,64,512]{2,1,0:T(8,128)(2,1)}), bf16[16,64,512]{2,1,0:T(8,128)(2,1)S(1)}, u32[]{:S(2)}, u32[]{:S(2)}) async-start(bf16[16,64,512]{2,1,0:T(8,128)(2,1)} %bitcast.26), calls=%async_computation.3 | async-start | bytes 2097152 | tf_op jit(solution)/shard_map/all_to_all | solution.py:232
  126.6 1.2 collective-permute-start.3
  127.8 6.6 %shard_map.80 = (bf16[1024,512]{1,0:T(8,128)(2,1)}, f32[2,128]{1,0:T(2,128)}) custom-call(s32[1]{0:T(128)} %bitcast.turn_ref, bf16[1024,512]{1,0:T(8,128)(2,1)} %bitcast.5.refs_0_, bf16[1024,512]{1,0:T(8,128)(2,1)} %collective-permute-done.2.refs_1_, bf16[3,512,1024]{2,1,0:T(8,128)(2,1)} %refs_2_.5, bf16[3,512,1024]{2,1,0:T(8,128)(2,1)} %refs_3_.5, ...), custom_call_target="tpu_custom_call" | custom-call | flops 2147483648 | bytes 6291456 | tf_op jit(solution)/shard_map/pallas_call | solution.py:180
  134.4 0.0 copy-done.1
  134.5 16.6 %collective-permute-done.3.refs_1_ = bf16[1024,512]{1,0:T(8,128)(2,1)} collective-permute-done((bf16[1024,512]{1,0:T(8,128)(2,1)S(1)}, bf16[1024,512]{1,0:T(8,128)(2,1)}, u32[]{:S(2)}, u32[]{:S(2)}) %collective-permute-start.3) | collective-permute-done | bytes 1048608 | tf_op jit(solution)/shard_map/ppermute | solution.py:204
  151.1 0.8 all-to-all-done.3.refs_0_
  151.9 6.1 %all-to-all-start.4 = ((bf16[16,64,512]{2,1,0:T(8,128)(2,1)}), bf16[16,64,512]{2,1,0:T(8,128)(2,1)S(1)}, u32[]{:S(2)}, u32[]{:S(2)}) async-start(bf16[16,64,512]{2,1,0:T(8,128)(2,1)} %bitcast.25), calls=%async_computation.4 | async-start | bytes 2097152 | tf_op jit(solution)/shard_map/all_to_all | solution.py:232
  157.9 1.2 slice.37
  159.1 0.0 copy-start.7
  159.1 0.0 copy-start.8
  159.1 1.3 collective-permute-start.4
  160.4 17.5 %collective-permute-done.4.refs_5_ = bf16[384,1024]{1,0:T(8,128)(2,1)S(1)} collective-permute-done((bf16[384,1024]{1,0:T(8,128)(2,1)S(1)}, bf16[384,1024]{1,0:T(8,128)(2,1)S(1)}, u32[]{:S(2)}, u32[]{:S(2)}) %collective-permute-start.4) | collective-permute-done | bytes 786464 | tf_op jit(solution)/shard_map/ppermute | solution.py:204
  178.0 0.9 copy-done.6
  178.8 6.7 %shard_map.81 = (bf16[1024,512]{1,0:T(8,128)(2,1)}, f32[2,128]{1,0:T(2,128)}) custom-call(s32[1]{0:T(128)} %bitcast.turn_ref, bf16[1024,512]{1,0:T(8,128)(2,1)} %bitcast.21, bf16[1024,512]{1,0:T(8,128)(2,1)} %collective-permute-done.3.refs_1_, bf16[3,512,1024]{2,1,0:T(8,128)(2,1)} %refs_2_.5, bf16[3,512,1024]{2,1,0:T(8,128)(2,1)} %refs_3_.5, ...), custom_call_target="tpu_custom_call" | custom-call | flops 2147483648 | bytes 6291456 | tf_op jit(solution)/shard_map/pallas_call | solution.py:180
  185.5 0.0 copy-done.2
  185.5 0.0 all-to-all-done.4.refs_1_
  185.5 0.0 copy-start.3
  185.5 6.9 %all-to-all-start.5 = ((bf16[16,64,512]{2,1,0:T(8,128)(2,1)}), bf16[16,64,512]{2,1,0:T(8,128)(2,1)S(1)}, u32[]{:S(2)}, u32[]{:S(2)}) async-start(bf16[16,64,512]{2,1,0:T(8,128)(2,1)} %bitcast.24), calls=%async_computation.5 | async-start | bytes 2097152 | tf_op jit(solution)/shard_map/all_to_all | solution.py:232
  192.4 0.1 broadcast_in_dim.29
  192.5 0.0 copy-done.7
  192.5 0.0 copy-done.8
  192.5 0.8 pad_maximum_fusion
  193.2 0.1 broadcast_in_dim.31
  193.3 0.1 broadcast_in_dim.32
  193.4 1.2 collective-permute-start.5
  194.6 1.5 collective-permute-done.5
  196.1 1.2 collective-permute-start.6
  197.3 0.3 collective-permute-start.7
  197.6 1.4 collective-permute-start.8
  199.0 0.0 collective-permute-done.6
  199.0 1.0 collective-permute-done.7
  200.1 1.0 collective-permute-done.8
  201.0 2.0 collective-permute-start.10
  203.0 0.0 collective-permute-start.11
  203.0 1.6 collective-permute-start.9
  204.6 10.7 %collective-permute-done.10 = f32[2,48]{1,0:T(2,128)S(1)} collective-permute-done((f32[2,48]{1,0:T(2,128)S(1)}, f32[2,48]{1,0:T(2,128)S(1)}, u32[]{:S(2)}, u32[]{:S(2)}) %collective-permute-start.10) | collective-permute-done | bytes 416 | tf_op jit(solution)/shard_map/ppermute | solution.py:213
  215.3 1.8 collective-permute-done.11
  217.1 0.0 collective-permute-done.9
  217.1 0.5 multiply_bitcast_fusion.scale_ref
  217.7 0.0 all-to-all-done.5.refs_2_
  217.7 0.0 copy-done.3
  217.7 1.0 copy-done.4
  218.6 4.6 %shard_map.82 = bf16[32,64,512]{2,1,0:T(8,128)(2,1)} custom-call(s32[32]{0:T(128)} %assign_ref.5, s32[16]{0:T(128)} %count_ref.5, f32[48]{0:T(128)} %multiply_bitcast_fusion.scale_ref, bf16[16,64,512]{2,1,0:T(8,128)(2,1)} %copy-done.2, bf16[16,64,512]{2,1,0:T(8,128)(2,1)} %copy-done.3, bf16[16,64,512]{2,1,0:T(8,128)(2,1)} %copy-done.4), custom_call_target="tpu_custom_call" | custom-call | tf_op jit(solution)/shard_map/pallas_call | solution.py:114
  (10 shorter events, 0.0 us)
Async XLA Ops:
  3.9 52.3 %collective-permute-start.1 = (bf16[1152,1024]{1,0:T(8,128)(2,1)}, bf16[1152,1024]{1,0:T(8,128)(2,1)S(1)}, u32[]{:S(2)}, u32[]{:S(2)}) collective-permute-start(bf16[1152,1024]{1,0:T(8,128)(2,1)} %slice.36), channel_id=1, source_target_pairs={{0,1},{1,0},{2,3},{3,2},{4,5},{5,4},{6,7},{7,6},{8,9},{9,8},{10,11... | collective-permute-start | bytes 7077896 | tf_op jit(solution)/shard_map/ppermute | solution.py:204
  9.2 32.0 %all-to-all-start = ((bf16[16,64,512]{2,1,0:T(8,128)(2,1)}), bf16[16,64,512]{2,1,0:T(8,128)(2,1)S(1)}, u32[]{:S(2)}, u32[]{:S(2)}) async-start(bf16[16,64,512]{2,1,0:T(8,128)(2,1)} %bitcast.27), calls=%async_computation | async-start | bytes 2097152 | tf_op jit(solution)/shard_map/all_to_all | solution.py:232
  41.3 47.7 %copy-start.5 = (bf16[16,64,512]{2,1,0:T(8,128)(2,1)}, bf16[16,64,512]{2,1,0:T(8,128)(2,1)S(1)}, u32[]{:S(2)}) copy-start(bf16[16,64,512]{2,1,0:T(8,128)(2,1)S(1)} %all-to-all-done) | copy-start | bytes 3145732
  56.2 40.0 %copy-start = (bf16[1152,1024]{1,0:T(8,128)(2,1)}, bf16[1152,1024]{1,0:T(8,128)(2,1)S(1)}, u32[]{:S(2)}) copy-start(bf16[1152,1024]{1,0:T(8,128)(2,1)S(1)} %collective-permute-done.1.refs_4_) | copy-start | bytes 7077892
  56.3 32.7 %all-to-all-start.1 = ((bf16[16,64,512]{2,1,0:T(8,128)(2,1)}), bf16[16,64,512]{2,1,0:T(8,128)(2,1)}, u32[]{:S(2)}, u32[]{:S(2)}) async-start(bf16[16,64,512]{2,1,0:T(8,128)(2,1)} %get-tuple-element.23), calls=%async_computation.1 | async-start | bytes 2097152 | tf_op jit(solution)/shard_map/all_to_all | solution.py:232
  63.7 24.5 %collective-permute-start = (bf16[1024,512]{1,0:T(8,128)(2,1)S(1)}, bf16[1024,512]{1,0:T(8,128)(2,1)}, u32[]{:S(2)}, u32[]{:S(2)}) collective-permute-start(bf16[1024,512]{1,0:T(8,128)(2,1)S(1)} %bitcast.22), channel_id=1, source_target_pairs={{0,1},{1,0},{2,3},{3,2},{4,5},{5,4},{6,7},{7,6},{8,9},{9,8},{10,11... | collective-permute-start | bytes 3145736 | tf_op jit(solution)/shard_map/ppermute | solution.py:204
  89.0 31.3 %all-to-all-start.2 = ((bf16[16,64,512]{2,1,0:T(8,128)(2,1)}), bf16[16,64,512]{2,1,0:T(8,128)(2,1)S(1)}, u32[]{:S(2)}, u32[]{:S(2)}) async-start(bf16[16,64,512]{2,1,0:T(8,128)(2,1)} %get-tuple-element.25), calls=%async_computation.2 | async-start | bytes 2097152 | tf_op jit(solution)/shard_map/all_to_all | solution.py:232
  95.0 24.7 %collective-permute-start.2 = (bf16[1024,512]{1,0:T(8,128)(2,1)}, bf16[1024,512]{1,0:T(8,128)(2,1)}, u32[]{:S(2)}, u32[]{:S(2)}) collective-permute-start(bf16[1024,512]{1,0:T(8,128)(2,1)} %bitcast.5.refs_0_), channel_id=1, source_target_pairs={{0,1},{1,0},{2,3},{3,2},{4,5},{5,4},{6,7},{7,6},{8,9},{9,8},{10,11... | collective-permute-start | bytes 3145736 | tf_op jit(solution)/shard_map/ppermute | solution.py:204
  120.3 14.2 %copy-start.1 = (bf16[16,64,512]{2,1,0:T(8,128)(2,1)}, bf16[16,64,512]{2,1,0:T(8,128)(2,1)S(1)}, u32[]{:S(2)}) copy-start(bf16[16,64,512]{2,1,0:T(8,128)(2,1)S(1)} %all-to-all-done.2) | copy-start | bytes 3145732
  120.3 31.6 %all-to-all-start.3 = ((bf16[16,64,512]{2,1,0:T(8,128)(2,1)}), bf16[16,64,512]{2,1,0:T(8,128)(2,1)S(1)}, u32[]{:S(2)}, u32[]{:S(2)}) async-start(bf16[16,64,512]{2,1,0:T(8,128)(2,1)} %bitcast.26), calls=%async_computation.3 | async-start | bytes 2097152 | tf_op jit(solution)/shard_map/all_to_all | solution.py:232
  126.6 24.5 %collective-permute-start.3 = (bf16[1024,512]{1,0:T(8,128)(2,1)S(1)}, bf16[1024,512]{1,0:T(8,128)(2,1)}, u32[]{:S(2)}, u32[]{:S(2)}) collective-permute-start(bf16[1024,512]{1,0:T(8,128)(2,1)S(1)} %bitcast.20), channel_id=1, source_target_pairs={{0,1},{1,0},{2,3},{3,2},{4,5},{5,4},{6,7},{7,6},{8,9},{9,8},{10,11... | collective-permute-start | bytes 3145736 | tf_op jit(solution)/shard_map/ppermute | solution.py:204
  151.9 33.6 %copy-start.2 = (bf16[16,64,512]{2,1,0:T(8,128)(2,1)}, bf16[16,64,512]{2,1,0:T(8,128)(2,1)S(1)}, u32[]{:S(2)}) copy-start(bf16[16,64,512]{2,1,0:T(8,128)(2,1)S(1)} %all-to-all-done.3.refs_0_) | copy-start | bytes 3145732
  151.9 33.6 %all-to-all-start.4 = ((bf16[16,64,512]{2,1,0:T(8,128)(2,1)}), bf16[16,64,512]{2,1,0:T(8,128)(2,1)S(1)}, u32[]{:S(2)}, u32[]{:S(2)}) async-start(bf16[16,64,512]{2,1,0:T(8,128)(2,1)} %bitcast.25), calls=%async_computation.4 | async-start | bytes 2097152 | tf_op jit(solution)/shard_map/all_to_all | solution.py:232
  159.1 33.4 %copy-start.7 = (f32[2,128]{1,0:T(2,128)S(1)}, f32[2,128]{1,0:T(2,128)}, u32[]{:S(2)}) copy-start(f32[2,128]{1,0:T(2,128)} %get-tuple-element.21) | copy-start | bytes 3076
  159.1 33.4 %copy-start.8 = (f32[2,128]{1,0:T(2,128)S(1)}, f32[2,128]{1,0:T(2,128)}, u32[]{:S(2)}) copy-start(f32[2,128]{1,0:T(2,128)} %get-tuple-element.24) | copy-start | bytes 3076
  159.1 18.8 %collective-permute-start.4 = (bf16[384,1024]{1,0:T(8,128)(2,1)S(1)}, bf16[384,1024]{1,0:T(8,128)(2,1)S(1)}, u32[]{:S(2)}, u32[]{:S(2)}) collective-permute-start(bf16[384,1024]{1,0:T(8,128)(2,1)S(1)} %slice.37), channel_id=1, source_target_pairs={{0,1},{1,0},{2,3},{3,2},{4,5},{5,4},{6,7},{7,6},{8,9},{9,8},{10,11... | collective-permute-start | bytes 2359304 | tf_op jit(solution)/shard_map/ppermute | solution.py:204
  178.0 0.9 copy-start.6
  185.5 32.2 %copy-start.3 = (bf16[16,64,512]{2,1,0:T(8,128)(2,1)}, bf16[16,64,512]{2,1,0:T(8,128)(2,1)S(1)}, u32[]{:S(2)}) copy-start(bf16[16,64,512]{2,1,0:T(8,128)(2,1)S(1)} %all-to-all-done.4.refs_1_) | copy-start | bytes 3145732
  185.5 32.2 %all-to-all-start.5 = ((bf16[16,64,512]{2,1,0:T(8,128)(2,1)}), bf16[16,64,512]{2,1,0:T(8,128)(2,1)S(1)}, u32[]{:S(2)}, u32[]{:S(2)}) async-start(bf16[16,64,512]{2,1,0:T(8,128)(2,1)} %bitcast.24), calls=%async_computation.5 | async-start | bytes 2097152 | tf_op jit(solution)/shard_map/all_to_all | solution.py:232
  193.4 2.7 %collective-permute-start.5 = (f32[2,48]{1,0:T(2,128)S(1)}, f32[2,48]{1,0:T(2,128)S(1)}, u32[]{:S(2)}, u32[]{:S(2)}) collective-permute-start(f32[2,48]{1,0:T(2,128)S(1)} %broadcast_select_fusion), channel_id=1, source_target_pairs={{0,1},{1,0},{2,3},{3,2},{4,5},{5,4},{6,7},{7,6},{8,9},{9,8},{10,11... | collective-permute-start | bytes 1160 | tf_op jit(solution)/shard_map/ppermute | solution.py:213
  196.1 2.9 %collective-permute-start.6 = (f32[2,48]{1,0:T(2,128)S(1)}, f32[2,48]{1,0:T(2,128)S(1)}, u32[]{:S(2)}, u32[]{:S(2)}) collective-permute-start(f32[2,48]{1,0:T(2,128)S(1)} %fusion), channel_id=1, source_target_pairs={{0,2},{2,0},{4,6},{6,4},{8,10},{10,8},{12,14},{14,12},{16,18},{18,... | collective-permute-start | bytes 1160 | tf_op jit(solution)/shard_map/ppermute | solution.py:213
  197.3 2.7 %collective-permute-start.7 = (f32[2,48]{1,0:T(2,128)S(1)}, f32[2,48]{1,0:T(2,128)S(1)}, u32[]{:S(2)}, u32[]{:S(2)}) collective-permute-start(f32[2,48]{1,0:T(2,128)S(1)} %fusion), channel_id=1, source_target_pairs={{0,4},{2,6},{4,0},{6,2},{8,12},{10,14},{12,8},{14,10},{16,20},{18,... | collective-permute-start | bytes 1160 | tf_op jit(solution)/shard_map/ppermute | solution.py:213
  197.6 3.4 %collective-permute-start.8 = (f32[2,48]{1,0:T(2,128)S(1)}, f32[2,48]{1,0:T(2,128)S(1)}, u32[]{:S(2)}, u32[]{:S(2)}) collective-permute-start(f32[2,48]{1,0:T(2,128)S(1)} %fusion), channel_id=1, source_target_pairs={{0,6},{2,4},{4,2},{6,0},{8,14},{10,12},{12,10},{14,8},{16,22},{18,... | collective-permute-start | bytes 1160 | tf_op jit(solution)/shard_map/ppermute | solution.py:213
  201.0 14.2 %collective-permute-start.10 = (f32[2,48]{1,0:T(2,128)S(1)}, f32[2,48]{1,0:T(2,128)S(1)}, u32[]{:S(2)}, u32[]{:S(2)}) collective-permute-start(f32[2,48]{1,0:T(2,128)S(1)} %add_add_fusion.1), channel_id=1, source_target_pairs={{0,16},{2,18},{4,20},{6,22},{8,24},{10,26},{12,28},{14,30},{16,0},... | collective-permute-start | bytes 1160 | tf_op jit(solution)/shard_map/ppermute | solution.py:213
  203.0 14.1 %collective-permute-start.11 = (f32[2,48]{1,0:T(2,128)S(1)}, f32[2,48]{1,0:T(2,128)S(1)}, u32[]{:S(2)}, u32[]{:S(2)}) collective-permute-start(f32[2,48]{1,0:T(2,128)S(1)} %add_add_fusion.1), channel_id=1, source_target_pairs={{0,24},{2,26},{4,28},{6,30},{8,16},{10,18},{12,20},{14,22},{16,8},... | collective-permute-start | bytes 1160 | tf_op jit(solution)/shard_map/ppermute | solution.py:213
  203.0 14.1 %collective-permute-start.9 = (f32[2,48]{1,0:T(2,128)S(1)}, f32[2,48]{1,0:T(2,128)S(1)}, u32[]{:S(2)}, u32[]{:S(2)}) collective-permute-start(f32[2,48]{1,0:T(2,128)S(1)} %add_add_fusion.1), channel_id=1, source_target_pairs={{0,8},{2,10},{4,12},{6,14},{8,0},{10,2},{12,4},{14,6},{16,24},{18,... | collective-permute-start | bytes 1160 | tf_op jit(solution)/shard_map/ppermute | solution.py:213
  217.7 1.0 copy-start.4

commit v3 on v2

--- a/solution.py
+++ b/solution.py
@@ -29,7 +29,8 @@
 
 def moment_kernel(slots, assign_ref, count_ref, *refs):
     grads, momentum = refs[:2]
-    moment_out, outgoing, grad, old, new, half, in_sem, out_sem = refs[-8:]
+    moment_out, outgoing = refs[-7 - len(slots)], refs[-6 - len(slots) : -6]
+    grad, old, new, half, in_sem, out_sem = refs[-6:]
 
     def reads(i, b):
         return (
@@ -39,7 +40,7 @@
 
     def writes(i, b, k, o):
         return (
-            pltpu.make_async_copy(half.at[i], outgoing.at[k, o], out_sem.at[0, i]),
+            pltpu.make_async_copy(half.at[i], outgoing[k].at[o], out_sem.at[0, i]),
             pltpu.make_async_copy(new.at[i], moment_out.at[b], out_sem.at[1, i]),
         )
 
@@ -74,7 +75,7 @@
             num_scalar_prefetch=2,
             grid=(1,),
             in_specs=[ANY] * (2 + len(earlier)),
-            out_specs=[ANY, ANY],
+            out_specs=[ANY] * (1 + len(slots)),
             scratch_shapes=[
                 pltpu.VMEM((n, rows, columns), jnp.bfloat16),
                 pltpu.VMEM((n, rows, columns), jnp.float32),
@@ -86,47 +87,49 @@
         ),
         out_shape=[
             jax.ShapeDtypeStruct((blocks, rows, columns), jnp.float32),
-            jax.ShapeDtypeStruct((len(slots), owners, rows, columns), jnp.bfloat16),
+            *[jax.ShapeDtypeStruct((owners, rows, columns), jnp.bfloat16)] * len(slots),
         ],
         input_output_aliases={4: 0} if earlier else {},
         compiler_params=pltpu.CompilerParams(vmem_limit_bytes=60 * MIB),
         cost_estimate=pl.CostEstimate(
-            flops=3 * n * rows * columns, bytes_accessed=12 * n * rows * columns, transcendentals=0
+            flops=300 * n * rows * columns, bytes_accessed=1200 * n * rows * columns, transcendentals=0
         ),
     )(assign_list, owner_counts, grads, momentum, *earlier)
 
 
-def finish_kernel(assign_ref, count_ref, scale_ref, *refs):
-    arrived, update = refs[:-1], refs[-1]
-    owners = count_ref.shape[0]
-
-    def one(i, b, k, o):
-        value = arrived[k][o].astype(jnp.float32) * scale_ref[k * owners + o]
-        update[b] = value.astype(jnp.bfloat16)
-
-    for_slots(range(len(arrived)), assign_ref, count_ref, one)
-
-
-def finish(assign_list, owner_counts, scale, arrived):
+def place_kernel(slots, assign_ref, count_ref, *refs):
+    arrived, update, sem = refs[: len(slots)], refs[-2], refs[-1]
+
+    def copy(i, b, k, o):
+        return pltpu.make_async_copy(arrived[k].at[o], update.at[b], sem.at[i])
+
+    for_slots(slots, assign_ref, count_ref, lambda *at: copy(*at).start())
+    for_slots(slots, assign_ref, count_ref, lambda *at: copy(*at).wait())
+
+
+def place(slots, assign_list, owner_counts, arrived, *earlier):
     owners, rows, columns = arrived[0].shape
-    blocks = assign_list.shape[0]
-    full = pl.BlockSpec((owners, rows, columns), lambda i, *_: (0, 0, 0))
-    return pl.pallas_call(
-        finish_kernel,
+    return pl.pallas_call(
+        functools.partial(place_kernel, slots),
         grid_spec=pltpu.PrefetchScalarGridSpec(
-            num_scalar_prefetch=3,
+            num_scalar_prefetch=2,
             grid=(1,),
-            in_specs=[full] * len(arrived),
-            out_specs=pl.BlockSpec((blocks, rows, columns), lambda i, *_: (0, 0, 0)),
-        ),
-        out_shape=jax.ShapeDtypeStruct((blocks, rows, columns), jnp.bfloat16),
-        compiler_params=pltpu.CompilerParams(vmem_limit_bytes=60 * MIB),
-    )(assign_list, owner_counts, scale, *arrived)
+            in_specs=[pl.BlockSpec(memory_space=pltpu.VMEM)] * len(arrived) + [ANY] * len(earlier),
+            out_specs=ANY,
+            scratch_shapes=[pltpu.SemaphoreType.DMA((len(slots) * owners,))],
+        ),
+        out_shape=jax.ShapeDtypeStruct((assign_list.shape[0], rows, columns), jnp.bfloat16),
+        input_output_aliases={2 + len(arrived): 0} if earlier else {},
+        compiler_params=pltpu.CompilerParams(vmem_limit_bytes=8 * MIB),
+        cost_estimate=pl.CostEstimate(
+            flops=0, bytes_accessed=4 * len(slots) * owners * rows * columns, transcendentals=0
+        ),
+    )(assign_list, owner_counts, *arrived, *earlier)
 
 
 def root_kernel(parts, count, turn_ref, *refs):
-    moments, right, own_left, lefts = refs[:parts], refs[parts], refs[parts + 1], refs[parts + 2 : -3]
-    out_ref, square_ref, product = refs[-3:]
+    moments, right, own_left, lefts = refs[:parts], refs[parts], refs[parts + 1], refs[parts + 2 : -4]
+    out_ref, moment_square, square, product = refs[-4:]
     order, width = moments[0].shape
     step = min(256, order)
     turn = turn_ref[0]
@@ -165,10 +168,10 @@
         small = 256 if height % 256 == 0 else height
         for i in range(height // small):
             direction = jnp.dot(left[i * small : (i + 1) * small, :], product[...], preferred_element_type=jnp.float32)
-            out_ref[pl.ds(pl.multiple_of(base + i * small, 16), small), :] = direction.astype(jnp.bfloat16)
+            out_ref[pl.ds(pl.multiple_of(base + i * small, 16), small), :] = direction
             squares = squares + jnp.sum(direction * direction, axis=0, keepdims=True)
-    for r, lines in enumerate((moment_squares, squares)):
-        square_ref[r : r + 1, :] = jnp.broadcast_to(jnp.sum(lines, axis=1, keepdims=True), (1, 128))
+    for ref, lines in ((moment_square, moment_squares), (square, squares)):
+        ref[...] = jnp.broadcast_to(jnp.sum(lines, axis=1, keepdims=True), (1, 128))
 
 
 def precondition(slot, turn, moments, right_root, left_root, lefts):
@@ -185,18 +188,38 @@
             in_specs=[whole] * parts
             + [picked, picked]
             + [pl.BlockSpec((rows, order), lambda i, t, at=at: (at, 0)) for _, rows, at in pieces],
-            out_specs=[whole, pl.BlockSpec((2, 128), lambda i, t: (0, 0))],
+            out_specs=[whole] + [pl.BlockSpec((1, 128), lambda i, t: (0, 0))] * 2,
             scratch_shapes=[pltpu.VMEM((order, width), jnp.bfloat16)],
         ),
         out_shape=[
-            jax.ShapeDtypeStruct((order, width), jnp.bfloat16),
-            jax.ShapeDtypeStruct((2, 128), jnp.float32),
+            jax.ShapeDtypeStruct((order, width), jnp.float32),
+            jax.ShapeDtypeStruct((1, 128), jnp.float32),
+            jax.ShapeDtypeStruct((1, 128), jnp.float32),
         ],
         compiler_params=pltpu.CompilerParams(vmem_limit_bytes=60 * MIB),
         cost_estimate=pl.CostEstimate(
-            flops=4 * order * order * width, bytes_accessed=12 * order * width, transcendentals=0
+            flops=400 * order * order * width, bytes_accessed=1200 * order * width, transcendentals=0
         ),
     )(turn, *moments, right_root, left_root, *[x for x, _, _ in pieces])
+
+
+def scale_kernel(cells, direction, moment_square, *refs):
+    squares, out_ref = refs[:-1], refs[-1]
+    total = sum([ref[0:1, 0:1] for ref in squares])
+    scale = jnp.sqrt(moment_square[0:1, 0:1] / cells + EPS) / jnp.sqrt(total / cells + EPS)
+    out_ref[...] = (direction[...] * scale).astype(jnp.bfloat16)
+
+
+def rescale(direction, moment_square, squares):
+    order, width = direction.shape
+    return pl.pallas_call(
+        functools.partial(scale_kernel, float(order * order)),
+        out_shape=jax.ShapeDtypeStruct((order, width), jnp.bfloat16),
+        compiler_params=pltpu.CompilerParams(vmem_limit_bytes=60 * MIB),
+        cost_estimate=pl.CostEstimate(
+            flops=order * width, bytes_accessed=6 * order * width, transcendentals=0
+        ),
+    )(direction, moment_square, *squares)
 
 
 def around(x, parts):
@@ -205,60 +228,79 @@
     ]
 
 
-def all_sum(x, axis, size):
-    stride = 1
-    while stride < size:
-        radix = min(4, size // stride)
-        terms = [
-            lax.ppermute(x, axis, [(s, s ^ (k * stride)) for s in range(size)]) for k in range(1, radix)
-        ]
-        x = sum(terms, x)
-        stride *= radix
-    return x
-
-
 def after(x, *others):
     return lax.optimization_barrier((x, *others))[0]
+
+
+def gate(x, *others):
+    return pl.pallas_call(
+        lambda *refs: None,
+        in_specs=[ANY] * (1 + len(others)),
+        out_specs=ANY,
+        out_shape=jax.ShapeDtypeStruct(x.shape, x.dtype),
+        input_output_aliases={0: 0},
+        compiler_params=pltpu.CompilerParams(vmem_limit_bytes=60 * MIB),
+        cost_estimate=pl.CostEstimate(flops=1 << 37, bytes_accessed=1 << 28, transcendentals=0),
+    )(x, *others)
 
 
 def body(parts, grads, momentum, left_root, right_root, assign_list, owner_counts):
     cap, width, order = left_root.shape
     owners = owner_counts.shape[0]
-    cells = float(order * order)
     turn = lax.axis_index("tensor").astype(jnp.int32).reshape(1)
-    me = lax.axis_index("dp")
 
     def swap(x):
         return lax.all_to_all(x, "dp", split_axis=0, concat_axis=0, tiled=True)
 
     def solve(s, columns, others, lefts):
-        direction, square = precondition(s, turn, [columns] + others, right_root, left_root, lefts)
-        return direction.reshape(owners, order // owners, width), square[:, 0]
+        direction, wanted, square = precondition(
+            s, turn, [columns] + others, right_root, left_root, lefts
+        )
+        squares = [square] + around(square, parts)
+        scaled = rescale(direction, wanted, squares)
+        return scaled.reshape(owners, order // owners, width), squares[-1]
 
     unit = width // 4
-    ahead = 9 * unit
     flat = left_root.reshape(cap * width, order)
-    p0 = around(flat[:ahead], parts)
+    sent = []
+
+    def send(first, end, *others):
+        rows = flat[first * unit : end * unit]
+        sent.append((first, end, around(after(rows, *others) if others else rows, parts)))
+        return sent[-1][2]
+
+    def lefts(s):
+        pieces = [[] for _ in range(parts - 1)]
+        for first, end, got in sent:
+            low, high = max(first, 4 * s), min(end, 4 * s + 4)
+            if low < high:
+                for d, x in enumerate(got):
+                    pieces[d].append((x, (high - low) * unit, (low - first) // (high - low)))
+        return pieces
+
+    p0 = send(0, 8)
     moment_out, out0 = make_moment((0,), assign_list, owner_counts, grads, momentum)
-    columns0 = swap(out0[0]).reshape(order, width)
-    moment_out, rest = make_moment((1, 2), assign_list, owner_counts, grads, momentum, moment_out)
+    columns0 = swap(out0).reshape(order, width)
+    moment_out, out1, out2 = make_moment((1, 2), assign_list, owner_counts, grads, momentum, moment_out)
     m0 = around(columns0, parts)
-    columns1 = swap(after(rest[0], columns0, *p0)).reshape(order, width)
+    e1 = send(8, 9, columns0)
+    columns1 = swap(gate(out1, columns0, *p0)).reshape(order, width)
+    out2 = gate(out2, columns0)
     m1 = around(columns1, parts)
-    columns2 = swap(after(rest[1], columns1, *m0)).reshape(order, width)
-    d0, q0 = solve(0, columns0, m0, [[(p, width, 0)] for p in p0])
+    e2 = []
+    columns2 = swap(gate(out2, columns1, *m0, *e1)).reshape(order, width)
+    d0, q0 = solve(0, columns0, m0, lefts(0))
     m2 = around(columns2, parts)
-    b0 = swap(after(d0, columns2, *m1))
-    d1, q1 = solve(1, columns1, m1, [[(p, width, 1)] for p in p0])
-    p1 = around(after(flat[ahead:], *m2), parts)
-    b1 = swap(after(d1, b0, *m2))
-    d2, q2 = solve(2, columns2, m2, [[(p, unit, 8), (q, 3 * unit, 0)] for p, q in zip(p0, p1)])
+    e3 = []
+    b0 = swap(gate(d0, columns2, *m1, *e2))
+    d1, q1 = solve(1, columns1, m1, lefts(1))
+    e4 = send(9, 12, q1)
+    b1 = swap(gate(d1, b0, *m2))
+    d2, q2 = solve(2, columns2, m2, lefts(2))
     b2 = swap(after(d2, b1))
-    squares = jnp.stack([q0, q1, q2], axis=1)
-    own = jnp.where(jnp.arange(owners)[None, None, :] == me, squares[:, :, None], 0.0)
-    sums = all_sum(all_sum(own.reshape(2, -1), "tensor", parts), "dp", owners)
-    scale = jnp.sqrt(sums[0] / (parts * cells) + EPS) / jnp.sqrt(sums[1] / cells + EPS)
-    return (moment_out, finish(assign_list, owner_counts, scale, [b0, b1, b2]))
+    update = place((0, 1), assign_list, owner_counts, [b0, b1])
+    update = place((2,), assign_list, owner_counts, [b2], update)
+    return (moment_out, update)
 
 
 def solution(mesh):

time: 227 us -> 207 us (0.912); the launches traced: 223 us -> 206 us
  starting transfers between devices: 53.5 us -> 41.5 us
  waiting for transfers between devices: 125 us -> 113 us
  Pallas kernels: 33.2 us -> 43.5 us
  local copies, waits for them, and re-layouts: 9.7 us -> 6.98 us
    all_to_all x6, waiting for transfers between devices: 19.6 us -> 73.5 us  [swap(): return lax.all_to_all(x, 'dp', split_axis=0, concat_axis=0, tiled=True)]
    ppermute x5 -> x9, waiting for transfers between devices: 89.2 us -> 39.5 us  [around(): lax.ppermute(x, 'tensor', [(s, (s + d) % parts) for s in range(parts)])]
    ppermute x7 -> x0, waiting for transfers between devices: 16 us -> none  [all_sum(): lax.ppermute(x, axis, [(s, s ^ k * stride) for s in range(size)])]
    pallas_call x1 -> x10, Pallas kernels: 4.59 us -> 13.8 us  [the longest x3 8.77 us: rescale(): pl.pallas_call(functools.partial(scale_kernel, float(order * order)), out...]
    ppermute x7 -> x0, starting transfers between devices: 7.69 us -> none  [all_sum(): lax.ppermute(x, axis, [(s, s ^ k * stride) for s in range(size)])]
    all_to_all x6, starting transfers between devices: 39.5 us -> 35.5 us  [swap(): return lax.all_to_all(x, 'dp', split_axis=0, concat_axis=0, tiled=True)]
    squeeze x1 -> x0, local copies, waits for them, and re-layouts: 3.1 us -> none  [body(): columns1 = swap(after(rest[0], columns0, *p0)).reshape(order, width)]
    ppermute x5 -> x9, starting transfers between devices: 6.26 us -> 5.99 us  [around(): lax.ppermute(x, 'tensor', [(s, (s + d) % parts) for s in range(parts)])]
  transfers between devices with their start and end apart: 18 -> 15, of which waited for: 14 -> 11; matrix products, arithmetic and copies ran while one was open for 3% -> 1% of each run, Pallas kernels for 13% -> 20%
where the time goes in v3:
time: 207 us; the launch traced here: 206 us
  waiting for transfers between devices  113 us (55%)
  Pallas kernels  43.5 us (21%)
  starting transfers between devices  41.5 us (20%)
  local copies, waits for them, and re-layouts  6.98 us (3%)
    all_to_all x6, waiting for transfers between devices, swap(): return lax.all_to_all(x, 'dp', split_axis=0, concat_axis=0, tiled=True)  73.5 us
    ppermute x9, waiting for transfers between devices, around(): lax.ppermute(x, 'tensor', [(s, (s + d) % parts) for s in range(parts)])  39.5 us
    all_to_all x6, starting transfers between devices, swap(): return lax.all_to_all(x, 'dp', split_axis=0, concat_axis=0, tiled=True)  35.5 us
    pallas_call x3, Pallas kernels, precondition(): pl.pallas_call(functools.partial(root_kernel, parts, len(lefts[0])), grid...  20.9 us
    pallas_call x3, Pallas kernels, rescale(): pl.pallas_call(functools.partial(scale_kernel, float(order * order)), out...  8.77 us
    pallas_call x2, Pallas kernels, make_moment(): pl.pallas_call(functools.partial(moment_kernel, slots), grid_spec=pltpu.P...  8.73 us
    ppermute x9, starting transfers between devices, around(): lax.ppermute(x, 'tensor', [(s, (s + d) % parts) for s in range(parts)])  5.99 us
    pallas_call x2, Pallas kernels, place(): pl.pallas_call(functools.partial(place_kernel, slots), grid_spec=pltpu.Pr...  5.06 us
  transfers between devices with their start and end apart: 15, of which 11 were waited for; matrix products, arithmetic and copies ran while one was open for 1% of the time, Pallas kernels for 20%

profile of v3, /device:TPU:11, one launch (start us, length us, event | category | flops | bytes accessed | tf_op | source)
XLA Modules:
  0.0 205.7 jit_solution(8962369751933712913)
XLA Ops:
  0.6 1.8 slice.12
  2.4 1.3 collective-permute-start
  3.7 4.1 %shard_map.77 = (f32[32,64,512]{2,1,0:T(8,128)}, bf16[16,64,512]{2,1,0:T(8,128)(2,1)}) custom-call(s32[32]{0:T(128)} %assign_ref.7, s32[16]{0:T(128)} %count_ref.7, bf16[32,64,512]{2,1,0:T(8,128)(2,1)} %refs_0_.3, f32[32,64,512]{2,1,0:T(8,128)} %refs_1_.3), custom_call_target="tpu_custom_call" | custom-call | flops 157286400 | bytes 629145600 | tf_op jit(solution)/shard_map/pallas_call | solution.py:72
  7.8 6.8 %all-to-all-start = ((bf16[16,64,512]{2,1,0:T(8,128)(2,1)}), bf16[16,64,512]{2,1,0:T(8,128)(2,1)}, u32[]{:S(2)}, u32[]{:S(2)}) async-start(bf16[16,64,512]{2,1,0:T(8,128)(2,1)} %get-tuple-element.22), calls=%async_computation | async-start | bytes 2097152 | tf_op jit(solution)/shard_map/all_to_all | solution.py:253
  14.6 1.7 slice.16
  16.3 4.7 %shard_map.78 = (f32[32,64,512]{2,1,0:T(8,128)}, bf16[16,64,512]{2,1,0:T(8,128)(2,1)}, bf16[16,64,512]{2,1,0:T(8,128)(2,1)}) custom-call(s32[32]{0:T(128)} %assign_ref.7, s32[16]{0:T(128)} %count_ref.7, bf16[32,64,512]{2,1,0:T(8,128)(2,1)} %refs_0_.3, f32[32,64,512]{2,1,0:T(8,128)} %refs_1_.3, ...), custom_call_target="tpu_custom_call", output_to_operand_aliasing={{0}: (4, {})} | custom-call | flops 314572800 | bytes 1258291200 | tf_op jit(solution)/shard_map/pallas_call | solution.py:72
  21.0 18.9 %all-to-all-done = bf16[16,64,512]{2,1,0:T(8,128)(2,1)} async-done(((bf16[16,64,512]{2,1,0:T(8,128)(2,1)}), bf16[16,64,512]{2,1,0:T(8,128)(2,1)}, u32[]{:S(2)}, u32[]{:S(2)}) %all-to-all-start) | async-done | bytes 1048608 | tf_op jit(solution)/shard_map/all_to_all | solution.py:253
  39.9 0.2 collective-permute-start.1
  40.1 1.2 collective-permute-start.2
  41.4 7.7 %collective-permute-done.refs_2_.refs_4_ = bf16[1024,1024]{1,0:T(8,128)(2,1)} collective-permute-done((bf16[1024,1024]{1,0:T(8,128)(2,1)S(1)}, bf16[1024,1024]{1,0:T(8,128)(2,1)}, u32[]{:S(2)}, u32[]{:S(2)}) %collective-permute-start) | collective-permute-done | bytes 2097184 | tf_op jit(solution)/shard_map/ppermute | solution.py:227
  49.1 8.6 %all-to-all-start.1 = ((bf16[16,64,512]{2,1,0:T(8,128)(2,1)}), bf16[16,64,512]{2,1,0:T(8,128)(2,1)}, u32[]{:S(2)}, u32[]{:S(2)}) async-start(bf16[16,64,512]{2,1,0:T(8,128)(2,1)} %shard_map.80), calls=%async_computation.1 | async-start | bytes 2097152 | tf_op jit(solution)/shard_map/all_to_all | solution.py:253
  57.6 25.0 %all-to-all-done.1 = bf16[16,64,512]{2,1,0:T(8,128)(2,1)} async-done(((bf16[16,64,512]{2,1,0:T(8,128)(2,1)}), bf16[16,64,512]{2,1,0:T(8,128)(2,1)}, u32[]{:S(2)}, u32[]{:S(2)}) %all-to-all-start.1) | async-done | bytes 1048608 | tf_op jit(solution)/shard_map/all_to_all | solution.py:253
  82.6 1.2 collective-permute-start.4
  83.9 0.0 collective-permute-done.2.refs_3_.refs_4_
  83.9 0.0 collective-permute-done.1.refs_2_.refs_1_
  83.9 5.2 %all-to-all-start.2 = ((bf16[16,64,512]{2,1,0:T(8,128)(2,1)}), bf16[16,64,512]{2,1,0:T(8,128)(2,1)}, u32[]{:S(2)}, u32[]{:S(2)}) async-start(bf16[16,64,512]{2,1,0:T(8,128)(2,1)} %shard_map.81), calls=%async_computation.2 | async-start | bytes 2097152 | tf_op jit(solution)/shard_map/all_to_all | solution.py:253
  89.1 7.0 %shard_map.86 = (f32[1024,512]{1,0:T(8,128)}, f32[1,128]{1,0:T(1,128)}, f32[1,128]{1,0:T(1,128)}) custom-call(s32[1]{0:T(128)} %bitcast.turn_ref, bf16[1024,512]{1,0:T(8,128)(2,1)} %bitcast.1.refs_1_.refs_0_, bf16[1024,512]{1,0:T(8,128)(2,1)} %collective-permute-done.1.refs_2_.refs_1_, bf16[3,512,1024]{2,1,0:T(8,128)(2,1)} %refs_2_.5, ...), custom_call_target="tpu_custom_call" | custom-call | flops 214748364800 | bytes 629145600 | tf_op jit(solution)/shard_map/pallas_call | solution.py:183
  96.1 0.2 collective-permute-start.8
  96.3 11.2 %collective-permute-done.8.refs_1_ = f32[1,128]{1,0:T(1,128)S(1)} collective-permute-done((f32[1,128]{1,0:T(1,128)}, f32[1,128]{1,0:T(1,128)S(1)}, u32[]{:S(2)}, u32[]{:S(2)}) %collective-permute-start.8) | collective-permute-done | bytes 544 | tf_op jit(solution)/shard_map/ppermute | solution.py:227
  107.5 0.0 copy-start.3
  107.5 0.5 copy-done.3
  108.0 2.9 %shard_map.87 = bf16[1024,512]{1,0:T(8,128)(2,1)} custom-call(f32[1024,512]{1,0:T(8,128)} %get-tuple-element.32.direction, f32[1,128]{1,0:T(1,128)} %get-tuple-element.33.moment_square, f32[1,128]{1,0:T(1,128)} %get-tuple-element.34.refs_0_, f32[1,128]{1,0:T(1,128)} %copy-done.3), custom_call_target="tpu_custom_call" | custom-call | flops 524288 | bytes 3145728 | tf_op jit(solution)/shard_map/pallas_call | solution.py:215
  111.0 3.1 %all-to-all-done.2 = bf16[16,64,512]{2,1,0:T(8,128)(2,1)} async-done(((bf16[16,64,512]{2,1,0:T(8,128)(2,1)}), bf16[16,64,512]{2,1,0:T(8,128)(2,1)}, u32[]{:S(2)}, u32[]{:S(2)}) %all-to-all-start.2) | async-done | bytes 1048608 | tf_op jit(solution)/shard_map/all_to_all | solution.py:253
  114.1 0.2 collective-permute-start.3
  114.3 0.0 collective-permute-done.4.refs_1_.refs_2_
  114.3 5.2 %all-to-all-start.3 = ((bf16[16,64,512]{2,1,0:T(8,128)(2,1)}), bf16[16,64,512]{2,1,0:T(8,128)(2,1)}, u32[]{:S(2)}, u32[]{:S(2)}) async-start(bf16[16,64,512]{2,1,0:T(8,128)(2,1)} %shard_map.88), calls=%async_computation.3 | async-start | bytes 2097152 | tf_op jit(solution)/shard_map/all_to_all | solution.py:253
  119.5 7.0 %shard_map.82 = (f32[1024,512]{1,0:T(8,128)}, f32[1,128]{1,0:T(1,128)}, f32[1,128]{1,0:T(1,128)}) custom-call(s32[1]{0:T(128)} %bitcast.turn_ref, bf16[1024,512]{1,0:T(8,128)(2,1)} %bitcast.3.refs_1_.refs_0_, bf16[1024,512]{1,0:T(8,128)(2,1)} %collective-permute-done.4.refs_1_.refs_2_, bf16[3,512,1024]{2,1,0:T(8,128)(2,1)} %refs_2_.5, ...), custom_call_target="tpu_custom_call" | custom-call | flops 214748364800 | bytes 629145600 | tf_op jit(solution)/shard_map/pallas_call | solution.py:183
  126.5 1.2 collective-permute-start.5
  127.7 1.2 slice.17
  128.9 10.0 %collective-permute-done.5.refs_1_ = f32[1,128]{1,0:T(1,128)S(1)} collective-permute-done((f32[1,128]{1,0:T(1,128)}, f32[1,128]{1,0:T(1,128)S(1)}, u32[]{:S(2)}, u32[]{:S(2)}) %collective-permute-start.5) | collective-permute-done | bytes 544 | tf_op jit(solution)/shard_map/ppermute | solution.py:227
  138.9 0.0 copy-start.2
  138.9 0.2 collective-permute-start.6
  139.2 0.3 copy-done.2
  139.5 2.9 %shard_map.85 = bf16[1024,512]{1,0:T(8,128)(2,1)} custom-call(f32[1024,512]{1,0:T(8,128)} %get-tuple-element.30.direction, f32[1,128]{1,0:T(1,128)} %get-tuple-element.31.moment_square, f32[1,128]{1,0:T(1,128)} %get-tuple-element.25.refs_0_, f32[1,128]{1,0:T(1,128)} %copy-done.2), custom_call_target="tpu_custom_call" | custom-call | flops 524288 | bytes 3145728 | tf_op jit(solution)/shard_map/pallas_call | solution.py:215
  142.4 0.0 collective-permute-done.3.refs_1_.refs_2_
  142.4 2.3 %all-to-all-done.3.refs_1_.refs_0_ = bf16[16,64,512]{2,1,0:T(8,128)(2,1)} async-done(((bf16[16,64,512]{2,1,0:T(8,128)(2,1)}), bf16[16,64,512]{2,1,0:T(8,128)(2,1)}, u32[]{:S(2)}, u32[]{:S(2)}) %all-to-all-start.3) | async-done | bytes 1048608 | tf_op jit(solution)/shard_map/all_to_all | solution.py:253
  144.7 4.7 %all-to-all-start.4 = ((bf16[16,64,512]{2,1,0:T(8,128)(2,1)}), bf16[16,64,512]{2,1,0:T(8,128)(2,1)}, u32[]{:S(2)}, u32[]{:S(2)}) async-start(bf16[16,64,512]{2,1,0:T(8,128)(2,1)} %shard_map.89), calls=%async_computation.4 | async-start | bytes 2097152 | tf_op jit(solution)/shard_map/all_to_all | solution.py:253
  149.4 7.6 %collective-permute-done.6.refs_5_ = bf16[384,1024]{1,0:T(8,128)(2,1)S(1)} collective-permute-done((bf16[384,1024]{1,0:T(8,128)(2,1)S(1)}, bf16[384,1024]{1,0:T(8,128)(2,1)S(1)}, u32[]{:S(2)}, u32[]{:S(2)}) %collective-permute-start.6) | collective-permute-done | bytes 786464 | tf_op jit(solution)/shard_map/ppermute | solution.py:227
  157.1 0.0 copy-start.5
  157.1 0.9 copy-done.5
  157.9 7.0 %shard_map.83 = (f32[1024,512]{1,0:T(8,128)}, f32[1,128]{1,0:T(1,128)}, f32[1,128]{1,0:T(1,128)}) custom-call(s32[1]{0:T(128)} %bitcast.turn_ref, bf16[1024,512]{1,0:T(8,128)(2,1)} %bitcast.5.refs_0_.refs_1_, bf16[1024,512]{1,0:T(8,128)(2,1)} %collective-permute-done.3.refs_1_.refs_2_, bf16[3,512,1024]{2,1,0:T(8,128)(2,1)} %refs_2_.5, ...), custom_call_target="tpu_custom_call" | custom-call | flops 214748364800 | bytes 629145600 | tf_op jit(solution)/shard_map/pallas_call | solution.py:183
  164.9 0.1 collective-permute-start.7
  165.0 2.9 %collective-permute-done.7.refs_1_ = f32[1,128]{1,0:T(1,128)S(1)} collective-permute-done((f32[1,128]{1,0:T(1,128)}, f32[1,128]{1,0:T(1,128)S(1)}, u32[]{:S(2)}, u32[]{:S(2)}) %collective-permute-start.7) | collective-permute-done | bytes 544 | tf_op jit(solution)/shard_map/ppermute | solution.py:227
  167.9 0.0 copy-start.4
  167.9 0.6 copy-done.4
  168.5 0.0 copy-start
  168.5 0.0 copy-start.1
  168.5 2.9 %shard_map.84 = bf16[1024,512]{1,0:T(8,128)(2,1)} custom-call(f32[1024,512]{1,0:T(8,128)} %get-tuple-element.27.direction, f32[1,128]{1,0:T(1,128)} %get-tuple-element.28.moment_square, f32[1,128]{1,0:T(1,128)} %get-tuple-element.29.refs_0_, f32[1,128]{1,0:T(1,128)} %copy-done.4), custom_call_target="tpu_custom_call" | custom-call | flops 524288 | bytes 3145728 | tf_op jit(solution)/shard_map/pallas_call | solution.py:215
  171.4 3.0 %all-to-all-done.4.refs_1_ = bf16[16,64,512]{2,1,0:T(8,128)(2,1)} async-done(((bf16[16,64,512]{2,1,0:T(8,128)(2,1)}), bf16[16,64,512]{2,1,0:T(8,128)(2,1)}, u32[]{:S(2)}, u32[]{:S(2)}) %all-to-all-start.4) | async-done | bytes 1048608 | tf_op jit(solution)/shard_map/all_to_all | solution.py:253
  174.4 4.9 %all-to-all-start.5 = ((bf16[16,64,512]{2,1,0:T(8,128)(2,1)}), bf16[16,64,512]{2,1,0:T(8,128)(2,1)S(1)}, u32[]{:S(2)}, u32[]{:S(2)}) async-start(bf16[16,64,512]{2,1,0:T(8,128)(2,1)} %bitcast.10), calls=%async_computation.5 | async-start | bytes 2097152 | tf_op jit(solution)/shard_map/all_to_all | solution.py:253
  179.4 0.0 copy-done
  179.4 0.0 copy-done.1
  179.4 3.6 %shard_map.90.refs_1_ = bf16[32,64,512]{2,1,0:T(8,128)(2,1)} custom-call(s32[32]{0:T(128)S(1)} %copy-done, s32[16]{0:T(128)S(1)} %copy-done.1, bf16[16,64,512]{2,1,0:T(8,128)(2,1)} %all-to-all-done.3.refs_1_.refs_0_, bf16[16,64,512]{2,1,0:T(8,128)(2,1)} %all-to-all-done.4.refs_1_), custom_call_target="tpu_custom_call" | custom-call | bytes 4194304 | tf_op jit(solution)/shard_map/pallas_call | solution.py:112
  183.0 21.3 %all-to-all-done.5.refs_0_ = bf16[16,64,512]{2,1,0:T(8,128)(2,1)S(1)} async-done(((bf16[16,64,512]{2,1,0:T(8,128)(2,1)}), bf16[16,64,512]{2,1,0:T(8,128)(2,1)S(1)}, u32[]{:S(2)}, u32[]{:S(2)}) %all-to-all-start.5) | async-done | bytes 1048608 | tf_op jit(solution)/shard_map/all_to_all | solution.py:253
  204.2 1.5 shard_map.91
  (5 shorter events, 0.0 us)
Async XLA Ops:
  2.4 46.7 %collective-permute-start = (bf16[1024,1024]{1,0:T(8,128)(2,1)S(1)}, bf16[1024,1024]{1,0:T(8,128)(2,1)}, u32[]{:S(2)}, u32[]{:S(2)}) collective-permute-start(bf16[1024,1024]{1,0:T(8,128)(2,1)S(1)} %bitcast.14), channel_id=1, source_target_pairs={{0,1},{1,0},{2,3},{3,2},{4,5},{5,4},{6,7},{7,6},{8,9},{9,8},{10,11... | collective-permute-start | bytes 6291464 | tf_op jit(solution)/shard_map/ppermute | solution.py:227
  7.8 32.1 %all-to-all-start = ((bf16[16,64,512]{2,1,0:T(8,128)(2,1)}), bf16[16,64,512]{2,1,0:T(8,128)(2,1)}, u32[]{:S(2)}, u32[]{:S(2)}) async-start(bf16[16,64,512]{2,1,0:T(8,128)(2,1)} %get-tuple-element.22), calls=%async_computation | async-start | bytes 2097152 | tf_op jit(solution)/shard_map/all_to_all | solution.py:253
  39.9 44.0 %collective-permute-start.1 = (bf16[1024,512]{1,0:T(8,128)(2,1)}, bf16[1024,512]{1,0:T(8,128)(2,1)}, u32[]{:S(2)}, u32[]{:S(2)}) collective-permute-start(bf16[1024,512]{1,0:T(8,128)(2,1)} %bitcast.1.refs_1_.refs_0_), channel_id=1, source_target_pairs={{0,1},{1,0},{2,3},{3,2},{4,5},{5,4},{6,7},{7,6},{8,9},{9,8},{10,11... | collective-permute-start | bytes 3145736 | tf_op jit(solution)/shard_map/ppermute | solution.py:227
  40.1 43.7 %collective-permute-start.2 = (bf16[128,1024]{1,0:T(8,128)(2,1)}, bf16[128,1024]{1,0:T(8,128)(2,1)}, u32[]{:S(2)}, u32[]{:S(2)}) collective-permute-start(bf16[128,1024]{1,0:T(8,128)(2,1)} %slice.16), channel_id=1, source_target_pairs={{0,1},{1,0},{2,3},{3,2},{4,5},{5,4},{6,7},{7,6},{8,9},{9,8},{10,11... | collective-permute-start | bytes 786440 | tf_op jit(solution)/shard_map/ppermute | solution.py:227
  49.1 33.6 %all-to-all-start.1 = ((bf16[16,64,512]{2,1,0:T(8,128)(2,1)}), bf16[16,64,512]{2,1,0:T(8,128)(2,1)}, u32[]{:S(2)}, u32[]{:S(2)}) async-start(bf16[16,64,512]{2,1,0:T(8,128)(2,1)} %shard_map.80), calls=%async_computation.1 | async-start | bytes 2097152 | tf_op jit(solution)/shard_map/all_to_all | solution.py:253
  82.6 31.7 %collective-permute-start.4 = (bf16[1024,512]{1,0:T(8,128)(2,1)}, bf16[1024,512]{1,0:T(8,128)(2,1)}, u32[]{:S(2)}, u32[]{:S(2)}) collective-permute-start(bf16[1024,512]{1,0:T(8,128)(2,1)} %bitcast.3.refs_1_.refs_0_), channel_id=1, source_target_pairs={{0,1},{1,0},{2,3},{3,2},{4,5},{5,4},{6,7},{7,6},{8,9},{9,8},{10,11... | collective-permute-start | bytes 3145736 | tf_op jit(solution)/shard_map/ppermute | solution.py:227
  83.9 30.2 %all-to-all-start.2 = ((bf16[16,64,512]{2,1,0:T(8,128)(2,1)}), bf16[16,64,512]{2,1,0:T(8,128)(2,1)}, u32[]{:S(2)}, u32[]{:S(2)}) async-start(bf16[16,64,512]{2,1,0:T(8,128)(2,1)} %shard_map.81), calls=%async_computation.2 | async-start | bytes 2097152 | tf_op jit(solution)/shard_map/all_to_all | solution.py:253
  96.1 11.4 %collective-permute-start.8 = (f32[1,128]{1,0:T(1,128)}, f32[1,128]{1,0:T(1,128)S(1)}, u32[]{:S(2)}, u32[]{:S(2)}) collective-permute-start(f32[1,128]{1,0:T(1,128)} %get-tuple-element.34.refs_0_), channel_id=1, source_target_pairs={{0,1},{1,0},{2,3},{3,2},{4,5},{5,4},{6,7},{7,6},{8,9},{9,8},{10,11... | collective-permute-start | bytes 1544 | tf_op jit(solution)/shard_map/ppermute | solution.py:227
  107.5 0.5 copy-start.3
  114.1 28.3 %collective-permute-start.3 = (bf16[1024,512]{1,0:T(8,128)(2,1)}, bf16[1024,512]{1,0:T(8,128)(2,1)}, u32[]{:S(2)}, u32[]{:S(2)}) collective-permute-start(bf16[1024,512]{1,0:T(8,128)(2,1)} %bitcast.5.refs_0_.refs_1_), channel_id=1, source_target_pairs={{0,1},{1,0},{2,3},{3,2},{4,5},{5,4},{6,7},{7,6},{8,9},{9,8},{10,11... | collective-permute-start | bytes 3145736 | tf_op jit(solution)/shard_map/ppermute | solution.py:227
  114.3 30.4 %all-to-all-start.3 = ((bf16[16,64,512]{2,1,0:T(8,128)(2,1)}), bf16[16,64,512]{2,1,0:T(8,128)(2,1)}, u32[]{:S(2)}, u32[]{:S(2)}) async-start(bf16[16,64,512]{2,1,0:T(8,128)(2,1)} %shard_map.88), calls=%async_computation.3 | async-start | bytes 2097152 | tf_op jit(solution)/shard_map/all_to_all | solution.py:253
  126.5 12.4 %collective-permute-start.5 = (f32[1,128]{1,0:T(1,128)}, f32[1,128]{1,0:T(1,128)S(1)}, u32[]{:S(2)}, u32[]{:S(2)}) collective-permute-start(f32[1,128]{1,0:T(1,128)} %get-tuple-element.25.refs_0_), channel_id=1, source_target_pairs={{0,1},{1,0},{2,3},{3,2},{4,5},{5,4},{6,7},{7,6},{8,9},{9,8},{10,11... | collective-permute-start | bytes 1544 | tf_op jit(solution)/shard_map/ppermute | solution.py:227
  138.9 0.5 copy-start.2
  138.9 18.1 %collective-permute-start.6 = (bf16[384,1024]{1,0:T(8,128)(2,1)S(1)}, bf16[384,1024]{1,0:T(8,128)(2,1)S(1)}, u32[]{:S(2)}, u32[]{:S(2)}) collective-permute-start(bf16[384,1024]{1,0:T(8,128)(2,1)S(1)} %slice.17), channel_id=1, source_target_pairs={{0,1},{1,0},{2,3},{3,2},{4,5},{5,4},{6,7},{7,6},{8,9},{9,8},{10,11... | collective-permute-start | bytes 2359304 | tf_op jit(solution)/shard_map/ppermute | solution.py:227
  144.7 29.7 %all-to-all-start.4 = ((bf16[16,64,512]{2,1,0:T(8,128)(2,1)}), bf16[16,64,512]{2,1,0:T(8,128)(2,1)}, u32[]{:S(2)}, u32[]{:S(2)}) async-start(bf16[16,64,512]{2,1,0:T(8,128)(2,1)} %shard_map.89), calls=%async_computation.4 | async-start | bytes 2097152 | tf_op jit(solution)/shard_map/all_to_all | solution.py:253
  157.1 0.9 copy-start.5
  164.9 3.0 %collective-permute-start.7 = (f32[1,128]{1,0:T(1,128)}, f32[1,128]{1,0:T(1,128)S(1)}, u32[]{:S(2)}, u32[]{:S(2)}) collective-permute-start(f32[1,128]{1,0:T(1,128)} %get-tuple-element.29.refs_0_), channel_id=1, source_target_pairs={{0,1},{1,0},{2,3},{3,2},{4,5},{5,4},{6,7},{7,6},{8,9},{9,8},{10,11... | collective-permute-start | bytes 1544 | tf_op jit(solution)/shard_map/ppermute | solution.py:227
  167.9 0.6 copy-start.4
  168.5 10.9 %copy-start = (s32[32]{0:T(128)S(1)}, s32[32]{0:T(128)}, u32[]{:S(2)}) copy-start(s32[32]{0:T(128)} %assign_ref.7) | copy-start | bytes 388
  168.5 10.9 %copy-start.1 = (s32[16]{0:T(128)S(1)}, s32[16]{0:T(128)}, u32[]{:S(2)}) copy-start(s32[16]{0:T(128)} %count_ref.7) | copy-start | bytes 196
  174.4 29.8 %all-to-all-start.5 = ((bf16[16,64,512]{2,1,0:T(8,128)(2,1)}), bf16[16,64,512]{2,1,0:T(8,128)(2,1)S(1)}, u32[]{:S(2)}, u32[]{:S(2)}) async-start(bf16[16,64,512]{2,1,0:T(8,128)(2,1)} %bitcast.10), calls=%async_computation.5 | async-start | bytes 2097152 | tf_op jit(solution)/shard_map/all_to_all | solution.py:253

commit v4 on v3

--- a/solution.py
+++ b/solution.py
@@ -203,6 +203,112 @@
     )(turn, *moments, right_root, left_root, *[x for x, _, _ in pieces])
 
 
+def product_kernel(parts, rows, turn_ref, *refs):
+    split = len(rows)
+    moments, right, product, square = refs[:-3], refs[-3], refs[-2], refs[-1]
+    owners, _, width = product.shape
+    turn = turn_ref[0]
+    squares = jnp.zeros((1, width), jnp.float32)
+    row = 0
+    for r, height in enumerate(rows):
+        group = min(owners, max(1, 256 // height))
+
+        def some_owners(i, squares, r=r, height=height, row=row, group=group):
+            some = pl.ds(i * group, group)
+            total = None
+            for d in range(parts):
+                moment = moments[d * split + r][some].reshape(group * height, width)
+                at = pl.multiple_of(lax.rem(turn - d + parts, parts) * width, width)
+                term = lax.dot_general(
+                    moment,
+                    right[0, :, pl.ds(at, width)],
+                    (((1,), (1,)), ((), ())),
+                    preferred_element_type=jnp.float32,
+                )
+                total = term if total is None else total + term
+                wide = moment.astype(jnp.float32)
+                squares = squares + jnp.sum(wide * wide, axis=0, keepdims=True)
+            half = total.astype(jnp.bfloat16).reshape(group, height, width)
+            product[some, row : row + height, :] = half
+            return squares
+
+        squares = lax.fori_loop(0, owners // group, some_owners, squares)
+        row += height
+    square[...] = jnp.broadcast_to(jnp.sum(squares, axis=1, keepdims=True), (1, 128))
+
+
+def make_product(slot, turn, moments, right_root):
+    parts = len(moments)
+    owners = moments[0][0][0].shape[0]
+    _, width, order = right_root.shape
+    rows = tuple(piece[1] for piece in moments[0])
+    shares = [piece for one in moments for piece in one]
+    shape = (owners, order // owners, width)
+    return pl.pallas_call(
+        functools.partial(product_kernel, parts, rows),
+        grid_spec=pltpu.PrefetchScalarGridSpec(
+            num_scalar_prefetch=1,
+            grid=(1,),
+            in_specs=[pl.BlockSpec((owners, n, width), lambda i, t, at=at: (0, at, 0)) for _, n, at in shares]
+            + [pl.BlockSpec((1, width, order), lambda i, t: (slot, 0, 0))],
+            out_specs=[pl.BlockSpec(shape, lambda i, t: (0, 0, 0)), pl.BlockSpec((1, 128), lambda i, t: (0, 0))],
+        ),
+        out_shape=[jax.ShapeDtypeStruct(shape, jnp.bfloat16), jax.ShapeDtypeStruct((1, 128), jnp.float32)],
+        compiler_params=pltpu.CompilerParams(vmem_limit_bytes=60 * MIB),
+        cost_estimate=pl.CostEstimate(
+            flops=400 * order * order * width, bytes_accessed=1200 * order * width, transcendentals=0
+        ),
+    )(turn, *[x for x, _, _ in shares], right_root)
+
+
+def direction_kernel(parts, count, turn_ref, product, own_left, *refs):
+    lefts, out_ref, square = refs[:-2], refs[-2], refs[-1]
+    order, width = product.shape
+    turn = turn_ref[0]
+
+    def position(d):
+        return pl.multiple_of(lax.rem(turn - d + parts, parts) * width, width)
+
+    squares = jnp.zeros((1, width), jnp.float32)
+    pieces = [(own_left.at[0], position(0))]
+    for d in range(1, parts):
+        base = position(d)
+        for ref in lefts[(d - 1) * count : d * count]:
+            pieces.append((ref, base))
+            base = base + ref.shape[0]
+    for left, base in pieces:
+        height = left.shape[0]
+        small = 256 if height % 256 == 0 else height
+        for i in range(height // small):
+            direction = jnp.dot(
+                left[i * small : (i + 1) * small, :], product[...], preferred_element_type=jnp.float32
+            )
+            out_ref[pl.ds(pl.multiple_of(base + i * small, 16), small), :] = direction
+            squares = squares + jnp.sum(direction * direction, axis=0, keepdims=True)
+    square[...] = jnp.broadcast_to(jnp.sum(squares, axis=1, keepdims=True), (1, 128))
+
+
+def make_direction(slot, turn, product, left_root, lefts):
+    _, width, order = left_root.shape
+    pieces = [piece for one in lefts for piece in one]
+    whole = pl.BlockSpec((order, width), lambda i, t: (0, 0))
+    return pl.pallas_call(
+        functools.partial(direction_kernel, len(lefts) + 1, len(lefts[0])),
+        grid_spec=pltpu.PrefetchScalarGridSpec(
+            num_scalar_prefetch=1,
+            grid=(1,),
+            in_specs=[whole, pl.BlockSpec((1, width, order), lambda i, t: (slot, 0, 0))]
+            + [pl.BlockSpec((n, order), lambda i, t, at=at: (at, 0)) for _, n, at in pieces],
+            out_specs=[whole, pl.BlockSpec((1, 128), lambda i, t: (0, 0))],
+        ),
+        out_shape=[jax.ShapeDtypeStruct((order, width), jnp.float32), jax.ShapeDtypeStruct((1, 128), jnp.float32)],
+        compiler_params=pltpu.CompilerParams(vmem_limit_bytes=60 * MIB),
+        cost_estimate=pl.CostEstimate(
+            flops=2 * order * order * width, bytes_accessed=6 * order * width, transcendentals=0
+        ),
+    )(turn, product.reshape(order, width), left_root, *[x for x, _, _ in pieces])
+
+
 def scale_kernel(cells, direction, moment_square, *refs):
     squares, out_ref = refs[:-1], refs[-1]
     total = sum([ref[0:1, 0:1] for ref in squares])
@@ -252,10 +358,16 @@
     def swap(x):
         return lax.all_to_all(x, "dp", split_axis=0, concat_axis=0, tiled=True)
 
-    def solve(s, columns, others, lefts):
-        direction, wanted, square = precondition(
-            s, turn, [columns] + others, right_root, left_root, lefts
-        )
+    def solve(s, columns, others, lefts, apart=False):
+        if apart:
+            shape = (owners, order // owners, width)
+            moments = [[(x.reshape(shape), shape[1], 0)] for x in [columns] + others]
+            product, wanted = make_product(s, turn, moments, right_root)
+            direction, square = make_direction(s, turn, product, left_root, lefts)
+        else:
+            direction, wanted, square = precondition(
+                s, turn, [columns] + others, right_root, left_root, lefts
+            )
         squares = [square] + around(square, parts)
         scaled = rescale(direction, wanted, squares)
         return scaled.reshape(owners, order // owners, width), squares[-1]
@@ -278,25 +390,26 @@
                     pieces[d].append((x, (high - low) * unit, (low - first) // (high - low)))
         return pieces
 
-    p0 = send(0, 8)
+    p0 = send(0, 6)
     moment_out, out0 = make_moment((0,), assign_list, owner_counts, grads, momentum)
     columns0 = swap(out0).reshape(order, width)
     moment_out, out1, out2 = make_moment((1, 2), assign_list, owner_counts, grads, momentum, moment_out)
+    out1 = gate(out1, *p0)
     m0 = around(columns0, parts)
-    e1 = send(8, 9, columns0)
-    columns1 = swap(gate(out1, columns0, *p0)).reshape(order, width)
-    out2 = gate(out2, columns0)
+    e1 = send(6, 7, columns0)
+    columns1 = swap(gate(out1, columns0)).reshape(order, width)
+    out2 = gate(out2, *m0, *e1)
     m1 = around(columns1, parts)
-    e2 = []
-    columns2 = swap(gate(out2, columns1, *m0, *e1)).reshape(order, width)
+    columns2 = swap(gate(out2, columns1)).reshape(order, width)
     d0, q0 = solve(0, columns0, m0, lefts(0))
+    e2 = send(7, 8, q0)
     m2 = around(columns2, parts)
     e3 = []
     b0 = swap(gate(d0, columns2, *m1, *e2))
     d1, q1 = solve(1, columns1, m1, lefts(1))
-    e4 = send(9, 12, q1)
+    e4 = send(8, 12, q1)
     b1 = swap(gate(d1, b0, *m2))
-    d2, q2 = solve(2, columns2, m2, lefts(2))
+    d2, q2 = solve(2, columns2, m2, lefts(2), apart=True)
     b2 = swap(after(d2, b1))
     update = place((0, 1), assign_list, owner_counts, [b0, b1])
     update = place((2,), assign_list, owner_counts, [b2], update)

time: 207 us -> 198 us (0.957)
  waiting for transfers between devices: 113 us -> 101 us
  Pallas kernels: 43.5 us -> 45.7 us
    all_to_all x6, waiting for transfers between devices: 73.5 us -> 33.5 us  [swap(): return lax.all_to_all(x, 'dp', split_axis=0, concat_axis=0, tiled=True)]
    ppermute x9 -> x10, waiting for transfers between devices: 39.5 us -> 67.3 us  [around(): lax.ppermute(x, 'tensor', [(s, (s + d) % parts) for s in range(parts)])]
    pallas_call x0 -> x2, Pallas kernels: none -> 9.22 us  [the longest x1 4.79 us: make_product(): pl.pallas_call(functools.partial(product_kernel, parts, rows), grid_spec=...]
    pallas_call x3 -> x2, Pallas kernels: 20.9 us -> 14 us  [precondition(): pl.pallas_call(functools.partial(root_kernel, parts, len(lefts[0])), grid...]
    ppermute x9 -> x10, starting transfers between devices: 5.99 us -> 7.36 us  [around(): lax.ppermute(x, 'tensor', [(s, (s + d) % parts) for s in range(parts)])]
  transfers between devices with their start and end apart: 15 -> 16, of which waited for: 11 -> 12; matrix products, arithmetic and copies ran while one was open for 1% -> 2% of each run, Pallas kernels for 20% -> 22%
where the time goes in v4:
time: 198 us; the launch traced here: 197 us
  waiting for transfers between devices  101 us (51%)
  Pallas kernels  45.7 us (23%)
  starting transfers between devices  41.8 us (21%)
  local copies, waits for them, and re-layouts  8.33 us (4%)
    ppermute x10, waiting for transfers between devices, around(): lax.ppermute(x, 'tensor', [(s, (s + d) % parts) for s in range(parts)])  67.3 us
    all_to_all x6, starting transfers between devices, swap(): return lax.all_to_all(x, 'dp', split_axis=0, concat_axis=0, tiled=True)  34.4 us
    all_to_all x6, waiting for transfers between devices, swap(): return lax.all_to_all(x, 'dp', split_axis=0, concat_axis=0, tiled=True)  33.5 us
    pallas_call x2, Pallas kernels, precondition(): pl.pallas_call(functools.partial(root_kernel, parts, len(lefts[0])), grid...  14 us
    pallas_call x3, Pallas kernels, rescale(): pl.pallas_call(functools.partial(scale_kernel, float(order * order)), out...  8.78 us
    pallas_call x2, Pallas kernels, make_moment(): pl.pallas_call(functools.partial(moment_kernel, slots), grid_spec=pltpu.P...  8.74 us
    ppermute x10, starting transfers between devices, around(): lax.ppermute(x, 'tensor', [(s, (s + d) % parts) for s in range(parts)])  7.36 us
    slice x3, local copies, waits for them, and re-layouts, send(): rows = flat[first * unit:end * unit]  5.6 us
  transfers between devices with their start and end apart: 16, of which 12 were waited for; matrix products, arithmetic and copies ran while one was open for 2% of the time, Pallas kernels for 22%

profile of v4, /device:TPU:11, one launch (start us, length us, event | category | flops | bytes accessed | tf_op | source)
XLA Modules:
  0.0 197.3 jit_solution(18144025778879431061)
XLA Ops:
  0.6 1.5 slice.21
  2.2 1.3 collective-permute-start.2
  3.5 4.1 %shard_map.77 = (f32[32,64,512]{2,1,0:T(8,128)}, bf16[16,64,512]{2,1,0:T(8,128)(2,1)}) custom-call(s32[32]{0:T(128)} %assign_ref.7, s32[16]{0:T(128)} %count_ref.7, bf16[32,64,512]{2,1,0:T(8,128)(2,1)} %refs_0_.3, f32[32,64,512]{2,1,0:T(8,128)} %refs_1_.3), custom_call_target="tpu_custom_call" | custom-call | flops 157286400 | bytes 629145600 | tf_op jit(solution)/shard_map/pallas_call | solution.py:72
  7.5 6.8 %all-to-all-start = ((bf16[16,64,512]{2,1,0:T(8,128)(2,1)}), bf16[16,64,512]{2,1,0:T(8,128)(2,1)S(1)}, u32[]{:S(2)}, u32[]{:S(2)}) async-start(bf16[16,64,512]{2,1,0:T(8,128)(2,1)} %get-tuple-element.24), calls=%async_computation | async-start | bytes 2097152 | tf_op jit(solution)/shard_map/all_to_all | solution.py:359
  14.4 4.7 %shard_map.78 = (f32[32,64,512]{2,1,0:T(8,128)}, bf16[16,64,512]{2,1,0:T(8,128)(2,1)}, bf16[16,64,512]{2,1,0:T(8,128)(2,1)}) custom-call(s32[32]{0:T(128)} %assign_ref.7, s32[16]{0:T(128)} %count_ref.7, bf16[32,64,512]{2,1,0:T(8,128)(2,1)} %refs_0_.3, f32[32,64,512]{2,1,0:T(8,128)} %refs_1_.3, ...), custom_call_target="tpu_custom_call", output_to_operand_aliasing={{0}: (4, {})} | custom-call | flops 314572800 | bytes 1258291200 | tf_op jit(solution)/shard_map/pallas_call | solution.py:72
  19.1 1.8 fusion
  20.8 16.7 %collective-permute-done.2.refs_1_.refs_4_ = bf16[768,1024]{1,0:T(8,128)(2,1)} collective-permute-done((bf16[768,1024]{1,0:T(8,128)(2,1)S(1)}, bf16[768,1024]{1,0:T(8,128)(2,1)}, u32[]{:S(2)}, u32[]{:S(2)}) %collective-permute-start.2) | collective-permute-done | bytes 1572896 | tf_op jit(solution)/shard_map/ppermute | solution.py:333
  37.6 1.7 all-to-all-done
  39.3 0.0 copy-start.2
  39.3 0.6 collective-permute-start
  39.9 0.8 collective-permute-start.1
  40.7 0.0 copy-done.2
  40.7 6.3 %all-to-all-start.1 = ((bf16[16,64,512]{2,1,0:T(8,128)(2,1)}), bf16[16,64,512]{2,1,0:T(8,128)(2,1)}, u32[]{:S(2)}, u32[]{:S(2)}) async-start(bf16[16,64,512]{2,1,0:T(8,128)(2,1)} %shard_map.81), calls=%async_computation.1 | async-start | bytes 2097152 | tf_op jit(solution)/shard_map/all_to_all | solution.py:359
  47.1 22.4 %collective-permute-done.1.refs_2_.refs_5_ = bf16[128,1024]{1,0:T(8,128)(2,1)S(1)} collective-permute-done((bf16[128,1024]{1,0:T(8,128)(2,1)S(1)}, bf16[128,1024]{1,0:T(8,128)(2,1)S(1)}, u32[]{:S(2)}, u32[]{:S(2)}) %collective-permute-start.1) | collective-permute-done | bytes 262176 | tf_op jit(solution)/shard_map/ppermute | solution.py:333
  69.4 0.0 copy-start.8
  69.4 0.0 collective-permute-done.refs_1_
  69.4 0.0 copy-start.7
  69.4 0.7 copy-done.8
  70.2 0.4 copy-done.7
  70.5 1.5 all-to-all-done.1
  72.0 1.2 collective-permute-start.4
  73.3 5.2 %all-to-all-start.2 = ((bf16[16,64,512]{2,1,0:T(8,128)(2,1)}), bf16[16,64,512]{2,1,0:T(8,128)(2,1)}, u32[]{:S(2)}, u32[]{:S(2)}) async-start(bf16[16,64,512]{2,1,0:T(8,128)(2,1)} %shard_map.82), calls=%async_computation.2 | async-start | bytes 2097152 | tf_op jit(solution)/shard_map/all_to_all | solution.py:359
  78.5 0.0 copy-start.3
  78.5 7.0 %shard_map.84 = (f32[1024,512]{1,0:T(8,128)}, f32[1,128]{1,0:T(1,128)}, f32[1,128]{1,0:T(1,128)}) custom-call(s32[1]{0:T(128)} %bitcast.turn_ref, bf16[1024,512]{1,0:T(8,128)(2,1)} %bitcast.19, bf16[1024,512]{1,0:T(8,128)(2,1)} %copy-done.7, bf16[3,512,1024]{2,1,0:T(8,128)(2,1)} %refs_2_.5, bf16[3,512,1024]{2,1,0:T(8,128)(2,1)} %own_left.1, ...), custom_call_target="tpu_custom_call" | custom-call | flops 214748364800 | bytes 629145600 | tf_op jit(solution)/shard_map/pallas_call | solution.py:183
  85.5 0.2 collective-permute-start.5
  85.7 11.2 %collective-permute-done.5.refs_1_ = f32[1,128]{1,0:T(1,128)S(1)} collective-permute-done((f32[1,128]{1,0:T(1,128)}, f32[1,128]{1,0:T(1,128)S(1)}, u32[]{:S(2)}, u32[]{:S(2)}) %collective-permute-start.5) | collective-permute-done | bytes 544 | tf_op jit(solution)/shard_map/ppermute | solution.py:333
  96.9 0.0 copy-start.4
  96.9 0.0 copy-done.3
  96.9 1.2 collective-permute-start.6
  98.2 0.0 copy-done.4
  98.2 2.9 %shard_map.89 = bf16[1024,512]{1,0:T(8,128)(2,1)} custom-call(f32[1024,512]{1,0:T(8,128)} %get-tuple-element.37.direction, f32[1,128]{1,0:T(1,128)} %get-tuple-element.38.moment_square, f32[1,128]{1,0:T(1,128)} %get-tuple-element.28.refs_0_, f32[1,128]{1,0:T(1,128)} %copy-done.4), custom_call_target="tpu_custom_call" | custom-call | flops 524288 | bytes 3145728 | tf_op jit(solution)/shard_map/pallas_call | solution.py:321
  101.1 2.6 %all-to-all-done.2.refs_0_ = bf16[16,64,512]{2,1,0:T(8,128)(2,1)} async-done(((bf16[16,64,512]{2,1,0:T(8,128)(2,1)}), bf16[16,64,512]{2,1,0:T(8,128)(2,1)}, u32[]{:S(2)}, u32[]{:S(2)}) %all-to-all-start.2) | async-done | bytes 1048608 | tf_op jit(solution)/shard_map/all_to_all | solution.py:359
  103.7 0.2 collective-permute-start.3
  103.9 0.0 collective-permute-done.6.refs_6_.refs_3_
  103.9 0.0 copy-start.9
  103.9 0.0 collective-permute-done.4.refs_1_.refs_2_
  103.9 0.7 copy-done.9
  104.6 6.5 %all-to-all-start.3 = ((bf16[16,64,512]{2,1,0:T(8,128)(2,1)}), bf16[16,64,512]{2,1,0:T(8,128)(2,1)}, u32[]{:S(2)}, u32[]{:S(2)}) async-start(bf16[16,64,512]{2,1,0:T(8,128)(2,1)} %shard_map.90), calls=%async_computation.3 | async-start | bytes 2097152 | tf_op jit(solution)/shard_map/all_to_all | solution.py:359
  111.1 6.9 %shard_map.85 = (f32[1024,512]{1,0:T(8,128)}, f32[1,128]{1,0:T(1,128)}, f32[1,128]{1,0:T(1,128)}) custom-call(s32[1]{0:T(128)} %bitcast.turn_ref, bf16[1024,512]{1,0:T(8,128)(2,1)} %bitcast.3.refs_1_.refs_0_, bf16[1024,512]{1,0:T(8,128)(2,1)} %collective-permute-done.4.refs_1_.refs_2_, bf16[3,512,1024]{2,1,0:T(8,128)(2,1)} %refs_2_.5, ...), custom_call_target="tpu_custom_call" | custom-call | flops 214748364800 | bytes 629145600 | tf_op jit(solution)/shard_map/pallas_call | solution.py:183
  118.0 1.2 collective-permute-start.7
  119.2 2.3 %slice_bitcast_fusion = bf16[512,1024]{1,0:T(8,128)(2,1)} fusion(bf16[3,512,1024]{2,1,0:T(8,128)(2,1)} %own_left.1), kind=kLoop, calls=%fused_computation | loop fusion | bytes 2097152 | tf_op jit(solution)/shard_map/slice | solution.py:380
  121.5 7.2 %collective-permute-done.7.refs_1_ = f32[1,128]{1,0:T(1,128)S(1)} collective-permute-done((f32[1,128]{1,0:T(1,128)}, f32[1,128]{1,0:T(1,128)S(1)}, u32[]{:S(2)}, u32[]{:S(2)}) %collective-permute-start.7) | collective-permute-done | bytes 544 | tf_op jit(solution)/shard_map/ppermute | solution.py:333
  128.8 0.0 copy-start.5
  128.8 0.2 collective-permute-start.8
  129.0 0.3 copy-done.5
  129.3 3.0 %shard_map.88 = bf16[1024,512]{1,0:T(8,128)(2,1)} custom-call(f32[1024,512]{1,0:T(8,128)} %get-tuple-element.35.direction, f32[1,128]{1,0:T(1,128)} %get-tuple-element.36.moment_square, f32[1,128]{1,0:T(1,128)} %get-tuple-element.30.refs_0_, f32[1,128]{1,0:T(1,128)} %copy-done.5), custom_call_target="tpu_custom_call" | custom-call | flops 524288 | bytes 3145728 | tf_op jit(solution)/shard_map/pallas_call | solution.py:321
  132.3 0.0 collective-permute-done.3.refs_2_
  132.3 4.1 %all-to-all-done.3.refs_1_.refs_0_ = bf16[16,64,512]{2,1,0:T(8,128)(2,1)} async-done(((bf16[16,64,512]{2,1,0:T(8,128)(2,1)}), bf16[16,64,512]{2,1,0:T(8,128)(2,1)}, u32[]{:S(2)}, u32[]{:S(2)}) %all-to-all-start.3) | async-done | bytes 1048608 | tf_op jit(solution)/shard_map/all_to_all | solution.py:359
  136.4 4.6 %all-to-all-start.4 = ((bf16[16,64,512]{2,1,0:T(8,128)(2,1)}), bf16[16,64,512]{2,1,0:T(8,128)(2,1)}, u32[]{:S(2)}, u32[]{:S(2)}) async-start(bf16[16,64,512]{2,1,0:T(8,128)(2,1)} %shard_map.91), calls=%async_computation.4 | async-start | bytes 2097152 | tf_op jit(solution)/shard_map/all_to_all | solution.py:359
  141.0 4.8 %shard_map.83 = (bf16[16,64,512]{2,1,0:T(8,128)(2,1)}, f32[1,128]{1,0:T(1,128)}) custom-call(s32[1]{0:T(128)} %bitcast.turn_ref, bf16[16,64,512]{2,1,0:T(8,128)(2,1)} %all-to-all-done.2.refs_0_, bf16[16,64,512]{2,1,0:T(8,128)(2,1)} %bitcast.5.refs_1_, bf16[3,512,1024]{2,1,0:T(8,128)(2,1)} %refs_2_.5), custom_call_target="tpu_custom_call" | custom-call | flops 214748364800 | bytes 629145600 | tf_op jit(solution)/shard_map/pallas_call | solution.py:247
  145.8 7.2 %collective-permute-done.8.refs_0_ = bf16[512,1024]{1,0:T(8,128)(2,1)} collective-permute-done((bf16[512,1024]{1,0:T(8,128)(2,1)}, bf16[512,1024]{1,0:T(8,128)(2,1)}, u32[]{:S(2)}, u32[]{:S(2)}) %collective-permute-start.8) | collective-permute-done | bytes 1048608 | tf_op jit(solution)/shard_map/ppermute | solution.py:333
  152.9 4.4 %shard_map.86 = (f32[1024,512]{1,0:T(8,128)}, f32[1,128]{1,0:T(1,128)}) custom-call(s32[1]{0:T(128)} %bitcast.turn_ref, bf16[1024,512]{1,0:T(8,128)(2,1)} %bitcast.20, bf16[3,512,1024]{2,1,0:T(8,128)(2,1)} %own_left.1, bf16[512,1024]{1,0:T(8,128)(2,1)} %collective-permute-done.8.refs_0_), custom_call_target="tpu_custom_call" | custom-call | flops 1073741824 | bytes 3145728 | tf_op jit(solution)/shard_map/pallas_call | solution.py:295
  157.4 0.2 collective-permute-start.9
  157.6 2.6 %collective-permute-done.9.refs_1_ = f32[1,128]{1,0:T(1,128)S(1)} collective-permute-done((f32[1,128]{1,0:T(1,128)}, f32[1,128]{1,0:T(1,128)S(1)}, u32[]{:S(2)}, u32[]{:S(2)}) %collective-permute-start.9) | collective-permute-done | bytes 544 | tf_op jit(solution)/shard_map/ppermute | solution.py:333
  160.2 0.0 copy-start.6
  160.2 0.6 copy-done.6
  160.8 2.9 %shard_map.87 = bf16[1024,512]{1,0:T(8,128)(2,1)} custom-call(f32[1024,512]{1,0:T(8,128)} %get-tuple-element.32.direction, f32[1,128]{1,0:T(1,128)} %get-tuple-element.33.moment_square, f32[1,128]{1,0:T(1,128)} %get-tuple-element.34.refs_0_, f32[1,128]{1,0:T(1,128)} %copy-done.6), custom_call_target="tpu_custom_call" | custom-call | flops 524288 | bytes 3145728 | tf_op jit(solution)/shard_map/pallas_call | solution.py:321
  163.7 2.3 %all-to-all-done.4.refs_1_ = bf16[16,64,512]{2,1,0:T(8,128)(2,1)} async-done(((bf16[16,64,512]{2,1,0:T(8,128)(2,1)}), bf16[16,64,512]{2,1,0:T(8,128)(2,1)}, u32[]{:S(2)}, u32[]{:S(2)}) %all-to-all-start.4) | async-done | bytes 1048608 | tf_op jit(solution)/shard_map/all_to_all | solution.py:359
  166.0 4.9 %all-to-all-start.5 = ((bf16[16,64,512]{2,1,0:T(8,128)(2,1)}), bf16[16,64,512]{2,1,0:T(8,128)(2,1)S(1)}, u32[]{:S(2)}, u32[]{:S(2)}) async-start(bf16[16,64,512]{2,1,0:T(8,128)(2,1)} %bitcast.15), calls=%async_computation.5 | async-start | bytes 2097152 | tf_op jit(solution)/shard_map/all_to_all | solution.py:359
  170.9 0.0 copy-done
  170.9 0.0 copy-done.1
  170.9 3.5 %shard_map.92.refs_1_ = bf16[32,64,512]{2,1,0:T(8,128)(2,1)} custom-call(s32[32]{0:T(128)S(1)} %copy-done, s32[16]{0:T(128)S(1)} %copy-done.1, bf16[16,64,512]{2,1,0:T(8,128)(2,1)} %all-to-all-done.3.refs_1_.refs_0_, bf16[16,64,512]{2,1,0:T(8,128)(2,1)} %all-to-all-done.4.refs_1_), custom_call_target="tpu_custom_call" | custom-call | bytes 4194304 | tf_op jit(solution)/shard_map/pallas_call | solution.py:112
  174.4 21.4 %all-to-all-done.5.refs_0_ = bf16[16,64,512]{2,1,0:T(8,128)(2,1)S(1)} async-done(((bf16[16,64,512]{2,1,0:T(8,128)(2,1)}), bf16[16,64,512]{2,1,0:T(8,128)(2,1)S(1)}, u32[]{:S(2)}, u32[]{:S(2)}) %all-to-all-start.5) | async-done | bytes 1048608 | tf_op jit(solution)/shard_map/all_to_all | solution.py:359
  195.8 1.5 shard_map.93
  (8 shorter events, 0.0 us)
Async XLA Ops:
  2.2 35.4 %collective-permute-start.2 = (bf16[768,1024]{1,0:T(8,128)(2,1)S(1)}, bf16[768,1024]{1,0:T(8,128)(2,1)}, u32[]{:S(2)}, u32[]{:S(2)}) collective-permute-start(bf16[768,1024]{1,0:T(8,128)(2,1)S(1)} %slice.21), channel_id=1, source_target_pairs={{0,1},{1,0},{2,3},{3,2},{4,5},{5,4},{6,7},{7,6},{8,9},{9,8},{10,11... | collective-permute-start | bytes 4718600 | tf_op jit(solution)/shard_map/ppermute | solution.py:333
  7.5 31.7 %all-to-all-start = ((bf16[16,64,512]{2,1,0:T(8,128)(2,1)}), bf16[16,64,512]{2,1,0:T(8,128)(2,1)S(1)}, u32[]{:S(2)}, u32[]{:S(2)}) async-start(bf16[16,64,512]{2,1,0:T(8,128)(2,1)} %get-tuple-element.24), calls=%async_computation | async-start | bytes 2097152 | tf_op jit(solution)/shard_map/all_to_all | solution.py:359
  39.3 1.5 copy-start.2
  39.3 30.2 %collective-permute-start = (bf16[1024,512]{1,0:T(8,128)(2,1)S(1)}, bf16[1024,512]{1,0:T(8,128)(2,1)S(1)}, u32[]{:S(2)}, u32[]{:S(2)}) collective-permute-start(bf16[1024,512]{1,0:T(8,128)(2,1)S(1)} %bitcast.17), channel_id=1, source_target_pairs={{0,1},{1,0},{2,3},{3,2},{4,5},{5,4},{6,7},{7,6},{8,9},{9,8},{10,11... | collective-permute-start | bytes 3145736 | tf_op jit(solution)/shard_map/ppermute | solution.py:333
  39.9 29.5 %collective-permute-start.1 = (bf16[128,1024]{1,0:T(8,128)(2,1)S(1)}, bf16[128,1024]{1,0:T(8,128)(2,1)S(1)}, u32[]{:S(2)}, u32[]{:S(2)}) collective-permute-start(bf16[128,1024]{1,0:T(8,128)(2,1)S(1)} %get-tuple-element.25), channel_id=1, source_target_pairs={{0,1},{1,0},{2,3},{3,2},{4,5},{5,4},{6,7},{7,6},{8,9},{9,8},{10,11... | collective-permute-start | bytes 786440 | tf_op jit(solution)/shard_map/ppermute | solution.py:333
  40.7 31.3 %all-to-all-start.1 = ((bf16[16,64,512]{2,1,0:T(8,128)(2,1)}), bf16[16,64,512]{2,1,0:T(8,128)(2,1)}, u32[]{:S(2)}, u32[]{:S(2)}) async-start(bf16[16,64,512]{2,1,0:T(8,128)(2,1)} %shard_map.81), calls=%async_computation.1 | async-start | bytes 2097152 | tf_op jit(solution)/shard_map/all_to_all | solution.py:359
  69.4 0.7 copy-start.8
  69.4 1.1 copy-start.7
  72.0 31.9 %collective-permute-start.4 = (bf16[1024,512]{1,0:T(8,128)(2,1)}, bf16[1024,512]{1,0:T(8,128)(2,1)}, u32[]{:S(2)}, u32[]{:S(2)}) collective-permute-start(bf16[1024,512]{1,0:T(8,128)(2,1)} %bitcast.3.refs_1_.refs_0_), channel_id=1, source_target_pairs={{0,1},{1,0},{2,3},{3,2},{4,5},{5,4},{6,7},{7,6},{8,9},{9,8},{10,11... | collective-permute-start | bytes 3145736 | tf_op jit(solution)/shard_map/ppermute | solution.py:333
  73.3 30.4 %all-to-all-start.2 = ((bf16[16,64,512]{2,1,0:T(8,128)(2,1)}), bf16[16,64,512]{2,1,0:T(8,128)(2,1)}, u32[]{:S(2)}, u32[]{:S(2)}) async-start(bf16[16,64,512]{2,1,0:T(8,128)(2,1)} %shard_map.82), calls=%async_computation.2 | async-start | bytes 2097152 | tf_op jit(solution)/shard_map/all_to_all | solution.py:359
  78.5 18.4 %copy-start.3 = (bf16[128,1024]{1,0:T(8,128)(2,1)S(1)}, bf16[128,1024]{1,0:T(8,128)(2,1)}, u32[]{:S(2)}) copy-start(bf16[128,1024]{1,0:T(8,128)(2,1)} %get-tuple-element.29) | copy-start | bytes 786436
  85.5 11.4 %collective-permute-start.5 = (f32[1,128]{1,0:T(1,128)}, f32[1,128]{1,0:T(1,128)S(1)}, u32[]{:S(2)}, u32[]{:S(2)}) collective-permute-start(f32[1,128]{1,0:T(1,128)} %get-tuple-element.28.refs_0_), channel_id=1, source_target_pairs={{0,1},{1,0},{2,3},{3,2},{4,5},{5,4},{6,7},{7,6},{8,9},{9,8},{10,11... | collective-permute-start | bytes 1544 | tf_op jit(solution)/shard_map/ppermute | solution.py:333
  96.9 1.2 copy-start.4
  96.9 7.0 %collective-permute-start.6 = (bf16[128,1024]{1,0:T(8,128)(2,1)S(1)}, bf16[128,1024]{1,0:T(8,128)(2,1)S(1)}, u32[]{:S(2)}, u32[]{:S(2)}) collective-permute-start(bf16[128,1024]{1,0:T(8,128)(2,1)S(1)} %copy-done.3), channel_id=1, source_target_pairs={{0,1},{1,0},{2,3},{3,2},{4,5},{5,4},{6,7},{7,6},{8,9},{9,8},{10,11... | collective-permute-start | bytes 786440 | tf_op jit(solution)/shard_map/ppermute | solution.py:333
  103.7 28.6 %collective-permute-start.3 = (bf16[1024,512]{1,0:T(8,128)(2,1)}, bf16[1024,512]{1,0:T(8,128)(2,1)}, u32[]{:S(2)}, u32[]{:S(2)}) collective-permute-start(bf16[1024,512]{1,0:T(8,128)(2,1)} %bitcast.4.refs_1_), channel_id=1, source_target_pairs={{0,1},{1,0},{2,3},{3,2},{4,5},{5,4},{6,7},{7,6},{8,9},{9,8},{10,11... | collective-permute-start | bytes 3145736 | tf_op jit(solution)/shard_map/ppermute | solution.py:333
  103.9 0.7 copy-start.9
  104.6 31.7 %all-to-all-start.3 = ((bf16[16,64,512]{2,1,0:T(8,128)(2,1)}), bf16[16,64,512]{2,1,0:T(8,128)(2,1)}, u32[]{:S(2)}, u32[]{:S(2)}) async-start(bf16[16,64,512]{2,1,0:T(8,128)(2,1)} %shard_map.90), calls=%async_computation.3 | async-start | bytes 2097152 | tf_op jit(solution)/shard_map/all_to_all | solution.py:359
  118.0 10.7 %collective-permute-start.7 = (f32[1,128]{1,0:T(1,128)}, f32[1,128]{1,0:T(1,128)S(1)}, u32[]{:S(2)}, u32[]{:S(2)}) collective-permute-start(f32[1,128]{1,0:T(1,128)} %get-tuple-element.30.refs_0_), channel_id=1, source_target_pairs={{0,1},{1,0},{2,3},{3,2},{4,5},{5,4},{6,7},{7,6},{8,9},{9,8},{10,11... | collective-permute-start | bytes 1544 | tf_op jit(solution)/shard_map/ppermute | solution.py:333
  128.8 0.6 copy-start.5
  128.8 24.2 %collective-permute-start.8 = (bf16[512,1024]{1,0:T(8,128)(2,1)}, bf16[512,1024]{1,0:T(8,128)(2,1)}, u32[]{:S(2)}, u32[]{:S(2)}) collective-permute-start(bf16[512,1024]{1,0:T(8,128)(2,1)} %slice_bitcast_fusion), channel_id=1, source_target_pairs={{0,1},{1,0},{2,3},{3,2},{4,5},{5,4},{6,7},{7,6},{8,9},{9,8},{10,11... | collective-permute-start | bytes 3145736 | tf_op jit(solution)/shard_map/ppermute | solution.py:333
  136.4 29.6 %all-to-all-start.4 = ((bf16[16,64,512]{2,1,0:T(8,128)(2,1)}), bf16[16,64,512]{2,1,0:T(8,128)(2,1)}, u32[]{:S(2)}, u32[]{:S(2)}) async-start(bf16[16,64,512]{2,1,0:T(8,128)(2,1)} %shard_map.91), calls=%async_computation.4 | async-start | bytes 2097152 | tf_op jit(solution)/shard_map/all_to_all | solution.py:359
  157.4 2.8 %collective-permute-start.9 = (f32[1,128]{1,0:T(1,128)}, f32[1,128]{1,0:T(1,128)S(1)}, u32[]{:S(2)}, u32[]{:S(2)}) collective-permute-start(f32[1,128]{1,0:T(1,128)} %get-tuple-element.34.refs_0_), channel_id=1, source_target_pairs={{0,1},{1,0},{2,3},{3,2},{4,5},{5,4},{6,7},{7,6},{8,9},{9,8},{10,11... | collective-permute-start | bytes 1544 | tf_op jit(solution)/shard_map/ppermute | solution.py:333
  160.2 0.6 copy-start.6
  160.8 10.1 %copy-start = (s32[32]{0:T(128)S(1)}, s32[32]{0:T(128)}, u32[]{:S(2)}) copy-start(s32[32]{0:T(128)} %assign_ref.7) | copy-start | bytes 388
  160.8 10.1 %copy-start.1 = (s32[16]{0:T(128)S(1)}, s32[16]{0:T(128)}, u32[]{:S(2)}) copy-start(s32[16]{0:T(128)} %count_ref.7) | copy-start | bytes 196
  166.0 29.8 %all-to-all-start.5 = ((bf16[16,64,512]{2,1,0:T(8,128)(2,1)}), bf16[16,64,512]{2,1,0:T(8,128)(2,1)S(1)}, u32[]{:S(2)}, u32[]{:S(2)}) async-start(bf16[16,64,512]{2,1,0:T(8,128)(2,1)} %bitcast.15), calls=%async_computation.5 | async-start | bytes 2097152 | tf_op jit(solution)/shard_map/all_to_all | solution.py:359

commit v5 on v4

--- a/solution.py
+++ b/solution.py
@@ -299,10 +299,10 @@
             grid=(1,),
             in_specs=[whole, pl.BlockSpec((1, width, order), lambda i, t: (slot, 0, 0))]
             + [pl.BlockSpec((n, order), lambda i, t, at=at: (at, 0)) for _, n, at in pieces],
-            out_specs=[whole, pl.BlockSpec((1, 128), lambda i, t: (0, 0))],
+            out_specs=[pl.BlockSpec(memory_space=pltpu.VMEM)] * 2,
         ),
         out_shape=[jax.ShapeDtypeStruct((order, width), jnp.float32), jax.ShapeDtypeStruct((1, 128), jnp.float32)],
-        compiler_params=pltpu.CompilerParams(vmem_limit_bytes=60 * MIB),
+        compiler_params=pltpu.CompilerParams(vmem_limit_bytes=40 * MIB),
         cost_estimate=pl.CostEstimate(
             flops=2 * order * order * width, bytes_accessed=6 * order * width, transcendentals=0
         ),
@@ -316,12 +316,16 @@
     out_ref[...] = (direction[...] * scale).astype(jnp.bfloat16)
 
 
-def rescale(direction, moment_square, squares):
+def rescale(direction, moment_square, squares, near):
     order, width = direction.shape
+    vmem = pl.BlockSpec(memory_space=pltpu.VMEM)
+    whole = pl.BlockSpec((order, width), lambda: (0, 0))
     return pl.pallas_call(
         functools.partial(scale_kernel, float(order * order)),
+        in_specs=[vmem if near else whole] + [vmem] * (1 + len(squares)),
+        out_specs=whole,
         out_shape=jax.ShapeDtypeStruct((order, width), jnp.bfloat16),
-        compiler_params=pltpu.CompilerParams(vmem_limit_bytes=60 * MIB),
+        compiler_params=pltpu.CompilerParams(vmem_limit_bytes=(32 if near else 60) * MIB),
         cost_estimate=pl.CostEstimate(
             flops=order * width, bytes_accessed=6 * order * width, transcendentals=0
         ),
@@ -369,7 +373,7 @@
                 s, turn, [columns] + others, right_root, left_root, lefts
             )
         squares = [square] + around(square, parts)
-        scaled = rescale(direction, wanted, squares)
+        scaled = rescale(direction, wanted, squares, apart)
         return scaled.reshape(owners, order // owners, width), squares[-1]
 
     unit = width // 4
@@ -405,7 +409,7 @@
     e2 = send(7, 8, q0)
     m2 = around(columns2, parts)
     e3 = []
-    b0 = swap(gate(d0, columns2, *m1, *e2))
+    b0 = swap(gate(d0, columns2, *m1))
     d1, q1 = solve(1, columns1, m1, lefts(1))
     e4 = send(8, 12, q1)
     b1 = swap(gate(d1, b0, *m2))

time: 198 us -> 196 us (0.990)
  Pallas kernels: 45.7 us -> 42.3 us
  waiting for transfers between devices: 101 us -> 103 us
    ppermute x10, waiting for transfers between devices: 67.3 us -> 70.3 us  [around(): lax.ppermute(x, 'tensor', [(s, (s + d) % parts) for s in range(parts)])]
  transfers between devices with their start and end apart: 16 -> 16, of which waited for: 12 -> 12; matrix products, arithmetic and copies ran while one was open for 2% -> 2% of each run, Pallas kernels for 22% -> 21%
where the time goes in v5:
time: 196 us; the launch traced here: 195 us
  waiting for transfers between devices  103 us (53%)
  Pallas kernels  42.3 us (22%)
  starting transfers between devices  40.4 us (21%)
  local copies, waits for them, and re-layouts  8.97 us (5%)
    ppermute x10, waiting for transfers between devices, around(): lax.ppermute(x, 'tensor', [(s, (s + d) % parts) for s in range(parts)])  70.3 us
    all_to_all x6, starting transfers between devices, swap(): return lax.all_to_all(x, 'dp', split_axis=0, concat_axis=0, tiled=True)  33 us
    all_to_all x6, waiting for transfers between devices, swap(): return lax.all_to_all(x, 'dp', split_axis=0, concat_axis=0, tiled=True)  32.4 us
    pallas_call x2, Pallas kernels, precondition(): pl.pallas_call(functools.partial(root_kernel, parts, len(lefts[0])), grid...  14 us
    pallas_call x2, Pallas kernels, make_moment(): pl.pallas_call(functools.partial(moment_kernel, slots), grid_spec=pltpu.P...  8.72 us
    ppermute x10, starting transfers between devices, around(): lax.ppermute(x, 'tensor', [(s, (s + d) % parts) for s in range(parts)])  7.36 us
    pallas_call x3, Pallas kernels, rescale(): pl.pallas_call(functools.partial(scale_kernel, float(order * order)), in_...  7.21 us
    slice x3, local copies, waits for them, and re-layouts, send(): rows = flat[first * unit:end * unit]  5.58 us
  transfers between devices with their start and end apart: 16, of which 12 were waited for; matrix products, arithmetic and copies ran while one was open for 2% of the time, Pallas kernels for 21%

profile of v5, /device:TPU:11, one launch (start us, length us, event | category | flops | bytes accessed | tf_op | source)
XLA Modules:
  0.0 195.1 jit_solution(5425420608209483015)
XLA Ops:
  0.6 1.5 slice.21
  2.2 1.3 collective-permute-start.2
  3.5 4.1 %shard_map.77 = (f32[32,64,512]{2,1,0:T(8,128)}, bf16[16,64,512]{2,1,0:T(8,128)(2,1)}) custom-call(s32[32]{0:T(128)} %assign_ref.7, s32[16]{0:T(128)} %count_ref.7, bf16[32,64,512]{2,1,0:T(8,128)(2,1)} %refs_0_.3, f32[32,64,512]{2,1,0:T(8,128)} %refs_1_.3), custom_call_target="tpu_custom_call" | custom-call | flops 157286400 | bytes 629145600 | tf_op jit(solution)/shard_map/pallas_call | solution.py:72
  7.5 6.8 %all-to-all-start = ((bf16[16,64,512]{2,1,0:T(8,128)(2,1)}), bf16[16,64,512]{2,1,0:T(8,128)(2,1)S(1)}, u32[]{:S(2)}, u32[]{:S(2)}) async-start(bf16[16,64,512]{2,1,0:T(8,128)(2,1)} %get-tuple-element.24), calls=%async_computation | async-start | bytes 2097152 | tf_op jit(solution)/shard_map/all_to_all | solution.py:363
  14.4 4.7 %shard_map.78 = (f32[32,64,512]{2,1,0:T(8,128)}, bf16[16,64,512]{2,1,0:T(8,128)(2,1)}, bf16[16,64,512]{2,1,0:T(8,128)(2,1)}) custom-call(s32[32]{0:T(128)} %assign_ref.7, s32[16]{0:T(128)} %count_ref.7, bf16[32,64,512]{2,1,0:T(8,128)(2,1)} %refs_0_.3, f32[32,64,512]{2,1,0:T(8,128)} %refs_1_.3, ...), custom_call_target="tpu_custom_call", output_to_operand_aliasing={{0}: (4, {})} | custom-call | flops 314572800 | bytes 1258291200 | tf_op jit(solution)/shard_map/pallas_call | solution.py:72
  19.1 1.8 fusion
  20.8 16.8 %collective-permute-done.2.refs_1_.refs_4_ = bf16[768,1024]{1,0:T(8,128)(2,1)} collective-permute-done((bf16[768,1024]{1,0:T(8,128)(2,1)S(1)}, bf16[768,1024]{1,0:T(8,128)(2,1)}, u32[]{:S(2)}, u32[]{:S(2)}) %collective-permute-start.2) | collective-permute-done | bytes 1572896 | tf_op jit(solution)/shard_map/ppermute | solution.py:337
  37.6 1.7 all-to-all-done
  39.3 0.0 copy-start.5
  39.3 0.6 collective-permute-start
  39.9 0.8 collective-permute-start.1
  40.7 0.0 copy-done.5
  40.7 6.3 %all-to-all-start.1 = ((bf16[16,64,512]{2,1,0:T(8,128)(2,1)}), bf16[16,64,512]{2,1,0:T(8,128)(2,1)}, u32[]{:S(2)}, u32[]{:S(2)}) async-start(bf16[16,64,512]{2,1,0:T(8,128)(2,1)} %shard_map.81), calls=%async_computation.1 | async-start | bytes 2097152 | tf_op jit(solution)/shard_map/all_to_all | solution.py:363
  47.1 22.4 %collective-permute-done.1.refs_2_.refs_5_ = bf16[128,1024]{1,0:T(8,128)(2,1)S(1)} collective-permute-done((bf16[128,1024]{1,0:T(8,128)(2,1)S(1)}, bf16[128,1024]{1,0:T(8,128)(2,1)S(1)}, u32[]{:S(2)}, u32[]{:S(2)}) %collective-permute-start.1) | collective-permute-done | bytes 262176 | tf_op jit(solution)/shard_map/ppermute | solution.py:337
  69.4 0.0 copy-start.10
  69.4 0.0 collective-permute-done.refs_1_
  69.4 0.0 copy-start.9
  69.4 0.7 copy-done.10
  70.2 0.4 copy-done.9
  70.5 1.5 all-to-all-done.1
  72.0 1.2 collective-permute-start.4
  73.3 5.2 %all-to-all-start.2 = ((bf16[16,64,512]{2,1,0:T(8,128)(2,1)}), bf16[16,64,512]{2,1,0:T(8,128)(2,1)}, u32[]{:S(2)}, u32[]{:S(2)}) async-start(bf16[16,64,512]{2,1,0:T(8,128)(2,1)} %shard_map.82), calls=%async_computation.2 | async-start | bytes 2097152 | tf_op jit(solution)/shard_map/all_to_all | solution.py:363
  78.5 0.0 copy-start.6
  78.5 7.0 %shard_map.84 = (f32[1024,512]{1,0:T(8,128)}, f32[1,128]{1,0:T(1,128)}, f32[1,128]{1,0:T(1,128)}) custom-call(s32[1]{0:T(128)} %bitcast.turn_ref, bf16[1024,512]{1,0:T(8,128)(2,1)} %bitcast.19, bf16[1024,512]{1,0:T(8,128)(2,1)} %copy-done.9, bf16[3,512,1024]{2,1,0:T(8,128)(2,1)} %refs_2_.5, bf16[3,512,1024]{2,1,0:T(8,128)(2,1)} %own_left.1, ...), custom_call_target="tpu_custom_call" | custom-call | flops 214748364800 | bytes 629145600 | tf_op jit(solution)/shard_map/pallas_call | solution.py:183
  85.5 0.2 collective-permute-start.5
  85.7 11.2 %collective-permute-done.5.refs_1_ = f32[1,128]{1,0:T(1,128)S(1)} collective-permute-done((f32[1,128]{1,0:T(1,128)}, f32[1,128]{1,0:T(1,128)S(1)}, u32[]{:S(2)}, u32[]{:S(2)}) %collective-permute-start.5) | collective-permute-done | bytes 544 | tf_op jit(solution)/shard_map/ppermute | solution.py:337
  96.9 0.0 copy-start.7
  96.9 0.0 copy-done.6
  96.9 1.2 collective-permute-start.6
  98.2 0.0 copy-done.7
  98.2 2.9 %shard_map.89 = bf16[1024,512]{1,0:T(8,128)(2,1)} custom-call(f32[1024,512]{1,0:T(8,128)} %get-tuple-element.37.direction, f32[1,128]{1,0:T(1,128)} %get-tuple-element.38.moment_square, f32[1,128]{1,0:T(1,128)} %get-tuple-element.28.refs_0_, f32[1,128]{1,0:T(1,128)} %copy-done.7), custom_call_target="tpu_custom_call" | custom-call | flops 524288 | bytes 3145728 | tf_op jit(solution)/shard_map/pallas_call | solution.py:323
  101.1 2.6 %all-to-all-done.2.refs_0_ = bf16[16,64,512]{2,1,0:T(8,128)(2,1)} async-done(((bf16[16,64,512]{2,1,0:T(8,128)(2,1)}), bf16[16,64,512]{2,1,0:T(8,128)(2,1)}, u32[]{:S(2)}, u32[]{:S(2)}) %all-to-all-start.2) | async-done | bytes 1048608 | tf_op jit(solution)/shard_map/all_to_all | solution.py:363
  103.7 0.2 collective-permute-start.3
  103.9 0.0 collective-permute-done.4.refs_1_.refs_2_
  103.9 5.0 %all-to-all-start.3 = ((bf16[16,64,512]{2,1,0:T(8,128)(2,1)}), bf16[16,64,512]{2,1,0:T(8,128)(2,1)}, u32[]{:S(2)}, u32[]{:S(2)}) async-start(bf16[16,64,512]{2,1,0:T(8,128)(2,1)} %shard_map.90), calls=%async_computation.3 | async-start | bytes 2097152 | tf_op jit(solution)/shard_map/all_to_all | solution.py:363
  108.9 0.0 collective-permute-done.6.refs_6_
  108.9 0.0 copy-start.11
  108.9 0.7 copy-done.11
  109.6 6.9 %shard_map.85 = (f32[1024,512]{1,0:T(8,128)}, f32[1,128]{1,0:T(1,128)}, f32[1,128]{1,0:T(1,128)}) custom-call(s32[1]{0:T(128)} %bitcast.turn_ref, bf16[1024,512]{1,0:T(8,128)(2,1)} %bitcast.3.refs_1_.refs_0_, bf16[1024,512]{1,0:T(8,128)(2,1)} %collective-permute-done.4.refs_1_.refs_2_, bf16[3,512,1024]{2,1,0:T(8,128)(2,1)} %refs_2_.5, ...), custom_call_target="tpu_custom_call" | custom-call | flops 214748364800 | bytes 629145600 | tf_op jit(solution)/shard_map/pallas_call | solution.py:183
  116.6 1.2 collective-permute-start.7
  117.8 2.3 %slice_bitcast_fusion = bf16[512,1024]{1,0:T(8,128)(2,1)} fusion(bf16[3,512,1024]{2,1,0:T(8,128)(2,1)} %own_left.1), kind=kLoop, calls=%fused_computation | loop fusion | bytes 2097152 | tf_op jit(solution)/shard_map/slice | solution.py:384
  120.1 8.7 %collective-permute-done.7.refs_1_ = f32[1,128]{1,0:T(1,128)S(1)} collective-permute-done((f32[1,128]{1,0:T(1,128)}, f32[1,128]{1,0:T(1,128)S(1)}, u32[]{:S(2)}, u32[]{:S(2)}) %collective-permute-start.7) | collective-permute-done | bytes 544 | tf_op jit(solution)/shard_map/ppermute | solution.py:337
  128.8 0.2 collective-permute-start.8
  129.0 0.3 copy-done.8
  129.3 3.0 %shard_map.88 = bf16[1024,512]{1,0:T(8,128)(2,1)} custom-call(f32[1024,512]{1,0:T(8,128)} %get-tuple-element.35.direction, f32[1,128]{1,0:T(1,128)} %get-tuple-element.36.moment_square, f32[1,128]{1,0:T(1,128)} %get-tuple-element.30.refs_0_, f32[1,128]{1,0:T(1,128)} %copy-done.8), custom_call_target="tpu_custom_call" | custom-call | flops 524288 | bytes 3145728 | tf_op jit(solution)/shard_map/pallas_call | solution.py:323
  132.3 0.0 collective-permute-done.3.refs_2_
  132.3 1.9 all-to-all-done.3.refs_1_.refs_0_
  134.2 4.6 %all-to-all-start.4 = ((bf16[16,64,512]{2,1,0:T(8,128)(2,1)}), bf16[16,64,512]{2,1,0:T(8,128)(2,1)}, u32[]{:S(2)}, u32[]{:S(2)}) async-start(bf16[16,64,512]{2,1,0:T(8,128)(2,1)} %shard_map.91), calls=%async_computation.4 | async-start | bytes 2097152 | tf_op jit(solution)/shard_map/all_to_all | solution.py:363
  138.9 4.9 %shard_map.83 = (bf16[16,64,512]{2,1,0:T(8,128)(2,1)}, f32[1,128]{1,0:T(1,128)}) custom-call(s32[1]{0:T(128)} %bitcast.turn_ref, bf16[16,64,512]{2,1,0:T(8,128)(2,1)} %all-to-all-done.2.refs_0_, bf16[16,64,512]{2,1,0:T(8,128)(2,1)} %bitcast.5.refs_1_, bf16[3,512,1024]{2,1,0:T(8,128)(2,1)} %refs_2_.5), custom_call_target="tpu_custom_call" | custom-call | flops 214748364800 | bytes 629145600 | tf_op jit(solution)/shard_map/pallas_call | solution.py:247
  143.8 9.2 %collective-permute-done.8.refs_0_ = bf16[512,1024]{1,0:T(8,128)(2,1)} collective-permute-done((bf16[512,1024]{1,0:T(8,128)(2,1)}, bf16[512,1024]{1,0:T(8,128)(2,1)}, u32[]{:S(2)}, u32[]{:S(2)}) %collective-permute-start.8) | collective-permute-done | bytes 1048608 | tf_op jit(solution)/shard_map/ppermute | solution.py:337
  152.9 0.0 copy-done
  152.9 1.2 copy-done.1
  154.2 2.6 %shard_map.86 = (f32[1024,512]{1,0:T(8,128)S(1)}, f32[1,128]{1,0:T(1,128)S(1)}) custom-call(s32[1]{0:T(128)} %bitcast.turn_ref, bf16[1024,512]{1,0:T(8,128)(2,1)S(1)} %bitcast.14, bf16[3,512,1024]{2,1,0:T(8,128)(2,1)S(1)} %copy-done, bf16[512,1024]{1,0:T(8,128)(2,1)} %collective-permute-done.8.refs_0_), custom_call_target="tpu_custom_call" | custom-call | flops 1073741824 | bytes 3145728 | tf_op jit(solution)/shard_map/pallas_call | solution.py:295
  156.7 0.2 collective-permute-start.9
  157.0 2.2 %collective-permute-done.9.refs_1_ = f32[1,128]{1,0:T(1,128)S(1)} collective-permute-done((f32[1,128]{1,0:T(1,128)S(1)}, f32[1,128]{1,0:T(1,128)S(1)}, u32[]{:S(2)}, u32[]{:S(2)}) %collective-permute-start.9) | collective-permute-done | bytes 544 | tf_op jit(solution)/shard_map/ppermute | solution.py:337
  159.1 0.0 copy-done.4
  159.1 1.3 shard_map.87
  160.5 3.4 %all-to-all-done.4.refs_1_ = bf16[16,64,512]{2,1,0:T(8,128)(2,1)} async-done(((bf16[16,64,512]{2,1,0:T(8,128)(2,1)}), bf16[16,64,512]{2,1,0:T(8,128)(2,1)}, u32[]{:S(2)}, u32[]{:S(2)}) %all-to-all-start.4) | async-done | bytes 1048608 | tf_op jit(solution)/shard_map/all_to_all | solution.py:363
  163.8 4.9 %all-to-all-start.5 = ((bf16[16,64,512]{2,1,0:T(8,128)(2,1)}), bf16[16,64,512]{2,1,0:T(8,128)(2,1)S(1)}, u32[]{:S(2)}, u32[]{:S(2)}) async-start(bf16[16,64,512]{2,1,0:T(8,128)(2,1)} %bitcast.8), calls=%async_computation.5 | async-start | bytes 2097152 | tf_op jit(solution)/shard_map/all_to_all | solution.py:363
  168.8 0.0 copy-done.2
  168.8 0.0 copy-done.3
  168.8 3.5 %shard_map.92.refs_1_ = bf16[32,64,512]{2,1,0:T(8,128)(2,1)} custom-call(s32[32]{0:T(128)S(1)} %copy-done.2, s32[16]{0:T(128)S(1)} %copy-done.3, bf16[16,64,512]{2,1,0:T(8,128)(2,1)} %all-to-all-done.3.refs_1_.refs_0_, bf16[16,64,512]{2,1,0:T(8,128)(2,1)} %all-to-all-done.4.refs_1_), custom_call_target="tpu_custom_call" | custom-call | bytes 4194304 | tf_op jit(solution)/shard_map/pallas_call | solution.py:112
  172.3 21.3 %all-to-all-done.5.refs_0_ = bf16[16,64,512]{2,1,0:T(8,128)(2,1)S(1)} async-done(((bf16[16,64,512]{2,1,0:T(8,128)(2,1)}), bf16[16,64,512]{2,1,0:T(8,128)(2,1)S(1)}, u32[]{:S(2)}, u32[]{:S(2)}) %all-to-all-start.5) | async-done | bytes 1048608 | tf_op jit(solution)/shard_map/all_to_all | solution.py:363
  193.6 1.5 shard_map.93
  (12 shorter events, 0.0 us)
Async XLA Ops:
  2.2 35.4 %collective-permute-start.2 = (bf16[768,1024]{1,0:T(8,128)(2,1)S(1)}, bf16[768,1024]{1,0:T(8,128)(2,1)}, u32[]{:S(2)}, u32[]{:S(2)}) collective-permute-start(bf16[768,1024]{1,0:T(8,128)(2,1)S(1)} %slice.21), channel_id=1, source_target_pairs={{0,1},{1,0},{2,3},{3,2},{4,5},{5,4},{6,7},{7,6},{8,9},{9,8},{10,11... | collective-permute-start | bytes 4718600 | tf_op jit(solution)/shard_map/ppermute | solution.py:337
  7.5 31.7 %all-to-all-start = ((bf16[16,64,512]{2,1,0:T(8,128)(2,1)}), bf16[16,64,512]{2,1,0:T(8,128)(2,1)S(1)}, u32[]{:S(2)}, u32[]{:S(2)}) async-start(bf16[16,64,512]{2,1,0:T(8,128)(2,1)} %get-tuple-element.24), calls=%async_computation | async-start | bytes 2097152 | tf_op jit(solution)/shard_map/all_to_all | solution.py:363
  39.3 1.5 copy-start.5
  39.3 30.2 %collective-permute-start = (bf16[1024,512]{1,0:T(8,128)(2,1)S(1)}, bf16[1024,512]{1,0:T(8,128)(2,1)S(1)}, u32[]{:S(2)}, u32[]{:S(2)}) collective-permute-start(bf16[1024,512]{1,0:T(8,128)(2,1)S(1)} %bitcast.17), channel_id=1, source_target_pairs={{0,1},{1,0},{2,3},{3,2},{4,5},{5,4},{6,7},{7,6},{8,9},{9,8},{10,11... | collective-permute-start | bytes 3145736 | tf_op jit(solution)/shard_map/ppermute | solution.py:337
  39.9 29.5 %collective-permute-start.1 = (bf16[128,1024]{1,0:T(8,128)(2,1)S(1)}, bf16[128,1024]{1,0:T(8,128)(2,1)S(1)}, u32[]{:S(2)}, u32[]{:S(2)}) collective-permute-start(bf16[128,1024]{1,0:T(8,128)(2,1)S(1)} %get-tuple-element.25), channel_id=1, source_target_pairs={{0,1},{1,0},{2,3},{3,2},{4,5},{5,4},{6,7},{7,6},{8,9},{9,8},{10,11... | collective-permute-start | bytes 786440 | tf_op jit(solution)/shard_map/ppermute | solution.py:337
  40.7 31.3 %all-to-all-start.1 = ((bf16[16,64,512]{2,1,0:T(8,128)(2,1)}), bf16[16,64,512]{2,1,0:T(8,128)(2,1)}, u32[]{:S(2)}, u32[]{:S(2)}) async-start(bf16[16,64,512]{2,1,0:T(8,128)(2,1)} %shard_map.81), calls=%async_computation.1 | async-start | bytes 2097152 | tf_op jit(solution)/shard_map/all_to_all | solution.py:363
  69.4 0.7 copy-start.10
  69.4 1.1 copy-start.9
  72.0 31.9 %collective-permute-start.4 = (bf16[1024,512]{1,0:T(8,128)(2,1)}, bf16[1024,512]{1,0:T(8,128)(2,1)}, u32[]{:S(2)}, u32[]{:S(2)}) collective-permute-start(bf16[1024,512]{1,0:T(8,128)(2,1)} %bitcast.3.refs_1_.refs_0_), channel_id=1, source_target_pairs={{0,1},{1,0},{2,3},{3,2},{4,5},{5,4},{6,7},{7,6},{8,9},{9,8},{10,11... | collective-permute-start | bytes 3145736 | tf_op jit(solution)/shard_map/ppermute | solution.py:337
  73.3 30.4 %all-to-all-start.2 = ((bf16[16,64,512]{2,1,0:T(8,128)(2,1)}), bf16[16,64,512]{2,1,0:T(8,128)(2,1)}, u32[]{:S(2)}, u32[]{:S(2)}) async-start(bf16[16,64,512]{2,1,0:T(8,128)(2,1)} %shard_map.82), calls=%async_computation.2 | async-start | bytes 2097152 | tf_op jit(solution)/shard_map/all_to_all | solution.py:363
  78.5 18.4 %copy-start.6 = (bf16[128,1024]{1,0:T(8,128)(2,1)S(1)}, bf16[128,1024]{1,0:T(8,128)(2,1)}, u32[]{:S(2)}) copy-start(bf16[128,1024]{1,0:T(8,128)(2,1)} %get-tuple-element.29) | copy-start | bytes 786436
  85.5 11.4 %collective-permute-start.5 = (f32[1,128]{1,0:T(1,128)}, f32[1,128]{1,0:T(1,128)S(1)}, u32[]{:S(2)}, u32[]{:S(2)}) collective-permute-start(f32[1,128]{1,0:T(1,128)} %get-tuple-element.28.refs_0_), channel_id=1, source_target_pairs={{0,1},{1,0},{2,3},{3,2},{4,5},{5,4},{6,7},{7,6},{8,9},{9,8},{10,11... | collective-permute-start | bytes 1544 | tf_op jit(solution)/shard_map/ppermute | solution.py:337
  96.9 1.2 copy-start.7
  96.9 12.0 %collective-permute-start.6 = (bf16[128,1024]{1,0:T(8,128)(2,1)S(1)}, bf16[128,1024]{1,0:T(8,128)(2,1)S(1)}, u32[]{:S(2)}, u32[]{:S(2)}) collective-permute-start(bf16[128,1024]{1,0:T(8,128)(2,1)S(1)} %copy-done.6), channel_id=1, source_target_pairs={{0,1},{1,0},{2,3},{3,2},{4,5},{5,4},{6,7},{7,6},{8,9},{9,8},{10,11... | collective-permute-start | bytes 786440 | tf_op jit(solution)/shard_map/ppermute | solution.py:337
  103.7 28.6 %collective-permute-start.3 = (bf16[1024,512]{1,0:T(8,128)(2,1)}, bf16[1024,512]{1,0:T(8,128)(2,1)}, u32[]{:S(2)}, u32[]{:S(2)}) collective-permute-start(bf16[1024,512]{1,0:T(8,128)(2,1)} %bitcast.4.refs_1_), channel_id=1, source_target_pairs={{0,1},{1,0},{2,3},{3,2},{4,5},{5,4},{6,7},{7,6},{8,9},{9,8},{10,11... | collective-permute-start | bytes 3145736 | tf_op jit(solution)/shard_map/ppermute | solution.py:337
  103.9 30.3 %all-to-all-start.3 = ((bf16[16,64,512]{2,1,0:T(8,128)(2,1)}), bf16[16,64,512]{2,1,0:T(8,128)(2,1)}, u32[]{:S(2)}, u32[]{:S(2)}) async-start(bf16[16,64,512]{2,1,0:T(8,128)(2,1)} %shard_map.90), calls=%async_computation.3 | async-start | bytes 2097152 | tf_op jit(solution)/shard_map/all_to_all | solution.py:363
  108.9 0.7 copy-start.11
  116.6 12.2 %collective-permute-start.7 = (f32[1,128]{1,0:T(1,128)}, f32[1,128]{1,0:T(1,128)S(1)}, u32[]{:S(2)}, u32[]{:S(2)}) collective-permute-start(f32[1,128]{1,0:T(1,128)} %get-tuple-element.30.refs_0_), channel_id=1, source_target_pairs={{0,1},{1,0},{2,3},{3,2},{4,5},{5,4},{6,7},{7,6},{8,9},{9,8},{10,11... | collective-permute-start | bytes 1544 | tf_op jit(solution)/shard_map/ppermute | solution.py:337
  128.8 0.6 copy-start.8
  128.8 24.2 %collective-permute-start.8 = (bf16[512,1024]{1,0:T(8,128)(2,1)}, bf16[512,1024]{1,0:T(8,128)(2,1)}, u32[]{:S(2)}, u32[]{:S(2)}) collective-permute-start(bf16[512,1024]{1,0:T(8,128)(2,1)} %slice_bitcast_fusion), channel_id=1, source_target_pairs={{0,1},{1,0},{2,3},{3,2},{4,5},{5,4},{6,7},{7,6},{8,9},{9,8},{10,11... | collective-permute-start | bytes 3145736 | tf_op jit(solution)/shard_map/ppermute | solution.py:337
  134.2 29.6 %all-to-all-start.4 = ((bf16[16,64,512]{2,1,0:T(8,128)(2,1)}), bf16[16,64,512]{2,1,0:T(8,128)(2,1)}, u32[]{:S(2)}, u32[]{:S(2)}) async-start(bf16[16,64,512]{2,1,0:T(8,128)(2,1)} %shard_map.91), calls=%async_computation.4 | async-start | bytes 2097152 | tf_op jit(solution)/shard_map/all_to_all | solution.py:363
  138.9 14.1 %copy-start = (bf16[3,512,1024]{2,1,0:T(8,128)(2,1)S(1)}, bf16[3,512,1024]{2,1,0:T(8,128)(2,1)}, u32[]{:S(2)}) copy-start(bf16[3,512,1024]{2,1,0:T(8,128)(2,1)} %own_left.1) | copy-start | bytes 9437188
  152.9 1.2 copy-start.1
  154.2 5.0 %copy-start.4 = (f32[1,128]{1,0:T(1,128)S(1)}, f32[1,128]{1,0:T(1,128)}, u32[]{:S(2)}) copy-start(f32[1,128]{1,0:T(1,128)} %get-tuple-element.33.moment_square) | copy-start | bytes 1540
  156.7 2.4 %collective-permute-start.9 = (f32[1,128]{1,0:T(1,128)S(1)}, f32[1,128]{1,0:T(1,128)S(1)}, u32[]{:S(2)}, u32[]{:S(2)}) collective-permute-start(f32[1,128]{1,0:T(1,128)S(1)} %get-tuple-element.34.refs_0_), channel_id=1, source_target_pairs={{0,1},{1,0},{2,3},{3,2},{4,5},{5,4},{6,7},{7,6},{8,9},{9,8},{10,11... | collective-permute-start | bytes 1544 | tf_op jit(solution)/shard_map/ppermute | solution.py:337
  159.1 9.6 %copy-start.2 = (s32[32]{0:T(128)S(1)}, s32[32]{0:T(128)}, u32[]{:S(2)}) copy-start(s32[32]{0:T(128)} %assign_ref.7) | copy-start | bytes 388
  159.1 9.6 %copy-start.3 = (s32[16]{0:T(128)S(1)}, s32[16]{0:T(128)}, u32[]{:S(2)}) copy-start(s32[16]{0:T(128)} %count_ref.7) | copy-start | bytes 196
  163.8 29.8 %all-to-all-start.5 = ((bf16[16,64,512]{2,1,0:T(8,128)(2,1)}), bf16[16,64,512]{2,1,0:T(8,128)(2,1)S(1)}, u32[]{:S(2)}, u32[]{:S(2)}) async-start(bf16[16,64,512]{2,1,0:T(8,128)(2,1)} %bitcast.8), calls=%async_computation.5 | async-start | bytes 2097152 | tf_op jit(solution)/shard_map/all_to_all | solution.py:363

commit v6 on v5

--- a/solution.py
+++ b/solution.py
@@ -402,14 +402,14 @@
     m0 = around(columns0, parts)
     e1 = send(6, 7, columns0)
     columns1 = swap(gate(out1, columns0)).reshape(order, width)
-    out2 = gate(out2, *m0, *e1)
+    out2 = gate(out2, *m0)
     m1 = around(columns1, parts)
     columns2 = swap(gate(out2, columns1)).reshape(order, width)
     d0, q0 = solve(0, columns0, m0, lefts(0))
     e2 = send(7, 8, q0)
     m2 = around(columns2, parts)
     e3 = []
-    b0 = swap(gate(d0, columns2, *m1))
+    b0 = swap(gate(d0, columns2, *m1, *e1))
     d1, q1 = solve(1, columns1, m1, lefts(1))
     e4 = send(8, 12, q1)
     b1 = swap(gate(d1, b0, *m2))

time: 196 us -> 196 us (level)
    ppermute x10, waiting for transfers between devices: 70.3 us -> 63.8 us  [around(): lax.ppermute(x, 'tensor', [(s, (s + d) % parts) for s in range(parts)])]
    all_to_all x6, waiting for transfers between devices: 32.4 us -> 38 us  [swap(): return lax.all_to_all(x, 'dp', split_axis=0, concat_axis=0, tiled=True)]
where the time goes in v6:
time: 196 us; the launch traced here: 195 us
  waiting for transfers between devices  102 us (52%)
  Pallas kernels  42.3 us (22%)
  starting transfers between devices  40.8 us (21%)
  local copies, waits for them, and re-layouts  9.01 us (5%)
    ppermute x10, waiting for transfers between devices, around(): lax.ppermute(x, 'tensor', [(s, (s + d) % parts) for s in range(parts)])  63.8 us
    all_to_all x6, waiting for transfers between devices, swap(): return lax.all_to_all(x, 'dp', split_axis=0, concat_axis=0, tiled=True)  38 us
    all_to_all x6, starting transfers between devices, swap(): return lax.all_to_all(x, 'dp', split_axis=0, concat_axis=0, tiled=True)  33 us
    pallas_call x2, Pallas kernels, precondition(): pl.pallas_call(functools.partial(root_kernel, parts, len(lefts[0])), grid...  14 us
    pallas_call x2, Pallas kernels, make_moment(): pl.pallas_call(functools.partial(moment_kernel, slots), grid_spec=pltpu.P...  8.72 us
    ppermute x10, starting transfers between devices, around(): lax.ppermute(x, 'tensor', [(s, (s + d) % parts) for s in range(parts)])  7.77 us
    pallas_call x3, Pallas kernels, rescale(): pl.pallas_call(functools.partial(scale_kernel, float(order * order)), in_...  7.19 us
    slice x3, local copies, waits for them, and re-layouts, send(): rows = flat[first * unit:end * unit]  5.72 us
  transfers between devices with their start and end apart: 16, of which 12 were waited for; matrix products, arithmetic and copies ran while one was open for 2% of the time, Pallas kernels for 21%

profile of v6, /device:TPU:11, one launch (start us, length us, event | category | flops | bytes accessed | tf_op | source)
XLA Modules:
  0.0 194.5 jit_solution(16765810335865099748)
XLA Ops:
  0.6 1.5 slice.20
  2.2 1.3 collective-permute-start.1
  3.5 4.1 %shard_map.77 = (f32[32,64,512]{2,1,0:T(8,128)}, bf16[16,64,512]{2,1,0:T(8,128)(2,1)}) custom-call(s32[32]{0:T(128)} %assign_ref.7, s32[16]{0:T(128)} %count_ref.7, bf16[32,64,512]{2,1,0:T(8,128)(2,1)} %refs_0_.3, f32[32,64,512]{2,1,0:T(8,128)} %refs_1_.3), custom_call_target="tpu_custom_call" | custom-call | flops 157286400 | bytes 629145600 | tf_op jit(solution)/shard_map/pallas_call | solution.py:72
  7.5 6.8 %all-to-all-start = ((bf16[16,64,512]{2,1,0:T(8,128)(2,1)}), bf16[16,64,512]{2,1,0:T(8,128)(2,1)S(1)}, u32[]{:S(2)}, u32[]{:S(2)}) async-start(bf16[16,64,512]{2,1,0:T(8,128)(2,1)} %get-tuple-element.24), calls=%async_computation | async-start | bytes 2097152 | tf_op jit(solution)/shard_map/all_to_all | solution.py:363
  14.4 4.7 %shard_map.78 = (f32[32,64,512]{2,1,0:T(8,128)}, bf16[16,64,512]{2,1,0:T(8,128)(2,1)}, bf16[16,64,512]{2,1,0:T(8,128)(2,1)}) custom-call(s32[32]{0:T(128)} %assign_ref.7, s32[16]{0:T(128)} %count_ref.7, bf16[32,64,512]{2,1,0:T(8,128)(2,1)} %refs_0_.3, f32[32,64,512]{2,1,0:T(8,128)} %refs_1_.3, ...), custom_call_target="tpu_custom_call", output_to_operand_aliasing={{0}: (4, {})} | custom-call | flops 314572800 | bytes 1258291200 | tf_op jit(solution)/shard_map/pallas_call | solution.py:72
  19.0 1.9 fusion
  21.0 16.6 %collective-permute-done.1.refs_1_.refs_4_ = bf16[768,1024]{1,0:T(8,128)(2,1)} collective-permute-done((bf16[768,1024]{1,0:T(8,128)(2,1)S(1)}, bf16[768,1024]{1,0:T(8,128)(2,1)}, u32[]{:S(2)}, u32[]{:S(2)}) %collective-permute-start.1) | collective-permute-done | bytes 1572896 | tf_op jit(solution)/shard_map/ppermute | solution.py:337
  37.6 1.7 all-to-all-done
  39.3 0.0 copy-start.5
  39.3 0.6 collective-permute-start
  39.9 0.3 copy-done.5
  40.2 6.3 %all-to-all-start.1 = ((bf16[16,64,512]{2,1,0:T(8,128)(2,1)}), bf16[16,64,512]{2,1,0:T(8,128)(2,1)}, u32[]{:S(2)}, u32[]{:S(2)}) async-start(bf16[16,64,512]{2,1,0:T(8,128)(2,1)} %shard_map.81), calls=%async_computation.1 | async-start | bytes 2097152 | tf_op jit(solution)/shard_map/all_to_all | solution.py:363
  46.6 0.7 collective-permute-start.4
  47.2 16.7 %collective-permute-done.refs_1_ = bf16[1024,512]{1,0:T(8,128)(2,1)S(1)} collective-permute-done((bf16[1024,512]{1,0:T(8,128)(2,1)S(1)}, bf16[1024,512]{1,0:T(8,128)(2,1)S(1)}, u32[]{:S(2)}, u32[]{:S(2)}) %collective-permute-start) | collective-permute-done | bytes 1048608 | tf_op jit(solution)/shard_map/ppermute | solution.py:337
  63.9 0.0 copy-start.9
  63.9 1.0 copy-done.9
  64.9 6.6 %all-to-all-done.1 = bf16[16,64,512]{2,1,0:T(8,128)(2,1)} async-done(((bf16[16,64,512]{2,1,0:T(8,128)(2,1)}), bf16[16,64,512]{2,1,0:T(8,128)(2,1)}, u32[]{:S(2)}, u32[]{:S(2)}) %all-to-all-start.1) | async-done | bytes 1048608 | tf_op jit(solution)/shard_map/all_to_all | solution.py:363
  71.5 0.7 collective-permute-start.3
  72.2 5.2 %all-to-all-start.2 = ((bf16[16,64,512]{2,1,0:T(8,128)(2,1)}), bf16[16,64,512]{2,1,0:T(8,128)(2,1)}, u32[]{:S(2)}, u32[]{:S(2)}) async-start(bf16[16,64,512]{2,1,0:T(8,128)(2,1)} %shard_map.82), calls=%async_computation.2 | async-start | bytes 2097152 | tf_op jit(solution)/shard_map/all_to_all | solution.py:363
  77.4 0.0 copy-start.6
  77.4 7.0 %shard_map.84 = (f32[1024,512]{1,0:T(8,128)}, f32[1,128]{1,0:T(1,128)}, f32[1,128]{1,0:T(1,128)}) custom-call(s32[1]{0:T(128)} %bitcast.turn_ref, bf16[1024,512]{1,0:T(8,128)(2,1)} %bitcast.19, bf16[1024,512]{1,0:T(8,128)(2,1)} %copy-done.9, bf16[3,512,1024]{2,1,0:T(8,128)(2,1)} %refs_2_.5, bf16[3,512,1024]{2,1,0:T(8,128)(2,1)} %own_left.1, ...), custom_call_target="tpu_custom_call" | custom-call | flops 214748364800 | bytes 629145600 | tf_op jit(solution)/shard_map/pallas_call | solution.py:183
  84.5 0.8 collective-permute-start.5
  85.2 11.2 %collective-permute-done.5.refs_1_ = f32[1,128]{1,0:T(1,128)S(1)} collective-permute-done((f32[1,128]{1,0:T(1,128)}, f32[1,128]{1,0:T(1,128)S(1)}, u32[]{:S(2)}, u32[]{:S(2)}) %collective-permute-start.5) | collective-permute-done | bytes 544 | tf_op jit(solution)/shard_map/ppermute | solution.py:337
  96.4 0.0 copy-start.7
  96.4 0.0 copy-done.6
  96.4 0.7 collective-permute-start.6
  97.1 0.0 copy-done.7
  97.1 2.9 %shard_map.89 = bf16[1024,512]{1,0:T(8,128)(2,1)} custom-call(f32[1024,512]{1,0:T(8,128)} %get-tuple-element.37.direction, f32[1,128]{1,0:T(1,128)} %get-tuple-element.38.moment_square, f32[1,128]{1,0:T(1,128)} %get-tuple-element.28.refs_0_, f32[1,128]{1,0:T(1,128)} %copy-done.7), custom_call_target="tpu_custom_call" | custom-call | flops 524288 | bytes 3145728 | tf_op jit(solution)/shard_map/pallas_call | solution.py:323
  100.0 2.6 %all-to-all-done.2.refs_0_ = bf16[16,64,512]{2,1,0:T(8,128)(2,1)} async-done(((bf16[16,64,512]{2,1,0:T(8,128)(2,1)}), bf16[16,64,512]{2,1,0:T(8,128)(2,1)}, u32[]{:S(2)}, u32[]{:S(2)}) %all-to-all-start.2) | async-done | bytes 1048608 | tf_op jit(solution)/shard_map/all_to_all | solution.py:363
  102.6 0.8 collective-permute-start.2
  103.4 0.0 collective-permute-done.4.refs_5_.refs_3_
  103.4 0.0 collective-permute-done.3.refs_1_.refs_2_
  103.4 5.0 %all-to-all-start.3 = ((bf16[16,64,512]{2,1,0:T(8,128)(2,1)}), bf16[16,64,512]{2,1,0:T(8,128)(2,1)}, u32[]{:S(2)}, u32[]{:S(2)}) async-start(bf16[16,64,512]{2,1,0:T(8,128)(2,1)} %shard_map.90), calls=%async_computation.3 | async-start | bytes 2097152 | tf_op jit(solution)/shard_map/all_to_all | solution.py:363
  108.4 0.0 collective-permute-done.6.refs_6_
  108.4 0.0 copy-start.10
  108.4 0.7 copy-done.10
  109.1 6.9 %shard_map.85 = (f32[1024,512]{1,0:T(8,128)}, f32[1,128]{1,0:T(1,128)}, f32[1,128]{1,0:T(1,128)}) custom-call(s32[1]{0:T(128)} %bitcast.turn_ref, bf16[1024,512]{1,0:T(8,128)(2,1)} %bitcast.3.refs_1_.refs_0_, bf16[1024,512]{1,0:T(8,128)(2,1)} %collective-permute-done.3.refs_1_.refs_2_, bf16[3,512,1024]{2,1,0:T(8,128)(2,1)} %refs_2_.5, ...), custom_call_target="tpu_custom_call" | custom-call | flops 214748364800 | bytes 629145600 | tf_op jit(solution)/shard_map/pallas_call | solution.py:183
  116.1 0.7 collective-permute-start.7
  116.8 2.3 %slice_bitcast_fusion = bf16[512,1024]{1,0:T(8,128)(2,1)} fusion(bf16[3,512,1024]{2,1,0:T(8,128)(2,1)} %own_left.1), kind=kLoop, calls=%fused_computation | loop fusion | bytes 2097152 | tf_op jit(solution)/shard_map/slice | solution.py:384
  119.0 8.7 %collective-permute-done.7.refs_1_ = f32[1,128]{1,0:T(1,128)S(1)} collective-permute-done((f32[1,128]{1,0:T(1,128)}, f32[1,128]{1,0:T(1,128)S(1)}, u32[]{:S(2)}, u32[]{:S(2)}) %collective-permute-start.7) | collective-permute-done | bytes 544 | tf_op jit(solution)/shard_map/ppermute | solution.py:337
  127.7 0.0 copy-start.8
  127.7 0.8 collective-permute-start.8
  128.5 0.0 copy-done.8
  128.5 3.0 %shard_map.88 = bf16[1024,512]{1,0:T(8,128)(2,1)} custom-call(f32[1024,512]{1,0:T(8,128)} %get-tuple-element.35.direction, f32[1,128]{1,0:T(1,128)} %get-tuple-element.36.moment_square, f32[1,128]{1,0:T(1,128)} %get-tuple-element.30.refs_0_, f32[1,128]{1,0:T(1,128)} %copy-done.8), custom_call_target="tpu_custom_call" | custom-call | flops 524288 | bytes 3145728 | tf_op jit(solution)/shard_map/pallas_call | solution.py:323
  131.4 0.0 collective-permute-done.2.refs_2_
  131.4 2.3 %all-to-all-done.3.refs_1_.refs_0_ = bf16[16,64,512]{2,1,0:T(8,128)(2,1)} async-done(((bf16[16,64,512]{2,1,0:T(8,128)(2,1)}), bf16[16,64,512]{2,1,0:T(8,128)(2,1)}, u32[]{:S(2)}, u32[]{:S(2)}) %all-to-all-start.3) | async-done | bytes 1048608 | tf_op jit(solution)/shard_map/all_to_all | solution.py:363
  133.7 4.6 %all-to-all-start.4 = ((bf16[16,64,512]{2,1,0:T(8,128)(2,1)}), bf16[16,64,512]{2,1,0:T(8,128)(2,1)}, u32[]{:S(2)}, u32[]{:S(2)}) async-start(bf16[16,64,512]{2,1,0:T(8,128)(2,1)} %shard_map.91), calls=%async_computation.4 | async-start | bytes 2097152 | tf_op jit(solution)/shard_map/all_to_all | solution.py:363
  138.4 0.0 copy-start
  138.4 4.9 %shard_map.83 = (bf16[16,64,512]{2,1,0:T(8,128)(2,1)}, f32[1,128]{1,0:T(1,128)}) custom-call(s32[1]{0:T(128)} %bitcast.turn_ref, bf16[16,64,512]{2,1,0:T(8,128)(2,1)} %all-to-all-done.2.refs_0_, bf16[16,64,512]{2,1,0:T(8,128)(2,1)} %bitcast.5.refs_1_, bf16[3,512,1024]{2,1,0:T(8,128)(2,1)} %refs_2_.5), custom_call_target="tpu_custom_call" | custom-call | flops 214748364800 | bytes 629145600 | tf_op jit(solution)/shard_map/pallas_call | solution.py:247
  143.3 8.6 %collective-permute-done.8.refs_0_ = bf16[512,1024]{1,0:T(8,128)(2,1)} collective-permute-done((bf16[512,1024]{1,0:T(8,128)(2,1)}, bf16[512,1024]{1,0:T(8,128)(2,1)}, u32[]{:S(2)}, u32[]{:S(2)}) %collective-permute-start.8) | collective-permute-done | bytes 1048608 | tf_op jit(solution)/shard_map/ppermute | solution.py:337
  151.9 0.0 copy-done
  151.9 1.2 copy-done.1
  153.1 2.6 %shard_map.86 = (f32[1024,512]{1,0:T(8,128)S(1)}, f32[1,128]{1,0:T(1,128)S(1)}) custom-call(s32[1]{0:T(128)} %bitcast.turn_ref, bf16[1024,512]{1,0:T(8,128)(2,1)S(1)} %bitcast.14, bf16[3,512,1024]{2,1,0:T(8,128)(2,1)S(1)} %copy-done, bf16[512,1024]{1,0:T(8,128)(2,1)} %collective-permute-done.8.refs_0_), custom_call_target="tpu_custom_call" | custom-call | flops 1073741824 | bytes 3145728 | tf_op jit(solution)/shard_map/pallas_call | solution.py:295
  155.7 0.8 collective-permute-start.9
  156.5 2.0 %collective-permute-done.9.refs_1_ = f32[1,128]{1,0:T(1,128)S(1)} collective-permute-done((f32[1,128]{1,0:T(1,128)S(1)}, f32[1,128]{1,0:T(1,128)S(1)}, u32[]{:S(2)}, u32[]{:S(2)}) %collective-permute-start.9) | collective-permute-done | bytes 544 | tf_op jit(solution)/shard_map/ppermute | solution.py:337
  158.5 0.0 copy-done.4
  158.5 1.3 shard_map.87
  159.8 3.5 %all-to-all-done.4.refs_1_ = bf16[16,64,512]{2,1,0:T(8,128)(2,1)} async-done(((bf16[16,64,512]{2,1,0:T(8,128)(2,1)}), bf16[16,64,512]{2,1,0:T(8,128)(2,1)}, u32[]{:S(2)}, u32[]{:S(2)}) %all-to-all-start.4) | async-done | bytes 1048608 | tf_op jit(solution)/shard_map/all_to_all | solution.py:363
  163.3 4.9 %all-to-all-start.5 = ((bf16[16,64,512]{2,1,0:T(8,128)(2,1)}), bf16[16,64,512]{2,1,0:T(8,128)(2,1)S(1)}, u32[]{:S(2)}, u32[]{:S(2)}) async-start(bf16[16,64,512]{2,1,0:T(8,128)(2,1)} %bitcast.8), calls=%async_computation.5 | async-start | bytes 2097152 | tf_op jit(solution)/shard_map/all_to_all | solution.py:363
  168.3 0.0 copy-done.2
  168.3 0.0 copy-done.3
  168.3 3.6 %shard_map.92.refs_1_ = bf16[32,64,512]{2,1,0:T(8,128)(2,1)} custom-call(s32[32]{0:T(128)S(1)} %copy-done.2, s32[16]{0:T(128)S(1)} %copy-done.3, bf16[16,64,512]{2,1,0:T(8,128)(2,1)} %all-to-all-done.3.refs_1_.refs_0_, bf16[16,64,512]{2,1,0:T(8,128)(2,1)} %all-to-all-done.4.refs_1_), custom_call_target="tpu_custom_call" | custom-call | bytes 4194304 | tf_op jit(solution)/shard_map/pallas_call | solution.py:112
  171.9 21.3 %all-to-all-done.5.refs_0_ = bf16[16,64,512]{2,1,0:T(8,128)(2,1)S(1)} async-done(((bf16[16,64,512]{2,1,0:T(8,128)(2,1)}), bf16[16,64,512]{2,1,0:T(8,128)(2,1)S(1)}, u32[]{:S(2)}, u32[]{:S(2)}) %all-to-all-start.5) | async-done | bytes 1048608 | tf_op jit(solution)/shard_map/all_to_all | solution.py:363
  193.1 1.4 shard_map.93
  (10 shorter events, 0.0 us)
Async XLA Ops:
  2.2 35.4 %collective-permute-start.1 = (bf16[768,1024]{1,0:T(8,128)(2,1)S(1)}, bf16[768,1024]{1,0:T(8,128)(2,1)}, u32[]{:S(2)}, u32[]{:S(2)}) collective-permute-start(bf16[768,1024]{1,0:T(8,128)(2,1)S(1)} %slice.20), channel_id=1, source_target_pairs={{0,1},{1,0},{2,3},{3,2},{4,5},{5,4},{6,7},{7,6},{8,9},{9,8},{10,11... | collective-permute-start | bytes 4718600 | tf_op jit(solution)/shard_map/ppermute | solution.py:337
  7.5 31.7 %all-to-all-start = ((bf16[16,64,512]{2,1,0:T(8,128)(2,1)}), bf16[16,64,512]{2,1,0:T(8,128)(2,1)S(1)}, u32[]{:S(2)}, u32[]{:S(2)}) async-start(bf16[16,64,512]{2,1,0:T(8,128)(2,1)} %get-tuple-element.24), calls=%async_computation | async-start | bytes 2097152 | tf_op jit(solution)/shard_map/all_to_all | solution.py:363
  39.3 1.0 copy-start.5
  39.3 24.7 %collective-permute-start = (bf16[1024,512]{1,0:T(8,128)(2,1)S(1)}, bf16[1024,512]{1,0:T(8,128)(2,1)S(1)}, u32[]{:S(2)}, u32[]{:S(2)}) collective-permute-start(bf16[1024,512]{1,0:T(8,128)(2,1)S(1)} %bitcast.17), channel_id=1, source_target_pairs={{0,1},{1,0},{2,3},{3,2},{4,5},{5,4},{6,7},{7,6},{8,9},{9,8},{10,11... | collective-permute-start | bytes 3145736 | tf_op jit(solution)/shard_map/ppermute | solution.py:337
  40.2 31.3 %all-to-all-start.1 = ((bf16[16,64,512]{2,1,0:T(8,128)(2,1)}), bf16[16,64,512]{2,1,0:T(8,128)(2,1)}, u32[]{:S(2)}, u32[]{:S(2)}) async-start(bf16[16,64,512]{2,1,0:T(8,128)(2,1)} %shard_map.81), calls=%async_computation.1 | async-start | bytes 2097152 | tf_op jit(solution)/shard_map/all_to_all | solution.py:363
  46.6 56.8 %collective-permute-start.4 = (bf16[128,1024]{1,0:T(8,128)(2,1)}, bf16[128,1024]{1,0:T(8,128)(2,1)}, u32[]{:S(2)}, u32[]{:S(2)}) collective-permute-start(bf16[128,1024]{1,0:T(8,128)(2,1)} %get-tuple-element.27), channel_id=1, source_target_pairs={{0,1},{1,0},{2,3},{3,2},{4,5},{5,4},{6,7},{7,6},{8,9},{9,8},{10,11... | collective-permute-start | bytes 786440 | tf_op jit(solution)/shard_map/ppermute | solution.py:337
  63.9 1.0 copy-start.9
  71.5 31.9 %collective-permute-start.3 = (bf16[1024,512]{1,0:T(8,128)(2,1)}, bf16[1024,512]{1,0:T(8,128)(2,1)}, u32[]{:S(2)}, u32[]{:S(2)}) collective-permute-start(bf16[1024,512]{1,0:T(8,128)(2,1)} %bitcast.3.refs_1_.refs_0_), channel_id=1, source_target_pairs={{0,1},{1,0},{2,3},{3,2},{4,5},{5,4},{6,7},{7,6},{8,9},{9,8},{10,11... | collective-permute-start | bytes 3145736 | tf_op jit(solution)/shard_map/ppermute | solution.py:337
  72.2 30.4 %all-to-all-start.2 = ((bf16[16,64,512]{2,1,0:T(8,128)(2,1)}), bf16[16,64,512]{2,1,0:T(8,128)(2,1)}, u32[]{:S(2)}, u32[]{:S(2)}) async-start(bf16[16,64,512]{2,1,0:T(8,128)(2,1)} %shard_map.82), calls=%async_computation.2 | async-start | bytes 2097152 | tf_op jit(solution)/shard_map/all_to_all | solution.py:363
  77.4 19.0 %copy-start.6 = (bf16[128,1024]{1,0:T(8,128)(2,1)S(1)}, bf16[128,1024]{1,0:T(8,128)(2,1)}, u32[]{:S(2)}) copy-start(bf16[128,1024]{1,0:T(8,128)(2,1)} %get-tuple-element.29) | copy-start | bytes 786436
  84.5 11.9 %collective-permute-start.5 = (f32[1,128]{1,0:T(1,128)}, f32[1,128]{1,0:T(1,128)S(1)}, u32[]{:S(2)}, u32[]{:S(2)}) collective-permute-start(f32[1,128]{1,0:T(1,128)} %get-tuple-element.28.refs_0_), channel_id=1, source_target_pairs={{0,1},{1,0},{2,3},{3,2},{4,5},{5,4},{6,7},{7,6},{8,9},{9,8},{10,11... | collective-permute-start | bytes 1544 | tf_op jit(solution)/shard_map/ppermute | solution.py:337
  96.4 0.7 copy-start.7
  96.4 12.0 %collective-permute-start.6 = (bf16[128,1024]{1,0:T(8,128)(2,1)S(1)}, bf16[128,1024]{1,0:T(8,128)(2,1)S(1)}, u32[]{:S(2)}, u32[]{:S(2)}) collective-permute-start(bf16[128,1024]{1,0:T(8,128)(2,1)S(1)} %copy-done.6), channel_id=1, source_target_pairs={{0,1},{1,0},{2,3},{3,2},{4,5},{5,4},{6,7},{7,6},{8,9},{9,8},{10,11... | collective-permute-start | bytes 786440 | tf_op jit(solution)/shard_map/ppermute | solution.py:337
  102.6 28.8 %collective-permute-start.2 = (bf16[1024,512]{1,0:T(8,128)(2,1)}, bf16[1024,512]{1,0:T(8,128)(2,1)}, u32[]{:S(2)}, u32[]{:S(2)}) collective-permute-start(bf16[1024,512]{1,0:T(8,128)(2,1)} %bitcast.4.refs_1_), channel_id=1, source_target_pairs={{0,1},{1,0},{2,3},{3,2},{4,5},{5,4},{6,7},{7,6},{8,9},{9,8},{10,11... | collective-permute-start | bytes 3145736 | tf_op jit(solution)/shard_map/ppermute | solution.py:337
  103.4 30.3 %all-to-all-start.3 = ((bf16[16,64,512]{2,1,0:T(8,128)(2,1)}), bf16[16,64,512]{2,1,0:T(8,128)(2,1)}, u32[]{:S(2)}, u32[]{:S(2)}) async-start(bf16[16,64,512]{2,1,0:T(8,128)(2,1)} %shard_map.90), calls=%async_computation.3 | async-start | bytes 2097152 | tf_op jit(solution)/shard_map/all_to_all | solution.py:363
  108.4 0.7 copy-start.10
  116.1 11.6 %collective-permute-start.7 = (f32[1,128]{1,0:T(1,128)}, f32[1,128]{1,0:T(1,128)S(1)}, u32[]{:S(2)}, u32[]{:S(2)}) collective-permute-start(f32[1,128]{1,0:T(1,128)} %get-tuple-element.30.refs_0_), channel_id=1, source_target_pairs={{0,1},{1,0},{2,3},{3,2},{4,5},{5,4},{6,7},{7,6},{8,9},{9,8},{10,11... | collective-permute-start | bytes 1544 | tf_op jit(solution)/shard_map/ppermute | solution.py:337
  127.7 0.8 copy-start.8
  127.7 24.2 %collective-permute-start.8 = (bf16[512,1024]{1,0:T(8,128)(2,1)}, bf16[512,1024]{1,0:T(8,128)(2,1)}, u32[]{:S(2)}, u32[]{:S(2)}) collective-permute-start(bf16[512,1024]{1,0:T(8,128)(2,1)} %slice_bitcast_fusion), channel_id=1, source_target_pairs={{0,1},{1,0},{2,3},{3,2},{4,5},{5,4},{6,7},{7,6},{8,9},{9,8},{10,11... | collective-permute-start | bytes 3145736 | tf_op jit(solution)/shard_map/ppermute | solution.py:337
  133.7 29.6 %all-to-all-start.4 = ((bf16[16,64,512]{2,1,0:T(8,128)(2,1)}), bf16[16,64,512]{2,1,0:T(8,128)(2,1)}, u32[]{:S(2)}, u32[]{:S(2)}) async-start(bf16[16,64,512]{2,1,0:T(8,128)(2,1)} %shard_map.91), calls=%async_computation.4 | async-start | bytes 2097152 | tf_op jit(solution)/shard_map/all_to_all | solution.py:363
  138.4 13.5 %copy-start = (bf16[3,512,1024]{2,1,0:T(8,128)(2,1)S(1)}, bf16[3,512,1024]{2,1,0:T(8,128)(2,1)}, u32[]{:S(2)}) copy-start(bf16[3,512,1024]{2,1,0:T(8,128)(2,1)} %own_left.1) | copy-start | bytes 9437188
  151.9 1.2 copy-start.1
  153.1 5.4 %copy-start.4 = (f32[1,128]{1,0:T(1,128)S(1)}, f32[1,128]{1,0:T(1,128)}, u32[]{:S(2)}) copy-start(f32[1,128]{1,0:T(1,128)} %get-tuple-element.33.moment_square) | copy-start | bytes 1540
  155.7 2.8 %collective-permute-start.9 = (f32[1,128]{1,0:T(1,128)S(1)}, f32[1,128]{1,0:T(1,128)S(1)}, u32[]{:S(2)}, u32[]{:S(2)}) collective-permute-start(f32[1,128]{1,0:T(1,128)S(1)} %get-tuple-element.34.refs_0_), channel_id=1, source_target_pairs={{0,1},{1,0},{2,3},{3,2},{4,5},{5,4},{6,7},{7,6},{8,9},{9,8},{10,11... | collective-permute-start | bytes 1544 | tf_op jit(solution)/shard_map/ppermute | solution.py:337
  158.5 9.8 %copy-start.2 = (s32[32]{0:T(128)S(1)}, s32[32]{0:T(128)}, u32[]{:S(2)}) copy-start(s32[32]{0:T(128)} %assign_ref.7) | copy-start | bytes 388
  158.5 9.8 %copy-start.3 = (s32[16]{0:T(128)S(1)}, s32[16]{0:T(128)}, u32[]{:S(2)}) copy-start(s32[16]{0:T(128)} %count_ref.7) | copy-start | bytes 196
  163.3 29.8 %all-to-all-start.5 = ((bf16[16,64,512]{2,1,0:T(8,128)(2,1)}), bf16[16,64,512]{2,1,0:T(8,128)(2,1)S(1)}, u32[]{:S(2)}, u32[]{:S(2)}) async-start(bf16[16,64,512]{2,1,0:T(8,128)(2,1)} %bitcast.8), calls=%async_computation.5 | async-start | bytes 2097152 | tf_op jit(solution)/shard_map/all_to_all | solution.py:363
